TPU v7x, 512 devices: a whole 4x4x16 slice. The times are simulated.
512 devices in a mesh: sn: 64 (over x, z), rhs: 8 (over y, core).
Axes of the slice: x: 4, y: 4, z: 16, core: 2. Of those that a mesh axis runs over, the one named last changes fastest.
Arguments:
- lanczos_block: float32 [512, 8, 16384], P(None, None, ('sn', 'rhs')), may hold values from -6 to 6
- diag_inv: bfloat16 [8, 128, 128, 128], P(None, 'sn')
- factor_tiles: bfloat16 [7, 1536, 128, 128], P(None, 'sn'), may hold values from -0.046875 to 0.046875
- tile_rows: int32 [7, 1536], replicated, may hold values from 128 to 1023, as said below
- tile_cols: int32 [7, 1536], replicated, may hold values from 0 to 895, as said below
Outputs:
- solution: bfloat16 [512, 8, 16384], P(None, None, ('sn', 'rhs'))
Inputs may be any that keep to these rules, and one draw needn't show every extreme that they name: Slot j of level l belongs to device j // 24; tile_rows[l, j] is a supernode of a level above l whose position lies among that device's positions, 2 * (j // 24) to 2 * (j // 24) + 1. tile_cols[l, j] is a supernode of level l whose position belongs to device (j // 24 + (j % 24) // 8 - 1) modulo 64, that is, positions 2 times that device to 2 times that device + 1.
All inputs are finite; a program needn't handle non-finite values.
Results may differ from a plain program's by a relative error of at most 0.011.
Values may be sent and summed in bfloat16 or wider, within the bound.
No kernel may reach another device: no remote copies, remote signals or barrier semaphores. Data moves between devices by JAX's collectives and lax.ppermute only.
A program may use at most 64 MiB of HBM per device.

v0:
```python
import jax
import jax.numpy as jnp
from jax import lax
from jax.sharding import PartitionSpec as P


def with_halo(shard, sides, width):
    for axis, dim in sides:
        peers, length = (lax.axis_size(axis), shard.shape[dim])
        up = [(i, (i + 1) % peers) for i in range(peers)]
        down = [(j, i) for i, j in up]
        last = lax.slice_in_dim(shard, length - width, length, axis=dim)
        initial = lax.slice_in_dim(shard, 0, width, axis=dim)
        before = lax.ppermute(last, axis, up)
        after = lax.ppermute(initial, axis, down)
        shard = jnp.concatenate([before, shard, after], axis=dim)
    return shard


def on_device(lanczos_block, diag_inv, factor_tiles, tile_rows, tile_cols):
    levels = diag_inv.shape[0]
    owned_count = diag_inv.shape[1]
    block_rows = diag_inv.shape[2]
    group_tiles = factor_tiles.shape[1]
    per_group = group_tiles // 3
    axis_size = lax.axis_size("sn")
    own_index = lax.axis_index("sn")
    per_level = owned_count * axis_size
    panels = lax.all_to_all(lanczos_block, "rhs", split_axis=0, concat_axis=2, tiled=True)
    columns = panels.shape[0]
    vectors = panels.reshape(columns, levels * owned_count, block_rows)
    my_rows = lax.dynamic_slice_in_dim(tile_rows, own_index * group_tiles, group_tiles, 1)
    my_cols = lax.dynamic_slice_in_dim(tile_cols, own_index * group_tiles, group_tiles, 1)
    group_index = (jnp.arange(group_tiles, dtype=jnp.int32) // per_group)[None, :]
    row_slot = my_rows // per_level * owned_count + my_rows % owned_count
    col_slot = group_index * owned_count + my_cols % owned_count
    row_onehot = (
        row_slot[:, :, None] == jnp.arange(levels * owned_count, dtype=jnp.int32)[None, None, :]
    ).astype(jnp.float32)
    updates = jnp.zeros((columns, levels * owned_count, block_rows), jnp.float32)
    solved = []
    for height in range(levels):
        first_slot = height * owned_count
        last_slot = first_slot + owned_count
        reduced = (vectors[:, first_slot:last_slot] - updates[:, first_slot:last_slot]).astype(
            jnp.bfloat16
        )
        solved_now = jnp.einsum(
            "rkb,kab->rka", reduced, diag_inv[height], preferred_element_type=jnp.float32
        ).astype(jnp.bfloat16)
        solved.append(solved_now)
        if height + 1 < levels:
            window = with_halo(solved_now, (("sn", 1),), owned_count)
            picked = jnp.take(window, col_slot[height], axis=1)
            partial_value = jnp.einsum(
                "rtb,tab->rta", picked, factor_tiles[height], preferred_element_type=jnp.float32
            )
            updates = updates + jnp.einsum(
                "ts,rta->rsa", row_onehot[height], partial_value, precision=lax.Precision.HIGHEST
            )
    results = [None] * levels
    term_onehot = (
        col_slot[:, :, None] == jnp.arange(3 * owned_count, dtype=jnp.int32)[None, None, :]
    ).astype(jnp.float32)
    answers = jnp.zeros((columns, levels * owned_count, block_rows), jnp.bfloat16)
    for height in reversed(range(levels)):
        if height + 1 < levels:
            picked = jnp.take(answers, row_slot[height], axis=1)
            partial_value = jnp.einsum(
                "rta,tab->rtb", picked, factor_tiles[height], preferred_element_type=jnp.float32
            )
            sums = jnp.einsum(
                "tw,rtb->rwb", term_onehot[height], partial_value, precision=lax.Precision.HIGHEST
            )
            outgoing = jnp.concatenate([sums[:, :owned_count], sums[:, 2 * owned_count :]], axis=1)
            arrived = with_halo(outgoing, (("sn", 1),), owned_count)
            terms = (
                sums[:, owned_count : 2 * owned_count]
                + arrived[:, :owned_count]
                + arrived[:, 3 * owned_count :]
            )
            reduced = (solved[height].astype(jnp.float32) - terms).astype(jnp.bfloat16)
        else:
            reduced = solved[height]
        answer = jnp.einsum(
            "rka,kab->rkb", reduced, diag_inv[height], preferred_element_type=jnp.float32
        ).astype(jnp.bfloat16)
        answers = answers.at[:, height * owned_count : (height + 1) * owned_count].set(answer)
        results[height] = answer
    combined = jnp.concatenate(results, axis=1).reshape(columns, levels, owned_count * block_rows)
    return lax.all_to_all(combined, "rhs", split_axis=2, concat_axis=0, tiled=True)


def solution(mesh):
    placed = (
        P(None, None, ("sn", "rhs")),
        P(None, "sn", None, None),
        P(None, "sn", None, None),
        P(),
        P(),
    )
    return jax.shard_map(
        on_device,
        mesh=mesh,
        in_specs=placed,
        out_specs=P(None, None, ("sn", "rhs")),
        check_vma=False,
    )
```

profile of v0, /device:TPU:1, one launch (start us, length us, event | category | flops | bytes accessed | tf_op | source)
XLA Modules:
  0.0 254.7 jit_solution(10722660862467126953)
XLA Ops:
  0.0 1.8 copy.167
  1.8 1.7 reshape.403
  3.6 10.3 %all-to-all-start = ((f32[8,1,16384]{2,1,0:T(1,128)}), f32[8,1,16384]{2,1,0:T(1,128)S(1)}, u32[]{:S(2)}, u32[]{:S(2)}) async-start(f32[8,1,16384]{2,1,0:T(1,128)} %reshape.403), calls=%async_computation | async-start | bytes 1048576 | tf_op jit(solution)/shard_map/all_to_all | solution.py:29
  15.5 7.8 %all-to-all-done = f32[8,1,16384]{2,1,0:T(1,128)S(1)} async-done(((f32[8,1,16384]{2,1,0:T(1,128)}), f32[8,1,16384]{2,1,0:T(1,128)S(1)}, u32[]{:S(2)}, u32[]{:S(2)}) %all-to-all-start) | async-done | bytes 524320 | tf_op jit(solution)/shard_map/all_to_all | solution.py:29
  23.8 1.9 reduce.14
  27.3 1.0 fusion
  28.3 9.0 %collective-permute-start.1 = (bf16[64,2,128]{2,0,1:T(8,128)(2,1)S(1)}, bf16[64,2,128]{2,0,1:T(8,128)(2,1)S(1)}, u32[]{:S(2)}, u32[]{:S(2)}) collective-permute-start(bf16[64,2,128]{2,0,1:T(8,128)(2,1)S(1)} %fusion), channel_id=1, source_target_pairs={{8,0},{16,8},{24,16},{32,24},{40,32},{48,40},{56,48},{64,56},{72,6... | collective-permute-start | bytes 98312 | tf_op jit(solution)/shard_map/ppermute | solution.py:15
  37.3 1.9 collective-permute-start
  39.4 5.9 %collective-permute-done = bf16[64,2,128]{2,0,1:T(8,128)(2,1)S(1)} collective-permute-done((bf16[64,2,128]{2,0,1:T(8,128)(2,1)S(1)}, bf16[64,2,128]{2,0,1:T(8,128)(2,1)S(1)}, u32[]{:S(2)}, u32[]{:S(2)}) %collective-permute-start) | collective-permute-done | bytes 32800 | tf_op jit(solution)/shard_map/ppermute | solution.py:14
  45.9 1.8 convolution_bitcast_fusion.13
  48.9 1.9 collective-permute-start.3
  50.8 3.4 %collective-permute-start.2 = (bf16[64,2,128]{2,0,1:T(8,128)(2,1)S(1)}, bf16[64,2,128]{2,0,1:T(8,128)(2,1)S(1)}, u32[]{:S(2)}, u32[]{:S(2)}) collective-permute-start(bf16[64,2,128]{2,0,1:T(8,128)(2,1)S(1)} %fusion.1), channel_id=1, source_target_pairs={{0,8},{8,16},{16,24},{24,32},{32,40},{40,48},{48,56},{56,64},{64,7... | collective-permute-start | bytes 98312 | tf_op jit(solution)/shard_map/ppermute | solution.py:14
  54.3 4.5 %collective-permute-done.2 = bf16[64,2,128]{2,0,1:T(8,128)(2,1)S(1)} collective-permute-done((bf16[64,2,128]{2,0,1:T(8,128)(2,1)S(1)}, bf16[64,2,128]{2,0,1:T(8,128)(2,1)S(1)}, u32[]{:S(2)}, u32[]{:S(2)}) %collective-permute-start.2) | collective-permute-done | bytes 32800 | tf_op jit(solution)/shard_map/ppermute | solution.py:14
  59.5 1.8 convolution_bitcast_fusion.12
  62.6 1.9 collective-permute-start.5
  64.5 3.4 %collective-permute-start.4 = (bf16[64,2,128]{2,0,1:T(8,128)(2,1)S(1)}, bf16[64,2,128]{2,0,1:T(8,128)(2,1)S(1)}, u32[]{:S(2)}, u32[]{:S(2)}) collective-permute-start(bf16[64,2,128]{2,0,1:T(8,128)(2,1)S(1)} %fusion.2), channel_id=1, source_target_pairs={{0,8},{8,16},{16,24},{24,32},{32,40},{40,48},{48,56},{56,64},{64,7... | collective-permute-start | bytes 98312 | tf_op jit(solution)/shard_map/ppermute | solution.py:14
  68.0 4.5 %collective-permute-done.4 = bf16[64,2,128]{2,0,1:T(8,128)(2,1)S(1)} collective-permute-done((bf16[64,2,128]{2,0,1:T(8,128)(2,1)S(1)}, bf16[64,2,128]{2,0,1:T(8,128)(2,1)S(1)}, u32[]{:S(2)}, u32[]{:S(2)}) %collective-permute-start.4) | collective-permute-done | bytes 32800 | tf_op jit(solution)/shard_map/ppermute | solution.py:14
  73.2 1.8 convolution_bitcast_fusion.11
  76.2 1.9 collective-permute-start.7
  78.2 3.4 %collective-permute-start.6 = (bf16[64,2,128]{2,0,1:T(8,128)(2,1)S(1)}, bf16[64,2,128]{2,0,1:T(8,128)(2,1)S(1)}, u32[]{:S(2)}, u32[]{:S(2)}) collective-permute-start(bf16[64,2,128]{2,0,1:T(8,128)(2,1)S(1)} %fusion.3), channel_id=1, source_target_pairs={{0,8},{8,16},{16,24},{24,32},{32,40},{40,48},{48,56},{56,64},{64,7... | collective-permute-start | bytes 98312 | tf_op jit(solution)/shard_map/ppermute | solution.py:14
  81.6 4.5 %collective-permute-done.6 = bf16[64,2,128]{2,0,1:T(8,128)(2,1)S(1)} collective-permute-done((bf16[64,2,128]{2,0,1:T(8,128)(2,1)S(1)}, bf16[64,2,128]{2,0,1:T(8,128)(2,1)S(1)}, u32[]{:S(2)}, u32[]{:S(2)}) %collective-permute-start.6) | collective-permute-done | bytes 32800 | tf_op jit(solution)/shard_map/ppermute | solution.py:14
  86.8 1.8 convolution_bitcast_fusion.10
  89.9 1.9 collective-permute-start.9
  91.8 3.5 %collective-permute-start.8 = (bf16[64,2,128]{2,0,1:T(8,128)(2,1)S(1)}, bf16[64,2,128]{2,0,1:T(8,128)(2,1)S(1)}, u32[]{:S(2)}, u32[]{:S(2)}) collective-permute-start(bf16[64,2,128]{2,0,1:T(8,128)(2,1)S(1)} %fusion.4), channel_id=1, source_target_pairs={{0,8},{8,16},{16,24},{24,32},{32,40},{40,48},{48,56},{56,64},{64,7... | collective-permute-start | bytes 98312 | tf_op jit(solution)/shard_map/ppermute | solution.py:14
  95.5 4.5 %collective-permute-done.8 = bf16[64,2,128]{2,0,1:T(8,128)(2,1)S(1)} collective-permute-done((bf16[64,2,128]{2,0,1:T(8,128)(2,1)S(1)}, bf16[64,2,128]{2,0,1:T(8,128)(2,1)S(1)}, u32[]{:S(2)}, u32[]{:S(2)}) %collective-permute-start.8) | collective-permute-done | bytes 32800 | tf_op jit(solution)/shard_map/ppermute | solution.py:14
  100.6 1.8 convolution_bitcast_fusion.9
  103.7 1.9 collective-permute-start.11
  105.6 3.4 %collective-permute-start.10 = (bf16[64,2,128]{2,0,1:T(8,128)(2,1)S(1)}, bf16[64,2,128]{2,0,1:T(8,128)(2,1)S(1)}, u32[]{:S(2)}, u32[]{:S(2)}) collective-permute-start(bf16[64,2,128]{2,0,1:T(8,128)(2,1)S(1)} %fusion.5), channel_id=1, source_target_pairs={{0,8},{8,16},{16,24},{24,32},{32,40},{40,48},{48,56},{56,64},{64,7... | collective-permute-start | bytes 98312 | tf_op jit(solution)/shard_map/ppermute | solution.py:14
  109.1 4.5 %collective-permute-done.10 = bf16[64,2,128]{2,0,1:T(8,128)(2,1)S(1)} collective-permute-done((bf16[64,2,128]{2,0,1:T(8,128)(2,1)S(1)}, bf16[64,2,128]{2,0,1:T(8,128)(2,1)S(1)}, u32[]{:S(2)}, u32[]{:S(2)}) %collective-permute-start.10) | collective-permute-done | bytes 32800 | tf_op jit(solution)/shard_map/ppermute | solution.py:14
  114.2 1.8 convolution_bitcast_fusion.8
  117.3 1.9 collective-permute-start.13
  119.2 3.4 %collective-permute-start.12 = (bf16[64,2,128]{2,0,1:T(8,128)(2,1)S(1)}, bf16[64,2,128]{2,0,1:T(8,128)(2,1)S(1)}, u32[]{:S(2)}, u32[]{:S(2)}) collective-permute-start(bf16[64,2,128]{2,0,1:T(8,128)(2,1)S(1)} %fusion.6), channel_id=1, source_target_pairs={{0,8},{8,16},{16,24},{24,32},{32,40},{40,48},{48,56},{56,64},{64,7... | collective-permute-start | bytes 98312 | tf_op jit(solution)/shard_map/ppermute | solution.py:14
  122.7 4.5 %collective-permute-done.12 = bf16[64,2,128]{2,0,1:T(8,128)(2,1)S(1)} collective-permute-done((bf16[64,2,128]{2,0,1:T(8,128)(2,1)S(1)}, bf16[64,2,128]{2,0,1:T(8,128)(2,1)S(1)}, u32[]{:S(2)}, u32[]{:S(2)}) %collective-permute-start.12) | collective-permute-done | bytes 32800 | tf_op jit(solution)/shard_map/ppermute | solution.py:14
  127.9 1.8 convolution_bitcast_fusion.7
  131.7 1.5 convolution_bitcast_fusion.6
  134.1 1.9 collective-permute-start.15
  136.0 3.4 %collective-permute-start.14 = (f32[64,2,128]{2,0,1:T(8,128)S(1)}, f32[64,2,128]{2,0,1:T(8,128)S(1)}, u32[]{:S(2)}, u32[]{:S(2)}) collective-permute-start(f32[64,2,128]{2,0,1:T(8,128)S(1)} %get-tuple-element.138), channel_id=1, source_target_pairs={{0,8},{8,16},{16,24},{24,32},{32,40},{40,48},{48,56},{56,64},{64,7... | collective-permute-start | bytes 196616 | tf_op jit(solution)/shard_map/ppermute | solution.py:14
  139.4 4.9 %collective-permute-done.14 = f32[64,2,128]{2,0,1:T(8,128)S(1)} collective-permute-done((f32[64,2,128]{2,0,1:T(8,128)S(1)}, f32[64,2,128]{2,0,1:T(8,128)S(1)}, u32[]{:S(2)}, u32[]{:S(2)}) %collective-permute-start.14) | collective-permute-done | bytes 65568 | tf_op jit(solution)/shard_map/ppermute | solution.py:14
  145.1 1.5 convolution_bitcast_fusion.5
  147.5 1.9 collective-permute-start.17
  149.5 3.4 %collective-permute-start.16 = (f32[64,2,128]{2,0,1:T(8,128)S(1)}, f32[64,2,128]{2,0,1:T(8,128)S(1)}, u32[]{:S(2)}, u32[]{:S(2)}) collective-permute-start(f32[64,2,128]{2,0,1:T(8,128)S(1)} %get-tuple-element.136), channel_id=1, source_target_pairs={{0,8},{8,16},{16,24},{24,32},{32,40},{40,48},{48,56},{56,64},{64,7... | collective-permute-start | bytes 196616 | tf_op jit(solution)/shard_map/ppermute | solution.py:14
  152.9 4.9 %collective-permute-done.16 = f32[64,2,128]{2,0,1:T(8,128)S(1)} collective-permute-done((f32[64,2,128]{2,0,1:T(8,128)S(1)}, f32[64,2,128]{2,0,1:T(8,128)S(1)}, u32[]{:S(2)}, u32[]{:S(2)}) %collective-permute-start.16) | collective-permute-done | bytes 65568 | tf_op jit(solution)/shard_map/ppermute | solution.py:14
  158.6 1.5 convolution_bitcast_fusion.4
  161.0 1.9 collective-permute-start.19
  162.9 3.4 %collective-permute-start.18 = (f32[64,2,128]{2,0,1:T(8,128)S(1)}, f32[64,2,128]{2,0,1:T(8,128)S(1)}, u32[]{:S(2)}, u32[]{:S(2)}) collective-permute-start(f32[64,2,128]{2,0,1:T(8,128)S(1)} %get-tuple-element.134), channel_id=1, source_target_pairs={{0,8},{8,16},{16,24},{24,32},{32,40},{40,48},{48,56},{56,64},{64,7... | collective-permute-start | bytes 196616 | tf_op jit(solution)/shard_map/ppermute | solution.py:14
  166.3 4.9 %collective-permute-done.18 = f32[64,2,128]{2,0,1:T(8,128)S(1)} collective-permute-done((f32[64,2,128]{2,0,1:T(8,128)S(1)}, f32[64,2,128]{2,0,1:T(8,128)S(1)}, u32[]{:S(2)}, u32[]{:S(2)}) %collective-permute-start.18) | collective-permute-done | bytes 65568 | tf_op jit(solution)/shard_map/ppermute | solution.py:14
  172.0 1.5 convolution_bitcast_fusion.3
  174.4 1.9 collective-permute-start.21
  176.4 3.6 %collective-permute-start.20 = (f32[64,2,128]{2,0,1:T(8,128)S(1)}, f32[64,2,128]{2,0,1:T(8,128)S(1)}, u32[]{:S(2)}, u32[]{:S(2)}) collective-permute-start(f32[64,2,128]{2,0,1:T(8,128)S(1)} %get-tuple-element.132), channel_id=1, source_target_pairs={{0,8},{8,16},{16,24},{24,32},{32,40},{40,48},{48,56},{56,64},{64,7... | collective-permute-start | bytes 196616 | tf_op jit(solution)/shard_map/ppermute | solution.py:14
  180.0 4.7 %collective-permute-done.20 = f32[64,2,128]{2,0,1:T(8,128)S(1)} collective-permute-done((f32[64,2,128]{2,0,1:T(8,128)S(1)}, f32[64,2,128]{2,0,1:T(8,128)S(1)}, u32[]{:S(2)}, u32[]{:S(2)}) %collective-permute-start.20) | collective-permute-done | bytes 65568 | tf_op jit(solution)/shard_map/ppermute | solution.py:14
  185.5 1.5 convolution_bitcast_fusion.2
  187.9 1.9 collective-permute-start.23
  189.8 3.4 %collective-permute-start.22 = (f32[64,2,128]{2,0,1:T(8,128)S(1)}, f32[64,2,128]{2,0,1:T(8,128)S(1)}, u32[]{:S(2)}, u32[]{:S(2)}) collective-permute-start(f32[64,2,128]{2,0,1:T(8,128)S(1)} %get-tuple-element.130), channel_id=1, source_target_pairs={{0,8},{8,16},{16,24},{24,32},{32,40},{40,48},{48,56},{56,64},{64,7... | collective-permute-start | bytes 196616 | tf_op jit(solution)/shard_map/ppermute | solution.py:14
  193.2 5.2 %collective-permute-done.22 = f32[64,2,128]{2,0,1:T(8,128)S(1)} collective-permute-done((f32[64,2,128]{2,0,1:T(8,128)S(1)}, f32[64,2,128]{2,0,1:T(8,128)S(1)}, u32[]{:S(2)}, u32[]{:S(2)}) %collective-permute-start.22) | collective-permute-done | bytes 65568 | tf_op jit(solution)/shard_map/ppermute | solution.py:14
  199.3 1.5 convolution_bitcast_fusion.1
  201.7 1.9 collective-permute-start.25
  203.6 3.4 %collective-permute-start.24 = (f32[64,2,128]{2,0,1:T(8,128)S(1)}, f32[64,2,128]{2,0,1:T(8,128)S(1)}, u32[]{:S(2)}, u32[]{:S(2)}) collective-permute-start(f32[64,2,128]{2,0,1:T(8,128)S(1)} %get-tuple-element.128), channel_id=1, source_target_pairs={{0,8},{8,16},{16,24},{24,32},{32,40},{40,48},{48,56},{56,64},{64,7... | collective-permute-start | bytes 196616 | tf_op jit(solution)/shard_map/ppermute | solution.py:14
  207.0 4.9 %collective-permute-done.24 = f32[64,2,128]{2,0,1:T(8,128)S(1)} collective-permute-done((f32[64,2,128]{2,0,1:T(8,128)S(1)}, f32[64,2,128]{2,0,1:T(8,128)S(1)}, u32[]{:S(2)}, u32[]{:S(2)}) %collective-permute-start.24) | collective-permute-done | bytes 65568 | tf_op jit(solution)/shard_map/ppermute | solution.py:14
  212.7 1.5 convolution_bitcast_fusion
  215.1 1.9 collective-permute-start.27
  217.1 3.4 %collective-permute-start.26 = (f32[64,2,128]{2,0,1:T(8,128)S(1)}, f32[64,2,128]{2,0,1:T(8,128)S(1)}, u32[]{:S(2)}, u32[]{:S(2)}) collective-permute-start(f32[64,2,128]{2,0,1:T(8,128)S(1)} %get-tuple-element.126), channel_id=1, source_target_pairs={{0,8},{8,16},{16,24},{24,32},{32,40},{40,48},{48,56},{56,64},{64,7... | collective-permute-start | bytes 196616 | tf_op jit(solution)/shard_map/ppermute | solution.py:14
  220.4 4.9 %collective-permute-done.26 = f32[64,2,128]{2,0,1:T(8,128)S(1)} collective-permute-done((f32[64,2,128]{2,0,1:T(8,128)S(1)}, f32[64,2,128]{2,0,1:T(8,128)S(1)}, u32[]{:S(2)}, u32[]{:S(2)}) %collective-permute-start.26) | collective-permute-done | bytes 65568 | tf_op jit(solution)/shard_map/ppermute | solution.py:14
  226.7 26.2 %all_to_all.33 = bf16[8,2,8192]{2,1,0:T(2,128)(2,1)S(1)} all-to-all(bf16[8,2,8192]{2,1,0:T(2,128)(2,1)S(1)} %reshape.405), channel_id=1, replica_groups=mesh['sn'=64,'rhs'=8] {'rhs'}, dimensions={0} | all-to-all | bytes 524288 | tf_op jit(solution)/shard_map/all_to_all | solution.py:91
  253.6 1.0 all_to_all.30
  (134 shorter events, 31.0 us)
Async XLA Ops:
  3.6 19.8 %all-to-all-start = ((f32[8,1,16384]{2,1,0:T(1,128)}), f32[8,1,16384]{2,1,0:T(1,128)S(1)}, u32[]{:S(2)}, u32[]{:S(2)}) async-start(f32[8,1,16384]{2,1,0:T(1,128)} %reshape.403), calls=%async_computation | async-start | bytes 1048576 | tf_op jit(solution)/shard_map/all_to_all | solution.py:29
  27.1 21.6 %copy-start = (bf16[8,2,128,128]{3,2,1,0:T(8,128)(2,1)S(1)}, bf16[8,2,128,128]{3,2,1,0:T(8,128)(2,1)}, u32[]{:S(2)}) copy-start(bf16[8,2,128,128]{3,2,1,0:T(8,128)(2,1)} %param.24) | copy-start | bytes 1572868
  28.3 11.1 %collective-permute-start.1 = (bf16[64,2,128]{2,0,1:T(8,128)(2,1)S(1)}, bf16[64,2,128]{2,0,1:T(8,128)(2,1)S(1)}, u32[]{:S(2)}, u32[]{:S(2)}) collective-permute-start(bf16[64,2,128]{2,0,1:T(8,128)(2,1)S(1)} %fusion), channel_id=1, source_target_pairs={{8,0},{16,8},{24,16},{32,24},{40,32},{48,40},{56,48},{64,56},{72,6... | collective-permute-start | bytes 98312 | tf_op jit(solution)/shard_map/ppermute | solution.py:15
  37.3 8.0 %collective-permute-start = (bf16[64,2,128]{2,0,1:T(8,128)(2,1)S(1)}, bf16[64,2,128]{2,0,1:T(8,128)(2,1)S(1)}, u32[]{:S(2)}, u32[]{:S(2)}) collective-permute-start(bf16[64,2,128]{2,0,1:T(8,128)(2,1)S(1)} %fusion), channel_id=1, source_target_pairs={{0,8},{8,16},{16,24},{24,32},{32,40},{40,48},{48,56},{56,64},{64,7... | collective-permute-start | bytes 98312 | tf_op jit(solution)/shard_map/ppermute | solution.py:14
  48.9 5.4 %collective-permute-start.3 = (bf16[64,2,128]{2,0,1:T(8,128)(2,1)S(1)}, bf16[64,2,128]{2,0,1:T(8,128)(2,1)S(1)}, u32[]{:S(2)}, u32[]{:S(2)}) collective-permute-start(bf16[64,2,128]{2,0,1:T(8,128)(2,1)S(1)} %fusion.1), channel_id=1, source_target_pairs={{8,0},{16,8},{24,16},{32,24},{40,32},{48,40},{56,48},{64,56},{72,6... | collective-permute-start | bytes 98312 | tf_op jit(solution)/shard_map/ppermute | solution.py:15
  50.8 8.0 %collective-permute-start.2 = (bf16[64,2,128]{2,0,1:T(8,128)(2,1)S(1)}, bf16[64,2,128]{2,0,1:T(8,128)(2,1)S(1)}, u32[]{:S(2)}, u32[]{:S(2)}) collective-permute-start(bf16[64,2,128]{2,0,1:T(8,128)(2,1)S(1)} %fusion.1), channel_id=1, source_target_pairs={{0,8},{8,16},{16,24},{24,32},{32,40},{40,48},{48,56},{56,64},{64,7... | collective-permute-start | bytes 98312 | tf_op jit(solution)/shard_map/ppermute | solution.py:14
  62.6 5.4 %collective-permute-start.5 = (bf16[64,2,128]{2,0,1:T(8,128)(2,1)S(1)}, bf16[64,2,128]{2,0,1:T(8,128)(2,1)S(1)}, u32[]{:S(2)}, u32[]{:S(2)}) collective-permute-start(bf16[64,2,128]{2,0,1:T(8,128)(2,1)S(1)} %fusion.2), channel_id=1, source_target_pairs={{8,0},{16,8},{24,16},{32,24},{40,32},{48,40},{56,48},{64,56},{72,6... | collective-permute-start | bytes 98312 | tf_op jit(solution)/shard_map/ppermute | solution.py:15
  64.5 8.0 %collective-permute-start.4 = (bf16[64,2,128]{2,0,1:T(8,128)(2,1)S(1)}, bf16[64,2,128]{2,0,1:T(8,128)(2,1)S(1)}, u32[]{:S(2)}, u32[]{:S(2)}) collective-permute-start(bf16[64,2,128]{2,0,1:T(8,128)(2,1)S(1)} %fusion.2), channel_id=1, source_target_pairs={{0,8},{8,16},{16,24},{24,32},{32,40},{40,48},{48,56},{56,64},{64,7... | collective-permute-start | bytes 98312 | tf_op jit(solution)/shard_map/ppermute | solution.py:14
  76.2 5.4 %collective-permute-start.7 = (bf16[64,2,128]{2,0,1:T(8,128)(2,1)S(1)}, bf16[64,2,128]{2,0,1:T(8,128)(2,1)S(1)}, u32[]{:S(2)}, u32[]{:S(2)}) collective-permute-start(bf16[64,2,128]{2,0,1:T(8,128)(2,1)S(1)} %fusion.3), channel_id=1, source_target_pairs={{8,0},{16,8},{24,16},{32,24},{40,32},{48,40},{56,48},{64,56},{72,6... | collective-permute-start | bytes 98312 | tf_op jit(solution)/shard_map/ppermute | solution.py:15
  78.2 8.0 %collective-permute-start.6 = (bf16[64,2,128]{2,0,1:T(8,128)(2,1)S(1)}, bf16[64,2,128]{2,0,1:T(8,128)(2,1)S(1)}, u32[]{:S(2)}, u32[]{:S(2)}) collective-permute-start(bf16[64,2,128]{2,0,1:T(8,128)(2,1)S(1)} %fusion.3), channel_id=1, source_target_pairs={{0,8},{8,16},{16,24},{24,32},{32,40},{40,48},{48,56},{56,64},{64,7... | collective-permute-start | bytes 98312 | tf_op jit(solution)/shard_map/ppermute | solution.py:14
  89.9 5.6 %collective-permute-start.9 = (bf16[64,2,128]{2,0,1:T(8,128)(2,1)S(1)}, bf16[64,2,128]{2,0,1:T(8,128)(2,1)S(1)}, u32[]{:S(2)}, u32[]{:S(2)}) collective-permute-start(bf16[64,2,128]{2,0,1:T(8,128)(2,1)S(1)} %fusion.4), channel_id=1, source_target_pairs={{8,0},{16,8},{24,16},{32,24},{40,32},{48,40},{56,48},{64,56},{72,6... | collective-permute-start | bytes 98312 | tf_op jit(solution)/shard_map/ppermute | solution.py:15
  91.8 8.2 %collective-permute-start.8 = (bf16[64,2,128]{2,0,1:T(8,128)(2,1)S(1)}, bf16[64,2,128]{2,0,1:T(8,128)(2,1)S(1)}, u32[]{:S(2)}, u32[]{:S(2)}) collective-permute-start(bf16[64,2,128]{2,0,1:T(8,128)(2,1)S(1)} %fusion.4), channel_id=1, source_target_pairs={{0,8},{8,16},{16,24},{24,32},{32,40},{40,48},{48,56},{56,64},{64,7... | collective-permute-start | bytes 98312 | tf_op jit(solution)/shard_map/ppermute | solution.py:14
  103.7 5.4 %collective-permute-start.11 = (bf16[64,2,128]{2,0,1:T(8,128)(2,1)S(1)}, bf16[64,2,128]{2,0,1:T(8,128)(2,1)S(1)}, u32[]{:S(2)}, u32[]{:S(2)}) collective-permute-start(bf16[64,2,128]{2,0,1:T(8,128)(2,1)S(1)} %fusion.5), channel_id=1, source_target_pairs={{8,0},{16,8},{24,16},{32,24},{40,32},{48,40},{56,48},{64,56},{72,6... | collective-permute-start | bytes 98312 | tf_op jit(solution)/shard_map/ppermute | solution.py:15
  105.6 8.0 %collective-permute-start.10 = (bf16[64,2,128]{2,0,1:T(8,128)(2,1)S(1)}, bf16[64,2,128]{2,0,1:T(8,128)(2,1)S(1)}, u32[]{:S(2)}, u32[]{:S(2)}) collective-permute-start(bf16[64,2,128]{2,0,1:T(8,128)(2,1)S(1)} %fusion.5), channel_id=1, source_target_pairs={{0,8},{8,16},{16,24},{24,32},{32,40},{40,48},{48,56},{56,64},{64,7... | collective-permute-start | bytes 98312 | tf_op jit(solution)/shard_map/ppermute | solution.py:14
  117.3 5.4 %collective-permute-start.13 = (bf16[64,2,128]{2,0,1:T(8,128)(2,1)S(1)}, bf16[64,2,128]{2,0,1:T(8,128)(2,1)S(1)}, u32[]{:S(2)}, u32[]{:S(2)}) collective-permute-start(bf16[64,2,128]{2,0,1:T(8,128)(2,1)S(1)} %fusion.6), channel_id=1, source_target_pairs={{8,0},{16,8},{24,16},{32,24},{40,32},{48,40},{56,48},{64,56},{72,6... | collective-permute-start | bytes 98312 | tf_op jit(solution)/shard_map/ppermute | solution.py:15
  119.2 8.0 %collective-permute-start.12 = (bf16[64,2,128]{2,0,1:T(8,128)(2,1)S(1)}, bf16[64,2,128]{2,0,1:T(8,128)(2,1)S(1)}, u32[]{:S(2)}, u32[]{:S(2)}) collective-permute-start(bf16[64,2,128]{2,0,1:T(8,128)(2,1)S(1)} %fusion.6), channel_id=1, source_target_pairs={{0,8},{8,16},{16,24},{24,32},{32,40},{40,48},{48,56},{56,64},{64,7... | collective-permute-start | bytes 98312 | tf_op jit(solution)/shard_map/ppermute | solution.py:14
  134.1 5.3 %collective-permute-start.15 = (f32[64,2,128]{2,0,1:T(8,128)S(1)}, f32[64,2,128]{2,0,1:T(8,128)S(1)}, u32[]{:S(2)}, u32[]{:S(2)}) collective-permute-start(f32[64,2,128]{2,0,1:T(8,128)S(1)} %get-tuple-element.139), channel_id=1, source_target_pairs={{8,0},{16,8},{24,16},{32,24},{40,32},{48,40},{56,48},{64,56},{72,6... | collective-permute-start | bytes 196616 | tf_op jit(solution)/shard_map/ppermute | solution.py:15
  136.0 8.3 %collective-permute-start.14 = (f32[64,2,128]{2,0,1:T(8,128)S(1)}, f32[64,2,128]{2,0,1:T(8,128)S(1)}, u32[]{:S(2)}, u32[]{:S(2)}) collective-permute-start(f32[64,2,128]{2,0,1:T(8,128)S(1)} %get-tuple-element.138), channel_id=1, source_target_pairs={{0,8},{8,16},{16,24},{24,32},{32,40},{40,48},{48,56},{56,64},{64,7... | collective-permute-start | bytes 196616 | tf_op jit(solution)/shard_map/ppermute | solution.py:14
  147.5 5.3 %collective-permute-start.17 = (f32[64,2,128]{2,0,1:T(8,128)S(1)}, f32[64,2,128]{2,0,1:T(8,128)S(1)}, u32[]{:S(2)}, u32[]{:S(2)}) collective-permute-start(f32[64,2,128]{2,0,1:T(8,128)S(1)} %get-tuple-element.137), channel_id=1, source_target_pairs={{8,0},{16,8},{24,16},{32,24},{40,32},{48,40},{56,48},{64,56},{72,6... | collective-permute-start | bytes 196616 | tf_op jit(solution)/shard_map/ppermute | solution.py:15
  149.5 8.3 %collective-permute-start.16 = (f32[64,2,128]{2,0,1:T(8,128)S(1)}, f32[64,2,128]{2,0,1:T(8,128)S(1)}, u32[]{:S(2)}, u32[]{:S(2)}) collective-permute-start(f32[64,2,128]{2,0,1:T(8,128)S(1)} %get-tuple-element.136), channel_id=1, source_target_pairs={{0,8},{8,16},{16,24},{24,32},{32,40},{40,48},{48,56},{56,64},{64,7... | collective-permute-start | bytes 196616 | tf_op jit(solution)/shard_map/ppermute | solution.py:14
  161.0 5.3 %collective-permute-start.19 = (f32[64,2,128]{2,0,1:T(8,128)S(1)}, f32[64,2,128]{2,0,1:T(8,128)S(1)}, u32[]{:S(2)}, u32[]{:S(2)}) collective-permute-start(f32[64,2,128]{2,0,1:T(8,128)S(1)} %get-tuple-element.135), channel_id=1, source_target_pairs={{8,0},{16,8},{24,16},{32,24},{40,32},{48,40},{56,48},{64,56},{72,6... | collective-permute-start | bytes 196616 | tf_op jit(solution)/shard_map/ppermute | solution.py:15
  162.9 8.3 %collective-permute-start.18 = (f32[64,2,128]{2,0,1:T(8,128)S(1)}, f32[64,2,128]{2,0,1:T(8,128)S(1)}, u32[]{:S(2)}, u32[]{:S(2)}) collective-permute-start(f32[64,2,128]{2,0,1:T(8,128)S(1)} %get-tuple-element.134), channel_id=1, source_target_pairs={{0,8},{8,16},{16,24},{24,32},{32,40},{40,48},{48,56},{56,64},{64,7... | collective-permute-start | bytes 196616 | tf_op jit(solution)/shard_map/ppermute | solution.py:14
  174.4 5.5 %collective-permute-start.21 = (f32[64,2,128]{2,0,1:T(8,128)S(1)}, f32[64,2,128]{2,0,1:T(8,128)S(1)}, u32[]{:S(2)}, u32[]{:S(2)}) collective-permute-start(f32[64,2,128]{2,0,1:T(8,128)S(1)} %get-tuple-element.133), channel_id=1, source_target_pairs={{8,0},{16,8},{24,16},{32,24},{40,32},{48,40},{56,48},{64,56},{72,6... | collective-permute-start | bytes 196616 | tf_op jit(solution)/shard_map/ppermute | solution.py:15
  176.4 8.3 %collective-permute-start.20 = (f32[64,2,128]{2,0,1:T(8,128)S(1)}, f32[64,2,128]{2,0,1:T(8,128)S(1)}, u32[]{:S(2)}, u32[]{:S(2)}) collective-permute-start(f32[64,2,128]{2,0,1:T(8,128)S(1)} %get-tuple-element.132), channel_id=1, source_target_pairs={{0,8},{8,16},{16,24},{24,32},{32,40},{40,48},{48,56},{56,64},{64,7... | collective-permute-start | bytes 196616 | tf_op jit(solution)/shard_map/ppermute | solution.py:14
  187.9 5.4 %collective-permute-start.23 = (f32[64,2,128]{2,0,1:T(8,128)S(1)}, f32[64,2,128]{2,0,1:T(8,128)S(1)}, u32[]{:S(2)}, u32[]{:S(2)}) collective-permute-start(f32[64,2,128]{2,0,1:T(8,128)S(1)} %get-tuple-element.131), channel_id=1, source_target_pairs={{8,0},{16,8},{24,16},{32,24},{40,32},{48,40},{56,48},{64,56},{72,6... | collective-permute-start | bytes 196616 | tf_op jit(solution)/shard_map/ppermute | solution.py:15
  189.8 8.7 %collective-permute-start.22 = (f32[64,2,128]{2,0,1:T(8,128)S(1)}, f32[64,2,128]{2,0,1:T(8,128)S(1)}, u32[]{:S(2)}, u32[]{:S(2)}) collective-permute-start(f32[64,2,128]{2,0,1:T(8,128)S(1)} %get-tuple-element.130), channel_id=1, source_target_pairs={{0,8},{8,16},{16,24},{24,32},{32,40},{40,48},{48,56},{56,64},{64,7... | collective-permute-start | bytes 196616 | tf_op jit(solution)/shard_map/ppermute | solution.py:14
  201.7 5.3 %collective-permute-start.25 = (f32[64,2,128]{2,0,1:T(8,128)S(1)}, f32[64,2,128]{2,0,1:T(8,128)S(1)}, u32[]{:S(2)}, u32[]{:S(2)}) collective-permute-start(f32[64,2,128]{2,0,1:T(8,128)S(1)} %get-tuple-element.129), channel_id=1, source_target_pairs={{8,0},{16,8},{24,16},{32,24},{40,32},{48,40},{56,48},{64,56},{72,6... | collective-permute-start | bytes 196616 | tf_op jit(solution)/shard_map/ppermute | solution.py:15
  203.6 8.3 %collective-permute-start.24 = (f32[64,2,128]{2,0,1:T(8,128)S(1)}, f32[64,2,128]{2,0,1:T(8,128)S(1)}, u32[]{:S(2)}, u32[]{:S(2)}) collective-permute-start(f32[64,2,128]{2,0,1:T(8,128)S(1)} %get-tuple-element.128), channel_id=1, source_target_pairs={{0,8},{8,16},{16,24},{24,32},{32,40},{40,48},{48,56},{56,64},{64,7... | collective-permute-start | bytes 196616 | tf_op jit(solution)/shard_map/ppermute | solution.py:14
  215.1 5.3 %collective-permute-start.27 = (f32[64,2,128]{2,0,1:T(8,128)S(1)}, f32[64,2,128]{2,0,1:T(8,128)S(1)}, u32[]{:S(2)}, u32[]{:S(2)}) collective-permute-start(f32[64,2,128]{2,0,1:T(8,128)S(1)} %get-tuple-element.127), channel_id=1, source_target_pairs={{8,0},{16,8},{24,16},{32,24},{40,32},{48,40},{56,48},{64,56},{72,6... | collective-permute-start | bytes 196616 | tf_op jit(solution)/shard_map/ppermute | solution.py:15
  217.1 8.3 %collective-permute-start.26 = (f32[64,2,128]{2,0,1:T(8,128)S(1)}, f32[64,2,128]{2,0,1:T(8,128)S(1)}, u32[]{:S(2)}, u32[]{:S(2)}) collective-permute-start(f32[64,2,128]{2,0,1:T(8,128)S(1)} %get-tuple-element.126), channel_id=1, source_target_pairs={{0,8},{8,16},{16,24},{24,32},{32,40},{40,48},{48,56},{56,64},{64,7... | collective-permute-start | bytes 196616 | tf_op jit(solution)/shard_map/ppermute | solution.py:14
where the time goes:
time: 256 us; the launch traced here: 255 us
  starting transfers between devices  90.3 us (35%)
  waiting for transfers between devices  75.4 us (29%)
  matrix products  38.1 us (15%)
  blocking collectives  26.2 us (10%)
  local copies, waits for them, and re-layouts  18.5 us (7%)
  other arithmetic  4.98 us (2%)
    ppermute x14, waiting for transfers between devices, with_halo(): before = lax.ppermute(last, axis, up)  67.5 us
    ppermute x14, starting transfers between devices, with_halo(): before = lax.ppermute(last, axis, up)  46 us
    ppermute x14, starting transfers between devices, with_halo(): after = lax.ppermute(initial, axis, down)  34 us
    all_to_all x1, blocking collectives, on_device(): lax.all_to_all(combined, 'rhs', split_axis=2, concat_axis=0, tiled=True)  26.2 us
    dot_general x7, matrix products, on_device(): jnp.einsum('rtb,tab->rta', picked, factor_tiles[height], preferred_elemen...  12.6 us
    dot_general x7, matrix products, on_device(): jnp.einsum('rta,tab->rtb', picked, factor_tiles[height], preferred_elemen...  10.7 us
    all_to_all x1, starting transfers between devices, on_device(): lax.all_to_all(lanczos_block, 'rhs', split_axis=0, concat_axis=2, tiled=T...  10.3 us
    all_to_all x1, waiting for transfers between devices, on_device(): lax.all_to_all(lanczos_block, 'rhs', split_axis=0, concat_axis=2, tiled=T...  7.83 us
  transfers between devices with their start and end apart: 29, of which 15 were waited for; matrix products, arithmetic and copies ran while one was open for 1% of the time, Pallas kernels for 0%

commit v1 on v0

v1 whole, which is shorter than its diff:
```python
import jax
import jax.numpy as jnp
from jax import lax
from jax.experimental import pallas as pl
from jax.experimental.pallas import tpu as pltpu
from jax.sharding import PartitionSpec as P

BF = jnp.bfloat16
F32 = jnp.float32


def build_operators(tiles, diag, row_slot, col_slot):
    levels, owned, b, _ = diag.shape
    count = tiles.shape[1]
    wide = 3 * owned * b
    tall = owned * b

    def body(row_ref, col_ref, t_ref, d_ref, *outs):
        s_refs, b_refs = outs[: levels - 1], outs[levels - 1 :]
        for l in range(levels - 1):
            s_refs[l][...] = jnp.zeros_like(s_refs[l])

            def add(t, carry):
                r = pl.multiple_of(row_ref[l, t] * b, b)
                c = pl.multiple_of(col_ref[l, t] * b, b)
                at = (pl.ds(r, b), pl.ds(c, b))
                s_refs[l][at] = s_refs[l][at] + t_ref[l, t]
                return carry

            lax.fori_loop(0, count, add, 0, unroll=4)
            for q in range(owned):
                rows = slice(q * b, (q + 1) * b)
                b_refs[l][rows, :] = jnp.dot(
                    d_ref[l + 1, q], s_refs[l][rows, :], preferred_element_type=F32
                ).astype(BF)

    shapes = [jax.ShapeDtypeStruct(((levels - 1 - l) * tall, wide), BF) for l in range(levels - 1)]
    shapes += [jax.ShapeDtypeStruct((tall, wide), BF) for _ in range(levels - 1)]
    vmem = pl.BlockSpec(memory_space=pltpu.VMEM)
    smem = pl.BlockSpec(memory_space=pltpu.SMEM)
    outs = pl.pallas_call(
        body,
        out_shape=shapes,
        in_specs=[smem, smem, vmem, vmem],
        out_specs=[vmem] * len(shapes),
        compiler_params=pltpu.CompilerParams(vmem_limit_bytes=40 * 2**20),
        cost_estimate=pl.CostEstimate(flops=4 * 10**8, bytes_accessed=24 * 2**20, transcendentals=0),
    )(row_slot, col_slot, tiles, diag)
    return outs[: levels - 1], outs[levels - 1 :]


def dot_t(a, w):
    return lax.dot_general(a, w, (((1,), (1,)), ((), ())), preferred_element_type=F32)


def dot_n(a, w):
    return lax.dot_general(a, w, (((1,), (0,)), ((), ())), preferred_element_type=F32)


def on_device(lanczos_block, diag_inv, factor_tiles, tile_rows, tile_cols):
    levels, owned, b = diag_inv.shape[:3]
    group_tiles = factor_tiles.shape[1]
    n = lax.axis_size("sn")
    own = lax.axis_index("sn")
    per_level = owned * n
    wide = owned * b
    odd = own % 2 == 1

    panels = lax.all_to_all(lanczos_block.astype(BF), "rhs", split_axis=0, concat_axis=2, tiled=True)
    columns = panels.shape[0]

    my_rows = lax.dynamic_slice_in_dim(tile_rows, own * group_tiles, group_tiles, 1)
    my_cols = lax.dynamic_slice_in_dim(tile_cols, own * group_tiles, group_tiles, 1)
    above = jnp.arange(1, levels, dtype=jnp.int32)[:, None]
    group = (jnp.arange(group_tiles, dtype=jnp.int32) // (group_tiles // 3))[None, :]
    row_slot = (my_rows // per_level - above) * owned + my_rows % owned
    col_slot = group * owned + my_cols % owned
    S, B = build_operators(factor_tiles, diag_inv, row_slot, col_slot)

    even_pairs = [[i, i + 1] for i in range(0, n, 2)]
    odd_swap = [(i, (i + 1) % n if i % 2 else (i - 1) % n) for i in range(n)]

    def diag_fwd(l, f):
        f = f.astype(BF).reshape(columns, owned, b)
        return jnp.einsum("rkb,kab->rka", f, diag_inv[l], preferred_element_type=F32).reshape(columns, wide)

    def diag_bwd(l, e):
        e = e.reshape(columns, owned, b)
        z = jnp.einsum("rka,kab->rkb", e, diag_inv[l], preferred_element_type=F32)
        return z.astype(BF).reshape(columns, wide)

    x = [panels[:, l, :].astype(F32) for l in range(levels)]
    y = [None] * levels
    y[0] = diag_fwd(0, x[0]).astype(BF)
    for l in range(levels - 1):
        far = lax.ppermute(y[l], "sn", odd_swap)
        near = lax.all_gather(y[l], "sn", axis_index_groups=even_pairs)
        y3 = jnp.concatenate(
            [jnp.where(odd, near[0], far), y[l], jnp.where(odd, far, near[1])], axis=1
        )
        y[l + 1] = (diag_fwd(l + 1, x[l + 1]) - dot_t(y3, B[l])).astype(BF)
        if l + 2 < levels:
            older = dot_t(y3, S[l][wide:])
            for k in range(l + 2, levels):
                x[k] = x[k] - older[:, (k - l - 2) * wide : (k - l - 1) * wide]

    z = [None] * levels
    e = y[levels - 1]
    z[levels - 1] = diag_bwd(levels - 1, e)
    for l in reversed(range(levels - 1)):
        part = dot_n(e, B[l])
        if l + 2 < levels:
            part = part + dot_n(jnp.concatenate(z[l + 2 :], axis=1), S[l][wide:])
        left, mid, right = (part[:, k * wide : (k + 1) * wide] for k in range(3))
        far = lax.ppermute(jnp.where(odd, right, left).astype(BF), "sn", odd_swap)
        near = lax.all_gather(jnp.where(odd, left, right).astype(BF), "sn", axis_index_groups=even_pairs)
        terms = mid + far.astype(F32) + jnp.where(odd, near[0], near[1]).astype(F32)
        e = (y[l].astype(F32) - terms).astype(BF)
        z[l] = diag_bwd(l, e)
    combined = jnp.stack(z, axis=1)
    return lax.all_to_all(combined, "rhs", split_axis=2, concat_axis=0, tiled=True)


def solution(mesh):
    placed = (
        P(None, None, ("sn", "rhs")),
        P(None, "sn", None, None),
        P(None, "sn", None, None),
        P(),
        P(),
    )
    return jax.shard_map(
        on_device,
        mesh=mesh,
        in_specs=placed,
        out_specs=P(None, None, ("sn", "rhs")),
        check_vma=False,
    )
```

time: 256 us -> 229 us (0.89)
  waiting for transfers between devices: 75.4 us -> 1.85 us
  blocking collectives: 26.2 us -> 79.5 us
  local copies, waits for them, and re-layouts: 18.5 us -> 43.4 us
  matrix products: 38.1 us -> 14.9 us
  starting transfers between devices: 90.3 us -> 74.4 us
  Pallas kernels: 0 us -> 7.02 us
    ppermute x28 -> x14, waiting for transfers between devices: 67.6 us -> 1.85 us  [the longest x7 1.61 us: on_device(): far = lax.ppermute(y[l], 'sn', odd_swap)]
    all_gather x0 -> x14, blocking collectives: none -> 49.9 us  [the longest x7 25.1 us: on_device(): near = lax.all_gather(y[l], 'sn', axis_index_groups=even_pairs)]
    dot_general x43 -> x42, matrix products: 38.1 us -> 14.9 us  [the longest x13 7.13 us: dot_t(): lax.dot_general(a, w, (((1,), (1,)), ((), ())), preferred_element_type=F32)]
    unnamed x21 -> x94, local copies, waits for them, and re-layouts: 5.67 us -> 25.3 us
    ppermute x28 -> x14, starting transfers between devices: 80.1 us -> 64.2 us  [the longest x7 33.4 us: on_device(): far = lax.ppermute(y[l], 'sn', odd_swap)]
    gather x14 -> x0, local copies, waits for them, and re-layouts: 8.71 us -> none  [the longest x7 4.36 us: on_device(): picked = jnp.take(answers, row_slot[height], axis=1)]
    all_to_all x1, waiting for transfers between devices: 7.83 us -> 0.01 us  [on_device(): lax.all_to_all(lanczos_block.astype(BF), 'rhs', split_axis=0, concat_axis...]
    pallas_call x0 -> x1, Pallas kernels: none -> 7.02 us  [build_operators(): pl.pallas_call(body, out_shape=shapes, in_specs=[smem, smem, vmem, vmem],...]
  transfers between devices with their start and end apart: 29 -> 15, of which waited for: 15 -> 5; matrix products, arithmetic and copies ran while one was open for 1% -> 10% of each run, Pallas kernels for 0% -> 3%
where the time goes in v1:
time: 229 us; the launch traced here: 226 us
  blocking collectives  79.5 us (35%)
  starting transfers between devices  74.4 us (32%)
  local copies, waits for them, and re-layouts  43.4 us (19%)
  matrix products  14.9 us (7%)
  Pallas kernels  7.02 us (3%)
  other arithmetic  4.46 us (2%)
    ppermute x7, starting transfers between devices, on_device(): far = lax.ppermute(y[l], 'sn', odd_swap)  33.4 us
    ppermute x7, starting transfers between devices, on_device(): far = lax.ppermute(jnp.where(odd, right, left).astype(BF), 'sn', odd_swap)  30.8 us
    all_to_all x1, blocking collectives, on_device(): lax.all_to_all(combined, 'rhs', split_axis=2, concat_axis=0, tiled=True)  29.6 us
    unnamed x94, local copies, waits for them, and re-layouts  25.3 us
    all_gather x7, blocking collectives, on_device(): near = lax.all_gather(y[l], 'sn', axis_index_groups=even_pairs)  25.1 us
    all_gather x7, blocking collectives, on_device(): lax.all_gather(jnp.where(odd, left, right).astype(BF), 'sn', axis_index_g...  24.8 us
    all_to_all x1, starting transfers between devices, on_device(): lax.all_to_all(lanczos_block.astype(BF), 'rhs', split_axis=0, concat_axis...  10.2 us
    dot_general x13, matrix products, dot_t(): lax.dot_general(a, w, (((1,), (1,)), ((), ())), preferred_element_type=F32)  7.13 us
  transfers between devices with their start and end apart: 15, of which 5 were waited for; matrix products, arithmetic and copies ran while one was open for 10% of the time, Pallas kernels for 3%

profile of v1, /device:TPU:1, one launch (start us, length us, event | category | flops | bytes accessed | tf_op | source)
XLA Modules:
  0.0 226.4 jit_solution(17212672267416844218)
XLA Ops:
  0.0 1.1 convert_element_type.297
  1.1 0.8 copy.177
  1.9 1.7 reshape.282
  3.6 10.2 %all-to-all-start = ((bf16[8,2,8192]{2,1,0:T(2,128)(2,1)}), bf16[8,2,8192]{2,1,0:T(2,128)(2,1)S(1)}, u32[]{:S(2)}, u32[]{:S(2)}) async-start(bf16[8,2,8192]{2,1,0:T(2,128)(2,1)} %reshape.282), calls=%async_computation | async-start | bytes 524288 | tf_op jit(solution)/shard_map/all_to_all | solution.py:69
  13.8 0.8 fusion.155
  14.6 7.0 %shard_map.55 = (bf16[1792,768]{1,0:T(8,128)(2,1)S(1)}, bf16[1536,768]{1,0:T(8,128)(2,1)S(1)}, bf16[1280,768]{1,0:T(8,128)(2,1)S(1)}, bf16[1024,768]{1,0:T(8,128...) custom-call(s32[7,24]{1,0:T(8,128)S(1)} %get-tuple-element.81.row_re, ...), custom_call_target="tpu_custom_call" | custom-call | flops 400000000 | bytes 25165824 | tf_op jit(solution)/shard_map/pallas_call | solution.py:41
  21.6 0.8 copy-done.1
  22.4 0.8 copy-done.2
  27.0 1.0 copy-done.14
  28.0 0.9 copy-done.16
  28.9 1.4 copy-done.18
  30.3 1.3 copy-done.20
  31.6 1.2 copy-done.22
  32.7 1.6 reshape.283
  34.3 2.7 %copy.178 = bf16[8,64,8,32]{1,3,0,2:T(8,128)(2,1)} copy(bf16[8,64,8,32]{3,2,1,0:T(8,128)(2,1)} %bitcast.316) | data formatting | bytes 524288 | tf_op jit(solution)/shard_map/all_to_all | solution.py:69
  37.0 1.8 fusion.177
  39.6 9.1 %collective-permute-start = (bf16[64,256]{1,0:T(8,128)(2,1)}, bf16[64,256]{1,0:T(8,128)(2,1)}, u32[]{:S(2)}, u32[]{:S(2)}) collective-permute-start(bf16[64,256]{1,0:T(8,128)(2,1)} %copy_bitcast_fusion.4), channel_id=1, source_target_pairs={{0,504},{8,16},{16,8},{24,32},{32,24},{40,48},{48,40},{56,64},{64,... | collective-permute-start | bytes 98312 | tf_op jit(solution)/shard_map/ppermute | solution.py:96
  48.8 1.5 copy.239
  51.1 1.5 copy.238
  52.6 1.5 copy.237
  54.1 0.9 copy.236
  55.8 3.7 %all_gather.82 = bf16[2,64,256]{2,1,0:T(8,128)(2,1)S(1)} all-gather(bf16[1,64,256]{2,1,0:T(8,128)(2,1)} %convert_element_type.302), channel_id=1, replica_groups={{0,8},{16,24},{32,40},{48,56},{64,72},{80,88},{96,104},{112,120},{128,1..., dimensions={0}, use_global_device_ids=true | all-gather | bytes 98304 | tf_op jit(solution)/shard_map/all_gather | solution.py:97
  59.5 0.8 fusion.150
  60.3 1.3 fusion.18
  61.6 1.9 collective-permute-start.1
  63.6 1.7 fusion.2
  65.5 3.6 %all-gather = bf16[128,256]{1,0:T(8,128)(2,1)S(1)} all-gather(bf16[64,256]{1,0:T(8,128)(2,1)S(1)} %fusion.18), channel_id=2, replica_groups={{0,8},{16,24},{32,40},{48,56},{64,72},{80,88},{96,104},{112,120},{128,1..., dimensions={0}, use_global_device_ids=true | all-gather | bytes 98304 | tf_op jit(solution)/shard_map/all_gather | solution.py:97
  69.9 6.1 %collective-permute-start.2 = (bf16[64,256]{1,0:T(8,128)(2,1)S(1)}, bf16[64,256]{1,0:T(8,128)(2,1)S(1)}, u32[]{:S(2)}, u32[]{:S(2)}) collective-permute-start(bf16[64,256]{1,0:T(8,128)(2,1)S(1)} %fusion.19), channel_id=1, source_target_pairs={{0,504},{8,16},{16,8},{24,32},{32,24},{40,48},{48,40},{56,64},{64,... | collective-permute-start | bytes 98312 | tf_op jit(solution)/shard_map/ppermute | solution.py:96
  76.8 3.9 %all-gather.1 = bf16[128,256]{1,0:T(8,128)(2,1)S(1)} all-gather(bf16[64,256]{1,0:T(8,128)(2,1)S(1)} %fusion.19), channel_id=3, replica_groups={{0,8},{16,24},{32,40},{48,56},{64,72},{80,88},{96,104},{112,120},{128,1..., dimensions={0}, use_global_device_ids=true | all-gather | bytes 98304 | tf_op jit(solution)/shard_map/all_gather | solution.py:97
  81.8 3.3 %collective-permute-start.3 = (bf16[64,256]{1,0:T(8,128)(2,1)S(1)}, bf16[64,256]{1,0:T(8,128)(2,1)S(1)}, u32[]{:S(2)}, u32[]{:S(2)}) collective-permute-start(bf16[64,256]{1,0:T(8,128)(2,1)S(1)} %fusion.20), channel_id=1, source_target_pairs={{0,504},{8,16},{16,8},{24,32},{32,24},{40,48},{48,40},{56,64},{64,... | collective-permute-start | bytes 98312 | tf_op jit(solution)/shard_map/ppermute | solution.py:96
  85.3 3.6 %all-gather.2 = bf16[128,256]{1,0:T(8,128)(2,1)S(1)} all-gather(bf16[64,256]{1,0:T(8,128)(2,1)S(1)} %fusion.20), channel_id=4, replica_groups={{0,8},{16,24},{32,40},{48,56},{64,72},{80,88},{96,104},{112,120},{128,1..., dimensions={0}, use_global_device_ids=true | all-gather | bytes 98304 | tf_op jit(solution)/shard_map/all_gather | solution.py:97
  88.8 0.9 collective-permute-done.3
  90.0 4.5 %collective-permute-start.4 = (bf16[64,256]{1,0:T(8,128)(2,1)S(1)}, bf16[64,256]{1,0:T(8,128)(2,1)S(1)}, u32[]{:S(2)}, u32[]{:S(2)}) collective-permute-start(bf16[64,256]{1,0:T(8,128)(2,1)S(1)} %fusion.21), channel_id=1, source_target_pairs={{0,504},{8,16},{16,8},{24,32},{32,24},{40,48},{48,40},{56,64},{64,... | collective-permute-start | bytes 98312 | tf_op jit(solution)/shard_map/ppermute | solution.py:96
  95.1 3.6 %all-gather.3 = bf16[128,256]{1,0:T(8,128)(2,1)S(1)} all-gather(bf16[64,256]{1,0:T(8,128)(2,1)S(1)} %fusion.21), channel_id=5, replica_groups={{0,8},{16,24},{32,40},{48,56},{64,72},{80,88},{96,104},{112,120},{128,1..., dimensions={0}, use_global_device_ids=true | all-gather | bytes 98304 | tf_op jit(solution)/shard_map/all_gather | solution.py:97
  99.6 4.2 %collective-permute-start.5 = (bf16[64,256]{1,0:T(8,128)(2,1)S(1)}, bf16[64,256]{1,0:T(8,128)(2,1)S(1)}, u32[]{:S(2)}, u32[]{:S(2)}) collective-permute-start(bf16[64,256]{1,0:T(8,128)(2,1)S(1)} %fusion.22), channel_id=1, source_target_pairs={{0,504},{8,16},{16,8},{24,32},{32,24},{40,48},{48,40},{56,64},{64,... | collective-permute-start | bytes 98312 | tf_op jit(solution)/shard_map/ppermute | solution.py:96
  103.9 3.4 %all-gather.4 = bf16[128,256]{1,0:T(8,128)(2,1)S(1)} all-gather(bf16[64,256]{1,0:T(8,128)(2,1)S(1)} %fusion.22), channel_id=6, replica_groups={{0,8},{16,24},{32,40},{48,56},{64,72},{80,88},{96,104},{112,120},{128,1..., dimensions={0}, use_global_device_ids=true | all-gather | bytes 98304 | tf_op jit(solution)/shard_map/all_gather | solution.py:97
  107.8 4.2 %collective-permute-start.6 = (bf16[64,256]{1,0:T(8,128)(2,1)S(1)}, bf16[64,256]{1,0:T(8,128)(2,1)S(1)}, u32[]{:S(2)}, u32[]{:S(2)}) collective-permute-start(bf16[64,256]{1,0:T(8,128)(2,1)S(1)} %fusion.23), channel_id=1, source_target_pairs={{0,504},{8,16},{16,8},{24,32},{32,24},{40,48},{48,40},{56,64},{64,... | collective-permute-start | bytes 98312 | tf_op jit(solution)/shard_map/ppermute | solution.py:96
  112.5 3.4 %all-gather.5 = bf16[128,256]{1,0:T(8,128)(2,1)S(1)} all-gather(bf16[64,256]{1,0:T(8,128)(2,1)S(1)} %fusion.23), channel_id=7, replica_groups={{0,8},{16,24},{32,40},{48,56},{64,72},{80,88},{96,104},{112,120},{128,1..., dimensions={0}, use_global_device_ids=true | all-gather | bytes 98304 | tf_op jit(solution)/shard_map/all_gather | solution.py:97
  116.6 4.4 %collective-permute-start.7 = (bf16[64,256]{1,0:T(8,128)(2,1)S(1)}, bf16[64,256]{1,0:T(8,128)(2,1)S(1)}, u32[]{:S(2)}, u32[]{:S(2)}) collective-permute-start(bf16[64,256]{1,0:T(8,128)(2,1)S(1)} %get-tuple-element.56), channel_id=1, source_target_pairs={{0,504},{8,16},{16,8},{24,32},{32,24},{40,48},{48,40},{56,64},{64,... | collective-permute-start | bytes 98312 | tf_op jit(solution)/shard_map/ppermute | solution.py:115
  121.0 3.6 %all-gather.6 = bf16[128,256]{1,0:T(8,128)(2,1)S(1)} all-gather(bf16[64,256]{1,0:T(8,128)(2,1)S(1)} %get-tuple-element.55), channel_id=8, replica_groups={{0,8},{16,24},{32,40},{48,56},{64,72},{80,88},{96,104},{112,120},{128,1..., dimensions={0}, use_global_device_ids=true | all-gather | bytes 98304 | tf_op jit(solution)/shard_map/all_gather | solution.py:116
  125.2 4.6 %collective-permute-start.8 = (bf16[64,256]{1,0:T(8,128)(2,1)S(1)}, bf16[64,256]{1,0:T(8,128)(2,1)S(1)}, u32[]{:S(2)}, u32[]{:S(2)}) collective-permute-start(bf16[64,256]{1,0:T(8,128)(2,1)S(1)} %get-tuple-element.54), channel_id=1, source_target_pairs={{0,504},{8,16},{16,8},{24,32},{32,24},{40,48},{48,40},{56,64},{64,... | collective-permute-start | bytes 98312 | tf_op jit(solution)/shard_map/ppermute | solution.py:115
  129.9 3.7 %all-gather.7 = bf16[128,256]{1,0:T(8,128)(2,1)S(1)} all-gather(bf16[64,256]{1,0:T(8,128)(2,1)S(1)} %get-tuple-element.53), channel_id=9, replica_groups={{0,8},{16,24},{32,40},{48,56},{64,72},{80,88},{96,104},{112,120},{128,1..., dimensions={0}, use_global_device_ids=true | all-gather | bytes 98304 | tf_op jit(solution)/shard_map/all_gather | solution.py:116
  134.3 4.2 %collective-permute-start.9 = (bf16[64,256]{1,0:T(8,128)(2,1)S(1)}, bf16[64,256]{1,0:T(8,128)(2,1)S(1)}, u32[]{:S(2)}, u32[]{:S(2)}) collective-permute-start(bf16[64,256]{1,0:T(8,128)(2,1)S(1)} %get-tuple-element.52), channel_id=1, source_target_pairs={{0,504},{8,16},{16,8},{24,32},{32,24},{40,48},{48,40},{56,64},{64,... | collective-permute-start | bytes 98312 | tf_op jit(solution)/shard_map/ppermute | solution.py:115
  138.8 3.4 %all-gather.8 = bf16[128,256]{1,0:T(8,128)(2,1)S(1)} all-gather(bf16[64,256]{1,0:T(8,128)(2,1)S(1)} %get-tuple-element.51), channel_id=10, replica_groups={{0,8},{16,24},{32,40},{48,56},{64,72},{80,88},{96,104},{112,120},{128,1..., dimensions={0}, use_global_device_ids=true | all-gather | bytes 98304 | tf_op jit(solution)/shard_map/all_gather | solution.py:116
  142.7 4.4 %collective-permute-start.10 = (bf16[64,256]{1,0:T(8,128)(2,1)S(1)}, bf16[64,256]{1,0:T(8,128)(2,1)S(1)}, u32[]{:S(2)}, u32[]{:S(2)}) collective-permute-start(bf16[64,256]{1,0:T(8,128)(2,1)S(1)} %get-tuple-element.50), channel_id=1, source_target_pairs={{0,504},{8,16},{16,8},{24,32},{32,24},{40,48},{48,40},{56,64},{64,... | collective-permute-start | bytes 98312 | tf_op jit(solution)/shard_map/ppermute | solution.py:115
  147.1 3.4 %all-gather.9 = bf16[128,256]{1,0:T(8,128)(2,1)S(1)} all-gather(bf16[64,256]{1,0:T(8,128)(2,1)S(1)} %get-tuple-element.49), channel_id=11, replica_groups={{0,8},{16,24},{32,40},{48,56},{64,72},{80,88},{96,104},{112,120},{128,1..., dimensions={0}, use_global_device_ids=true | all-gather | bytes 98304 | tf_op jit(solution)/shard_map/all_gather | solution.py:116
  151.3 4.4 %collective-permute-start.11 = (bf16[64,256]{1,0:T(8,128)(2,1)S(1)}, bf16[64,256]{1,0:T(8,128)(2,1)S(1)}, u32[]{:S(2)}, u32[]{:S(2)}) collective-permute-start(bf16[64,256]{1,0:T(8,128)(2,1)S(1)} %get-tuple-element.48), channel_id=1, source_target_pairs={{0,504},{8,16},{16,8},{24,32},{32,24},{40,48},{48,40},{56,64},{64,... | collective-permute-start | bytes 98312 | tf_op jit(solution)/shard_map/ppermute | solution.py:115
  155.8 3.4 %all-gather.10 = bf16[128,256]{1,0:T(8,128)(2,1)S(1)} all-gather(bf16[64,256]{1,0:T(8,128)(2,1)S(1)} %get-tuple-element.47), channel_id=12, replica_groups={{0,8},{16,24},{32,40},{48,56},{64,72},{80,88},{96,104},{112,120},{128,1..., dimensions={0}, use_global_device_ids=true | all-gather | bytes 98304 | tf_op jit(solution)/shard_map/all_gather | solution.py:116
  160.9 4.5 %collective-permute-start.12 = (bf16[64,256]{1,0:T(8,128)(2,1)}, bf16[64,256]{1,0:T(8,128)(2,1)}, u32[]{:S(2)}, u32[]{:S(2)}) collective-permute-start(bf16[64,256]{1,0:T(8,128)(2,1)} %get-tuple-element.46), channel_id=1, source_target_pairs={{0,504},{8,16},{16,8},{24,32},{32,24},{40,48},{48,40},{56,64},{64,... | collective-permute-start | bytes 98312 | tf_op jit(solution)/shard_map/ppermute | solution.py:115
  166.1 1.4 stack_reshape.31
  168.1 1.4 stack_reshape.30
  169.5 0.8 copy.209
  170.9 0.8 copy.211
  172.4 0.8 copy.213
  173.8 0.8 copy.215
  175.2 3.6 %all-gather.11 = bf16[128,256]{1,0:T(8,128)(2,1)S(1)} all-gather(bf16[64,256]{1,0:T(8,128)(2,1)} %get-tuple-element.45), channel_id=13, replica_groups={{0,8},{16,24},{32,40},{48,56},{64,72},{80,88},{96,104},{112,120},{128,1..., dimensions={0}, use_global_device_ids=true | all-gather | bytes 98304 | tf_op jit(solution)/shard_map/all_gather | solution.py:116
  178.9 0.8 fusion.60
  179.7 1.2 fusion.182
  180.8 1.5 fusion.15
  182.3 4.2 %collective-permute-start.13 = (bf16[64,256]{1,0:T(8,128)(2,1)S(1)}, bf16[64,256]{1,0:T(8,128)(2,1)S(1)}, u32[]{:S(2)}, u32[]{:S(2)}) collective-permute-start(bf16[64,256]{1,0:T(8,128)(2,1)S(1)} %get-tuple-element.44), channel_id=1, source_target_pairs={{0,504},{8,16},{16,8},{24,32},{32,24},{40,48},{48,40},{56,64},{64,... | collective-permute-start | bytes 98312 | tf_op jit(solution)/shard_map/ppermute | solution.py:115
  186.8 3.4 %all-gather.12 = bf16[128,256]{1,0:T(8,128)(2,1)S(1)} all-gather(bf16[64,256]{1,0:T(8,128)(2,1)S(1)} %get-tuple-element.43), channel_id=14, replica_groups={{0,8},{16,24},{32,40},{48,56},{64,72},{80,88},{96,104},{112,120},{128,1..., dimensions={0}, use_global_device_ids=true | all-gather | bytes 98304 | tf_op jit(solution)/shard_map/all_gather | solution.py:116
  190.6 0.8 constant_dynamic-update-slice_fusion.16
  195.1 29.6 %all_to_all.36 = bf16[8,2,8192]{2,1,0:T(2,128)(2,1)S(1)} all-to-all(bf16[8,2,8192]{2,1,0:T(2,128)(2,1)S(1)} %reshape.284), channel_id=1, replica_groups=mesh['sn'=64,'rhs'=8] {'rhs'}, dimensions={0} | all-to-all | bytes 524288 | tf_op jit(solution)/shard_map/all_to_all | solution.py:121
  225.4 1.0 all_to_all.33
  (175 shorter events, 25.5 us)
Async XLA Ops:
  0.0 14.6 %copy-start = (bf16[8,2,128,128]{3,2,1,0:T(8,128)(2,1)S(1)}, bf16[8,2,128,128]{3,2,1,0:T(8,128)(2,1)}, u32[]{:S(2)}) copy-start(bf16[8,2,128,128]{3,2,1,0:T(8,128)(2,1)} %d_ref.1) | copy-start | bytes 1572868
  3.6 29.2 %all-to-all-start = ((bf16[8,2,8192]{2,1,0:T(2,128)(2,1)}), bf16[8,2,8192]{2,1,0:T(2,128)(2,1)S(1)}, u32[]{:S(2)}, u32[]{:S(2)}) async-start(bf16[8,2,8192]{2,1,0:T(2,128)(2,1)} %reshape.282), calls=%async_computation | async-start | bytes 524288 | tf_op jit(solution)/shard_map/all_to_all | solution.py:69
  21.6 0.8 copy-start.1
  22.4 0.8 copy-start.2
  23.2 0.7 copy-start.4
  23.9 0.8 copy-start.6
  24.7 0.8 copy-start.8
  25.5 0.7 copy-start.10
  26.2 0.8 copy-start.12
  27.0 1.0 copy-start.14
  28.0 0.9 copy-start.16
  28.9 1.4 copy-start.18
  30.3 1.3 copy-start.20
  31.6 1.2 copy-start.22
  38.9 26.4 %copy-start.26 = (bf16[2,128,64]{1,2,0:T(8,128)(2,1)}, bf16[2,128,64]{1,2,0:T(8,128)(2,1)S(1)}, u32[]{:S(2)}) copy-start(bf16[2,128,64]{1,2,0:T(8,128)(2,1)S(1)} %convolution_convert_fusion.8) | copy-start | bytes 98308
  39.6 19.9 %collective-permute-start = (bf16[64,256]{1,0:T(8,128)(2,1)}, bf16[64,256]{1,0:T(8,128)(2,1)}, u32[]{:S(2)}, u32[]{:S(2)}) collective-permute-start(bf16[64,256]{1,0:T(8,128)(2,1)} %copy_bitcast_fusion.4), channel_id=1, source_target_pairs={{0,504},{8,16},{16,8},{24,32},{32,24},{40,48},{48,40},{56,64},{64,... | collective-permute-start | bytes 98312 | tf_op jit(solution)/shard_map/ppermute | solution.py:96
  60.3 9.3 %copy-start.3 = (bf16[256,768]{1,0:T(8,128)(2,1)S(1)}, bf16[256,768]{1,0:T(8,128)(2,1)}, u32[]{:S(2)}) copy-start(bf16[256,768]{1,0:T(8,128)(2,1)} %copy-done.2) | copy-start | bytes 1179652
  61.6 8.0 %collective-permute-start.1 = (bf16[64,256]{1,0:T(8,128)(2,1)S(1)}, bf16[64,256]{1,0:T(8,128)(2,1)S(1)}, u32[]{:S(2)}, u32[]{:S(2)}) collective-permute-start(bf16[64,256]{1,0:T(8,128)(2,1)S(1)} %fusion.18), channel_id=1, source_target_pairs={{0,504},{8,16},{16,8},{24,32},{32,24},{40,48},{48,40},{56,64},{64,... | collective-permute-start | bytes 98312 | tf_op jit(solution)/shard_map/ppermute | solution.py:96
  63.6 12.5 %copy-start.19 = (bf16[1536,768]{1,0:T(8,128)(2,1)S(1)}, bf16[1536,768]{1,0:T(8,128)(2,1)}, u32[]{:S(2)}) copy-start(bf16[1536,768]{1,0:T(8,128)(2,1)} %copy-done.18) | copy-start | bytes 7077892
  65.3 15.4 %copy-start.21 = (bf16[1280,768]{1,0:T(8,128)(2,1)S(1)}, bf16[1280,768]{1,0:T(8,128)(2,1)}, u32[]{:S(2)}) copy-start(bf16[1280,768]{1,0:T(8,128)(2,1)} %copy-done.20) | copy-start | bytes 5898244
  69.9 10.8 %collective-permute-start.2 = (bf16[64,256]{1,0:T(8,128)(2,1)S(1)}, bf16[64,256]{1,0:T(8,128)(2,1)S(1)}, u32[]{:S(2)}, u32[]{:S(2)}) collective-permute-start(bf16[64,256]{1,0:T(8,128)(2,1)S(1)} %fusion.19), channel_id=1, source_target_pairs={{0,504},{8,16},{16,8},{24,32},{32,24},{40,48},{48,40},{56,64},{64,... | collective-permute-start | bytes 98312 | tf_op jit(solution)/shard_map/ppermute | solution.py:96
  76.0 5.3 %copy-start.31 = (bf16[64,1,256]{2,0,1:T(8,128)(2,1)S(1)}, bf16[64,1,256]{2,0,1:T(8,128)(2,1)}, u32[]{:S(2)}) copy-start(bf16[64,1,256]{2,0,1:T(8,128)(2,1)} %copy.235) | copy-start | bytes 98308
  76.7 4.7 %copy-start.5 = (bf16[256,768]{1,0:T(8,128)(2,1)S(1)}, bf16[256,768]{1,0:T(8,128)(2,1)}, u32[]{:S(2)}) copy-start(bf16[256,768]{1,0:T(8,128)(2,1)} %copy-done.4) | copy-start | bytes 1179652
  76.8 13.0 %copy-start.7 = (bf16[256,768]{1,0:T(8,128)(2,1)S(1)}, bf16[256,768]{1,0:T(8,128)(2,1)}, u32[]{:S(2)}) copy-start(bf16[256,768]{1,0:T(8,128)(2,1)} %copy-done.6) | copy-start | bytes 1179652
  80.7 13.9 %copy-start.23 = (bf16[1024,768]{1,0:T(8,128)(2,1)S(1)}, bf16[1024,768]{1,0:T(8,128)(2,1)}, u32[]{:S(2)}) copy-start(bf16[1024,768]{1,0:T(8,128)(2,1)} %copy-done.22) | copy-start | bytes 4718596
  81.3 17.4 %copy-start.15 = (bf16[768,768]{1,0:T(8,128)(2,1)S(1)}, bf16[768,768]{1,0:T(8,128)(2,1)}, u32[]{:S(2)}) copy-start(bf16[768,768]{1,0:T(8,128)(2,1)} %copy-done.14) | copy-start | bytes 3538948
  81.8 8.0 %collective-permute-start.3 = (bf16[64,256]{1,0:T(8,128)(2,1)S(1)}, bf16[64,256]{1,0:T(8,128)(2,1)S(1)}, u32[]{:S(2)}, u32[]{:S(2)}) collective-permute-start(bf16[64,256]{1,0:T(8,128)(2,1)S(1)} %fusion.20), channel_id=1, source_target_pairs={{0,504},{8,16},{16,8},{24,32},{32,24},{40,48},{48,40},{56,64},{64,... | collective-permute-start | bytes 98312 | tf_op jit(solution)/shard_map/ppermute | solution.py:96
  85.2 13.8 %copy-start.32 = (bf16[64,1,256]{2,0,1:T(8,128)(2,1)S(1)}, bf16[64,1,256]{2,0,1:T(8,128)(2,1)}, u32[]{:S(2)}) copy-start(bf16[64,1,256]{2,0,1:T(8,128)(2,1)} %copy.238) | copy-start | bytes 98308
  85.2 13.8 %copy-start.33 = (bf16[64,1,256]{2,0,1:T(8,128)(2,1)S(1)}, bf16[64,1,256]{2,0,1:T(8,128)(2,1)}, u32[]{:S(2)}) copy-start(bf16[64,1,256]{2,0,1:T(8,128)(2,1)} %copy.237) | copy-start | bytes 98308
  90.0 9.2 %copy-start.9 = (bf16[256,768]{1,0:T(8,128)(2,1)S(1)}, bf16[256,768]{1,0:T(8,128)(2,1)}, u32[]{:S(2)}) copy-start(bf16[256,768]{1,0:T(8,128)(2,1)} %copy-done.8) | copy-start | bytes 1179652
  90.0 8.6 %collective-permute-start.4 = (bf16[64,256]{1,0:T(8,128)(2,1)S(1)}, bf16[64,256]{1,0:T(8,128)(2,1)S(1)}, u32[]{:S(2)}, u32[]{:S(2)}) collective-permute-start(bf16[64,256]{1,0:T(8,128)(2,1)S(1)} %fusion.21), channel_id=1, source_target_pairs={{0,504},{8,16},{16,8},{24,32},{32,24},{40,48},{48,40},{56,64},{64,... | collective-permute-start | bytes 98312 | tf_op jit(solution)/shard_map/ppermute | solution.py:96
  95.1 12.5 %copy-start.11 = (bf16[256,768]{1,0:T(8,128)(2,1)S(1)}, bf16[256,768]{1,0:T(8,128)(2,1)}, u32[]{:S(2)}) copy-start(bf16[256,768]{1,0:T(8,128)(2,1)} %copy-done.10) | copy-start | bytes 1179652
  95.1 17.0 %copy-start.17 = (bf16[512,768]{1,0:T(8,128)(2,1)S(1)}, bf16[512,768]{1,0:T(8,128)(2,1)}, u32[]{:S(2)}) copy-start(bf16[512,768]{1,0:T(8,128)(2,1)} %copy-done.16) | copy-start | bytes 2359300
  95.1 17.0 %copy-start.35 = (bf16[64,1,256]{2,0,1:T(8,128)(2,1)S(1)}, bf16[64,1,256]{2,0,1:T(8,128)(2,1)}, u32[]{:S(2)}) copy-start(bf16[64,1,256]{2,0,1:T(8,128)(2,1)} %copy.239) | copy-start | bytes 98308
  99.1 16.9 %copy-start.13 = (bf16[256,768]{1,0:T(8,128)(2,1)S(1)}, bf16[256,768]{1,0:T(8,128)(2,1)}, u32[]{:S(2)}) copy-start(bf16[256,768]{1,0:T(8,128)(2,1)} %copy-done.12) | copy-start | bytes 1179652
  99.6 8.0 %collective-permute-start.5 = (bf16[64,256]{1,0:T(8,128)(2,1)S(1)}, bf16[64,256]{1,0:T(8,128)(2,1)S(1)}, u32[]{:S(2)}, u32[]{:S(2)}) collective-permute-start(bf16[64,256]{1,0:T(8,128)(2,1)S(1)} %fusion.22), channel_id=1, source_target_pairs={{0,504},{8,16},{16,8},{24,32},{32,24},{40,48},{48,40},{56,64},{64,... | collective-permute-start | bytes 98312 | tf_op jit(solution)/shard_map/ppermute | solution.py:96
  107.8 8.1 %collective-permute-start.6 = (bf16[64,256]{1,0:T(8,128)(2,1)S(1)}, bf16[64,256]{1,0:T(8,128)(2,1)S(1)}, u32[]{:S(2)}, u32[]{:S(2)}) collective-permute-start(bf16[64,256]{1,0:T(8,128)(2,1)S(1)} %fusion.23), channel_id=1, source_target_pairs={{0,504},{8,16},{16,8},{24,32},{32,24},{40,48},{48,40},{56,64},{64,... | collective-permute-start | bytes 98312 | tf_op jit(solution)/shard_map/ppermute | solution.py:96
  116.6 8.0 %collective-permute-start.7 = (bf16[64,256]{1,0:T(8,128)(2,1)S(1)}, bf16[64,256]{1,0:T(8,128)(2,1)S(1)}, u32[]{:S(2)}, u32[]{:S(2)}) collective-permute-start(bf16[64,256]{1,0:T(8,128)(2,1)S(1)} %get-tuple-element.56), channel_id=1, source_target_pairs={{0,504},{8,16},{16,8},{24,32},{32,24},{40,48},{48,40},{56,64},{64,... | collective-permute-start | bytes 98312 | tf_op jit(solution)/shard_map/ppermute | solution.py:115
  125.2 8.4 %collective-permute-start.8 = (bf16[64,256]{1,0:T(8,128)(2,1)S(1)}, bf16[64,256]{1,0:T(8,128)(2,1)S(1)}, u32[]{:S(2)}, u32[]{:S(2)}) collective-permute-start(bf16[64,256]{1,0:T(8,128)(2,1)S(1)} %get-tuple-element.54), channel_id=1, source_target_pairs={{0,504},{8,16},{16,8},{24,32},{32,24},{40,48},{48,40},{56,64},{64,... | collective-permute-start | bytes 98312 | tf_op jit(solution)/shard_map/ppermute | solution.py:115
  134.0 26.3 %copy-start.24 = (bf16[2,64,128]{2,1,0:T(8,128)(2,1)}, bf16[2,64,128]{2,1,0:T(8,128)(2,1)S(1)}, u32[]{:S(2)}) copy-start(bf16[2,64,128]{2,1,0:T(8,128)(2,1)S(1)} %convolution_convert_fusion.5) | copy-start | bytes 98308
  134.3 8.0 %collective-permute-start.9 = (bf16[64,256]{1,0:T(8,128)(2,1)S(1)}, bf16[64,256]{1,0:T(8,128)(2,1)S(1)}, u32[]{:S(2)}, u32[]{:S(2)}) collective-permute-start(bf16[64,256]{1,0:T(8,128)(2,1)S(1)} %get-tuple-element.52), channel_id=1, source_target_pairs={{0,504},{8,16},{16,8},{24,32},{32,24},{40,48},{48,40},{56,64},{64,... | collective-permute-start | bytes 98312 | tf_op jit(solution)/shard_map/ppermute | solution.py:115
  142.4 17.1 %copy-start.25 = (bf16[2,64,128]{2,1,0:T(8,128)(2,1)}, bf16[2,64,128]{2,1,0:T(8,128)(2,1)S(1)}, u32[]{:S(2)}) copy-start(bf16[2,64,128]{2,1,0:T(8,128)(2,1)S(1)} %convolution_convert_fusion.4) | copy-start | bytes 98308
  142.7 8.0 %collective-permute-start.10 = (bf16[64,256]{1,0:T(8,128)(2,1)S(1)}, bf16[64,256]{1,0:T(8,128)(2,1)S(1)}, u32[]{:S(2)}, u32[]{:S(2)}) collective-permute-start(bf16[64,256]{1,0:T(8,128)(2,1)S(1)} %get-tuple-element.50), channel_id=1, source_target_pairs={{0,504},{8,16},{16,8},{24,32},{32,24},{40,48},{48,40},{56,64},{64,... | collective-permute-start | bytes 98312 | tf_op jit(solution)/shard_map/ppermute | solution.py:115
  151.3 8.0 %collective-permute-start.11 = (bf16[64,256]{1,0:T(8,128)(2,1)S(1)}, bf16[64,256]{1,0:T(8,128)(2,1)S(1)}, u32[]{:S(2)}, u32[]{:S(2)}) collective-permute-start(bf16[64,256]{1,0:T(8,128)(2,1)S(1)} %get-tuple-element.48), channel_id=1, source_target_pairs={{0,504},{8,16},{16,8},{24,32},{32,24},{40,48},{48,40},{56,64},{64,... | collective-permute-start | bytes 98312 | tf_op jit(solution)/shard_map/ppermute | solution.py:115
  155.8 4.4 %copy-start.28 = (bf16[2,64,128]{2,1,0:T(8,128)(2,1)}, bf16[2,64,128]{2,1,0:T(8,128)(2,1)S(1)}, u32[]{:S(2)}) copy-start(bf16[2,64,128]{2,1,0:T(8,128)(2,1)S(1)} %convolution_convert_fusion.3) | copy-start | bytes 98308
  159.4 1.5 copy-start.29
  159.6 1.4 copy-start.30
  160.9 17.9 %collective-permute-start.12 = (bf16[64,256]{1,0:T(8,128)(2,1)}, bf16[64,256]{1,0:T(8,128)(2,1)}, u32[]{:S(2)}, u32[]{:S(2)}) collective-permute-start(bf16[64,256]{1,0:T(8,128)(2,1)} %get-tuple-element.46), channel_id=1, source_target_pairs={{0,504},{8,16},{16,8},{24,32},{32,24},{40,48},{48,40},{56,64},{64,... | collective-permute-start | bytes 98312 | tf_op jit(solution)/shard_map/ppermute | solution.py:115
  179.6 10.7 %copy-start.27 = (bf16[2,128,64]{1,2,0:T(8,128)(2,1)S(1)}, bf16[2,128,64]{1,2,0:T(8,128)(2,1)}, u32[]{:S(2)}) copy-start(bf16[2,128,64]{1,2,0:T(8,128)(2,1)} %copy-done.26) | copy-start | bytes 98308
  180.8 13.5 %copy-start.34 = (bf16[64,1,256]{2,0,1:T(8,128)(2,1)S(1)}, bf16[64,1,256]{2,0,1:T(8,128)(2,1)}, u32[]{:S(2)}) copy-start(bf16[64,1,256]{2,0,1:T(8,128)(2,1)} %stack_reshape.31) | copy-start | bytes 98308
  182.3 8.0 %collective-permute-start.13 = (bf16[64,256]{1,0:T(8,128)(2,1)S(1)}, bf16[64,256]{1,0:T(8,128)(2,1)S(1)}, u32[]{:S(2)}, u32[]{:S(2)}) collective-permute-start(bf16[64,256]{1,0:T(8,128)(2,1)S(1)} %get-tuple-element.44), channel_id=1, source_target_pairs={{0,504},{8,16},{16,8},{24,32},{32,24},{40,48},{48,40},{56,64},{64,... | collective-permute-start | bytes 98312 | tf_op jit(solution)/shard_map/ppermute | solution.py:115

commit v2 on v1

v2 whole, which is shorter than its diff:
```python
import jax
import jax.numpy as jnp
from jax import lax
from jax.experimental import pallas as pl
from jax.experimental.pallas import tpu as pltpu
from jax.sharding import PartitionSpec as P

BF = jnp.bfloat16
F32 = jnp.float32
VMEM = pl.BlockSpec(memory_space=pltpu.VMEM)
SMEM = pl.BlockSpec(memory_space=pltpu.SMEM)


def dot_t(a, w):
    return lax.dot_general(a, w, (((1,), (1,)), ((), ())), preferred_element_type=F32)


def dot_n(a, w):
    return lax.dot_general(a, w, (((1,), (0,)), ((), ())), preferred_element_type=F32)


def call(body, outs, args, scratch=(), flops=10**8, mib=16):
    specs = [SMEM if a.dtype == jnp.int32 else VMEM for a in args]
    size = sum(a.size * a.dtype.itemsize for a in args)
    return pl.pallas_call(
        body,
        out_shape=[jax.ShapeDtypeStruct(s, d) for s, d in outs],
        in_specs=specs,
        out_specs=[VMEM] * len(outs),
        scratch_shapes=list(scratch),
        compiler_params=pltpu.CompilerParams(vmem_limit_bytes=mib * 2**20),
        cost_estimate=pl.CostEstimate(flops=flops, bytes_accessed=size, transcendentals=0),
    )(*args)


def build_operators(tiles, diag, row_slot, col_slot):
    levels, owned, b, _ = diag.shape
    count = tiles.shape[1]
    wide = 3 * owned * b
    tall = owned * b
    slots = [(0, 0), (1, 0), (2, 0), (3, 0), (2, 1), (3, 1), (2, 2)]

    def body(row_ref, col_ref, t_ref, d_ref, *outs):
        s_refs, b_refs = outs[: levels - 1], outs[levels - 1 :]
        for l in range(levels - 1):
            s_refs[l][...] = jnp.zeros_like(s_refs[l])

            def add(t, carry):
                r = pl.multiple_of(row_ref[l, t] * b, b)
                c = pl.multiple_of(col_ref[l, t] * b, b)
                at = (pl.ds(r, b), pl.ds(c, b))
                s_refs[l][at] = s_refs[l][at] + t_ref[l, t]
                return carry

            lax.fori_loop(0, count, add, 0, unroll=8)
            which, index = slots[l]
            for q in range(owned):
                rows = slice(q * b, (q + 1) * b)
                b_refs[which][index, rows, :] = dot_n(d_ref[l + 1, q], s_refs[l][rows, :]).astype(BF)

    outs = [(((levels - 1 - l) * tall, wide), BF) for l in range(levels - 1)]
    outs += [((k, tall, wide), BF) for k in (1, 1, 3, 2)]
    res = call(body, outs, (row_slot, col_slot, tiles, diag), flops=4 * 10**8, mib=32)
    return res[: levels - 1], res[levels - 1 :], slots


def on_device(lanczos_block, diag_inv, factor_tiles, tile_rows, tile_cols):
    levels, owned, b = diag_inv.shape[:3]
    group_tiles = factor_tiles.shape[1]
    n = lax.axis_size("sn")
    own = lax.axis_index("sn")
    per_level = owned * n
    w = owned * b
    parity = (own % 2).astype(jnp.int32).reshape(1)

    panels = lax.all_to_all(lanczos_block.astype(BF), "rhs", split_axis=0, concat_axis=2, tiled=True)
    cols = panels.shape[0]
    panels = panels.reshape(cols, levels * w)

    my_rows = lax.dynamic_slice_in_dim(tile_rows, own * group_tiles, group_tiles, 1)
    my_cols = lax.dynamic_slice_in_dim(tile_cols, own * group_tiles, group_tiles, 1)
    above = jnp.arange(1, levels, dtype=jnp.int32)[:, None]
    group = (jnp.arange(group_tiles, dtype=jnp.int32) // (group_tiles // 3))[None, :]
    row_slot = (my_rows // per_level - above) * owned + my_rows % owned
    col_slot = group * owned + my_cols % owned
    S, B, slots = build_operators(factor_tiles, diag_inv, row_slot, col_slot)

    pairs = [
        [[i, i + 1] for i in range(0, n, 2)],
        [[i, (i + 1) % n] for i in range(1, n, 2)],
    ]
    swaps = [[(p, q) for p, q in g] + [(q, p) for p, q in g] for g in pairs]
    B_far = [lax.ppermute(B[k], "sn", swaps[1 - k % 2]) for k in range(4)]

    def own_op(l):
        which, index = slots[l - 1]
        return B[which], index

    def far_op(l):
        which, index = slots[l - 1]
        return B_far[which], index

    def swap(l, message):
        return lax.all_gather(message, "sn", axis_index_groups=pairs[l % 2])

    def diag_fwd(d_ref, l, f):
        f = f.astype(BF)
        return jnp.concatenate(
            [dot_t(f[:, q * b : (q + 1) * b], d_ref[l, q]) for q in range(owned)], axis=1
        )

    def diag_bwd(d_ref, l, e):
        return jnp.concatenate(
            [dot_n(e[:, q * b : (q + 1) * b], d_ref[l, q]) for q in range(owned)], axis=1
        ).astype(BF)

    def side_of(par_ref, l):
        return par_ref[0] if l % 2 == 0 else 1 - par_ref[0]

    def at(start, size):
        return pl.ds(pl.multiple_of(start, w), size)

    def forward_step(l, message, acc):
        got = swap(l, message)
        b_own, i_own = own_op(l)
        b_par, i_par = far_op(l)
        more, rest_levels = l + 1 < levels, levels - l - 2
        base = 2 * w if l == 1 else 0

        def step(par_ref, g_ref, bo_ref, bp_ref, *rest):
            y4 = rest[-1]
            s = side_of(par_ref, l)
            y4[:, : 2 * w] = g_ref[0, :, : 2 * w]
            y4[:, 2 * w :] = g_ref[1, :, : 2 * w]
            mine = y4[:, at(s * w, 3 * w)]
            theirs = y4[:, at((1 - s) * w, 3 * w)]
            h_own = g_ref[s, :, 2 * w :].astype(F32)
            h_par = g_ref[1 - s, :, 2 * w :].astype(F32)
            m_ref = rest[3] if more else rest[0]
            m_ref[:, at(s * w, w)] = (h_own - dot_t(mine, bo_ref[i_own])).astype(BF)
            m_ref[:, at((1 - s) * w, w)] = (h_par - dot_t(theirs, bp_ref[i_par])).astype(BF)
            if more:
                s_ref, d_ref, acc_ref = rest[:3]
                f = acc_ref[:, base : base + w].astype(F32) - dot_t(mine, s_ref[w : 2 * w, :])
                m_ref[:, 2 * w :] = diag_fwd(d_ref, l + 1, f).astype(BF)
                if rest_levels:
                    rest[4][...] = acc_ref[:, base + w :].astype(F32) - dot_t(mine, s_ref[2 * w :, :])

        args, outs = (parity, got, b_own, b_par), [((cols, 3 * w if more else 2 * w), BF)]
        if more:
            args += (S[l - 1], diag_inv, acc)
            if rest_levels:
                outs.append(((cols, rest_levels * w), F32))
        res = call(step, outs, args, [pltpu.VMEM((cols, 4 * w), BF)])
        return res[0], res[-1]

    def backward_step(l, got, y_pair, older, above):
        b_own, i_own = own_op(l)
        b_par, i_par = far_op(l)
        top, more = l == levels - 1, l >= 2
        args = (parity, y_pair, b_own, b_par, diag_inv)
        if not top:
            args += (got, older)
        if more:
            args += (S[l - 2], *above)
        n_in = len(args)
        outs = [((cols, 3 * w if more else 2 * w), BF), ((cols, w), BF)]
        if more:
            outs.append(((cols, 3 * w), F32))

        def step(*refs):
            par_ref, y_ref, bo_ref, bp_ref, d_ref = refs[:5]
            m_ref, z_ref = refs[n_in : n_in + 2]
            e_ref = refs[-1]
            s = side_of(par_ref, l)
            e = y_ref[:, : 2 * w]
            if not top:
                g_ref, old_ref = refs[5:7]
                e = e.astype(F32) - g_ref[0, :, : 2 * w].astype(F32) - g_ref[1, :, : 2 * w].astype(F32)
            e_ref[...] = e.astype(BF)
            e_own, e_par = e_ref[:, at(s * w, w)], e_ref[:, at((1 - s) * w, w)]
            z_own = diag_bwd(d_ref, l, e_own)
            z_ref[...] = z_own
            part = dot_n(e_own, bo_ref[i_own, :, at(s * w, 2 * w)])
            extra = dot_n(e_par, bp_ref[i_par, :, at(s * 2 * w, w)])
            if not top:
                part = part + old_ref[:, at(s * w, 2 * w)]
                extra = extra + g_ref[1 - s, :, 2 * w :].astype(F32)
            for k in range(2):
                piece = part[:, k * w : (k + 1) * w]
                m_ref[:, k * w : (k + 1) * w] = jnp.where(s == 1 - k, piece + extra, piece).astype(BF)
            if more:
                s_ref, old_out = refs[n_in - 1 - len(above)], refs[n_in + 2]
                total = dot_n(z_own, s_ref[w : 2 * w, :])
                for k, zr in enumerate(refs[n_in - len(above) : n_in]):
                    total = total + dot_n(zr[...], s_ref[(k + 2) * w : (k + 3) * w, :])
                old_out[...] = total
                m_ref[:, 2 * w :] = old_out[:, at(s * 2 * w, w)].astype(BF)

        res = call(step, outs, args, [pltpu.VMEM((cols, 2 * w), BF)])
        return res[0], res[1], res[2] if more else None

    def start(x_ref, d_ref, y_ref, h_ref):
        y_ref[...] = diag_fwd(d_ref, 0, x_ref[:, :w]).astype(BF)
        h_ref[...] = diag_fwd(d_ref, 1, x_ref[:, w : 2 * w]).astype(BF)

    y0, h1 = call(start, [((cols, w), BF)] * 2, (panels, diag_inv))
    both = swap(0, y0)
    message = jnp.concatenate([both[0], both[1], h1], axis=1)

    pair_y = [None] * levels
    acc = panels
    for l in range(1, levels):
        pair_y[l], acc = forward_step(l, message, acc)
        message = pair_y[l]

    z = [None] * levels
    got, older = None, None
    for l in range(levels - 1, 0, -1):
        message, z[l], older = backward_step(l, got, pair_y[l], older, z[l + 1 :])
        got = swap(l - 1, message)

    def finish(par_ref, g_ref, y_ref, d_ref, *rest):
        o_ref = rest[-1]
        here = at(par_ref[0] * w, w)
        terms = g_ref[0, :, here].astype(F32) + g_ref[1, :, here].astype(F32)
        e = (y_ref[...].astype(F32) - terms).astype(BF)
        o_ref[:, :w] = diag_bwd(d_ref, 0, e)
        for k in range(1, levels):
            o_ref[:, k * w : (k + 1) * w] = rest[k - 1][...]

    (combined,) = call(finish, [((cols, levels * w), BF)], (parity, got, y0, diag_inv, *z[1:]))
    combined = combined.reshape(cols, levels, w)
    return lax.all_to_all(combined, "rhs", split_axis=2, concat_axis=0, tiled=True)


def solution(mesh):
    placed = (
        P(None, None, ("sn", "rhs")),
        P(None, "sn", None, None),
        P(None, "sn", None, None),
        P(),
        P(),
    )
    return jax.shard_map(
        on_device,
        mesh=mesh,
        in_specs=placed,
        out_specs=P(None, None, ("sn", "rhs")),
        check_vma=False,
    )
```

time: 229 us -> 208 us (0.908)
  starting transfers between devices: 74.4 us -> 26.9 us
  blocking collectives: 79.5 us -> 127 us
  Pallas kernels: 7.02 us -> 23.5 us
  local copies, waits for them, and re-layouts: 43.4 us -> 28.2 us
  matrix products: 14.9 us -> 0 us
  other arithmetic: 4.46 us -> 0.85 us
    all_gather x14 -> x15, blocking collectives: 49.9 us -> 99.2 us  [swap(): return lax.all_gather(message, 'sn', axis_index_groups=pairs[l % 2])]
    ppermute x14 -> x4, starting transfers between devices: 64.2 us -> 21.4 us  [on_device(): B_far = [lax.ppermute(B[k], 'sn', swaps[1 - k % 2]) for k in range(4)]]
    pallas_call x1 -> x17, Pallas kernels: 7.02 us -> 23.5 us  [call(): pl.pallas_call(body, out_shape=[jax.ShapeDtypeStruct(s, d) for s, d in ou...]
    dot_general x42 -> x0, matrix products: 14.9 us -> none  [the longest x13 7.13 us: dot_t(): lax.dot_general(a, w, (((1,), (1,)), ((), ())), preferred_element_type=F32)]
    convert_element_type x11 -> x0, local copies, waits for them, and re-layouts: 5.82 us -> none  [the longest x8 4.51 us: diag_bwd(): return z.astype(BF).reshape(columns, wide)]
    another operation x10 -> x0, local copies, waits for them, and re-layouts: 5.65 us -> none  [on_device(): combined = jnp.stack(z, axis=1)]
    all_to_all x1, starting transfers between devices: 10.2 us -> 5.42 us  [on_device(): lax.all_to_all(lanczos_block.astype(BF), 'rhs', split_axis=0, concat_axis...]
    unnamed x94 -> x49, local copies, waits for them, and re-layouts: 25.3 us -> 20.8 us
  transfers between devices with their start and end apart: 15 -> 5, of which waited for: 5 -> 0; matrix products, arithmetic and copies ran while one was open for 10% -> 5% of each run, Pallas kernels for 3% -> 3%
where the time goes in v2:
time: 208 us; the launch traced here: 207 us
  blocking collectives  127 us (61%)
  local copies, waits for them, and re-layouts  28.2 us (14%)
  starting transfers between devices  26.9 us (13%)
  Pallas kernels  23.5 us (11%)
    all_gather x15, blocking collectives, swap(): return lax.all_gather(message, 'sn', axis_index_groups=pairs[l % 2])  99.2 us
    all_to_all x1, blocking collectives, on_device(): lax.all_to_all(combined, 'rhs', split_axis=2, concat_axis=0, tiled=True)  27.7 us
    pallas_call x17, Pallas kernels, call(): pl.pallas_call(body, out_shape=[jax.ShapeDtypeStruct(s, d) for s, d in ou...  23.5 us
    ppermute x4, starting transfers between devices, on_device(): B_far = [lax.ppermute(B[k], 'sn', swaps[1 - k % 2]) for k in range(4)]  21.4 us
    unnamed x49, local copies, waits for them, and re-layouts  20.8 us
    all_to_all x1, starting transfers between devices, on_device(): lax.all_to_all(lanczos_block.astype(BF), 'rhs', split_axis=0, concat_axis...  5.42 us
  transfers between devices with their start and end apart: 5, of which 0 were waited for; matrix products, arithmetic and copies ran while one was open for 5% of the time, Pallas kernels for 3%

profile of v2, /device:TPU:1, one launch (start us, length us, event | category | flops | bytes accessed | tf_op | source)
XLA Modules:
  0.0 206.5 jit_solution(10087753120560825345)
XLA Ops:
  0.0 0.8 fusion.3
  0.8 0.0 copy-start
  0.8 1.0 copy-done
  1.9 2.6 %copy-done.13 = bf16[7,24,128,128]{3,2,1,0:T(8,128)(2,1)S(1)} copy-done((bf16[7,24,128,128]{3,2,1,0:T(8,128)(2,1)S(1)}, bf16[7,24,128,128]{3,2,1,0:T(8,128)(2,1)}, u32[]{:S(2)}) %copy-start.13) | copy-done | bytes 5505048
  4.4 4.9 %shard_map.56 = (bf16[1792,768]{1,0:T(8,128)(2,1)S(1)}, bf16[1536,768]{1,0:T(8,128)(2,1)S(1)}, bf16[1280,768]{1,0:T(8,128)(2,1)S(1)}, bf16[1024,768]{1,0:T(8,128...) custom-call(s32[7,24]{1,0:T(8,128)S(1)} %get-tuple-element.91.row_re, ...), custom_call_target="tpu_custom_call" | custom-call | flops 400000000 | bytes 6030656 | tf_op jit(solution)/shard_map/pallas_call | solution.py:25
  9.3 0.9 copy-done.2
  10.2 1.5 copy-done.4
  11.7 1.5 copy-done.7
  13.2 1.3 copy-done.9
  14.5 1.2 copy-done.11
  15.7 1.0 copy-done.14
  16.7 0.9 copy-done.16
  17.6 0.7 copy-done.18
  18.4 14.1 %collective-permute-start.2 = (bf16[3,256,768]{2,1,0:T(8,128)(2,1)S(1)}, bf16[3,256,768]{2,1,0:T(8,128)(2,1)S(1)}, u32[]{:S(2)}, u32[]{:S(2)}) collective-permute-start(bf16[3,256,768]{2,1,0:T(8,128)(2,1)S(1)} %get-tuple-element.56.bo_ref.refs_2_), channel_id=1, source_target_pairs={{8,16},{24,32},{40,48},{56,64},{72,80},{88,96},{104,112},{120,128}... | collective-permute-start | bytes 3538952 | tf_op jit(solution)/shard_map/ppermute | solution.py:93
  32.5 1.7 copy.24
  34.2 3.1 %reshape.51 = bf16[8,2,8192]{2,1,0:T(2,128)(2,1)} reshape(bf16[512,8,32]{2,1,0:T(8,128)(2,1)} %copy.24) | data formatting | bytes 524288
  37.3 5.4 %all-to-all-start = ((bf16[8,2,8192]{2,1,0:T(2,128)(2,1)}), bf16[8,2,8192]{2,1,0:T(2,128)(2,1)S(1)}, u32[]{:S(2)}, u32[]{:S(2)}) async-start(bf16[8,2,8192]{2,1,0:T(2,128)(2,1)} %reshape.51), calls=%async_computation | async-start | bytes 524288 | tf_op jit(solution)/shard_map/all_to_all | solution.py:76
  42.8 2.0 collective-permute-start.3
  44.8 3.4 %collective-permute-start = (bf16[1,256,768]{2,1,0:T(8,128)(2,1)}, bf16[1,256,768]{2,1,0:T(8,128)(2,1)}, u32[]{:S(2)}, u32[]{:S(2)}) collective-permute-start(bf16[1,256,768]{2,1,0:T(8,128)(2,1)} %copy-done.18), channel_id=1, source_target_pairs={{8,16},{24,32},{40,48},{56,64},{72,80},{88,96},{104,112},{120,128}... | collective-permute-start | bytes 1179656 | tf_op jit(solution)/shard_map/ppermute | solution.py:93
  48.2 1.9 collective-permute-start.1
  50.1 0.0 all-to-all-done
  50.1 1.5 reshape.52
  51.6 2.7 %copy.25 = bf16[8,64,8,32]{1,3,0,2:T(8,128)(2,1)} copy(bf16[8,64,8,32]{3,2,1,0:T(8,128)(2,1)} %bitcast.45) | data formatting | bytes 524288 | tf_op jit(solution)/shard_map/all_to_all | solution.py:76
  54.3 1.2 copy.26.x_ref.rest_2_
  55.5 0.2 shard_map.55
  55.7 17.7 %all-gather = bf16[128,256]{1,0:T(8,128)(2,1)S(1)} all-gather(bf16[64,256]{1,0:T(8,128)(2,1)S(1)} %get-tuple-element.47.y_ref), channel_id=2, replica_groups={{0,8},{16,24},{32,40},{48,56},{64,72},{80,88},{96,104},{112,120},{128,1..., dimensions={0}, use_global_device_ids=true | all-gather | bytes 98304 | tf_op jit(solution)/shard_map/all_gather | solution.py:104
  73.4 7.5 %all-gather.1 = bf16[128,768]{1,0:T(8,128)(2,1)S(1)} all-gather(bf16[64,768]{1,0:T(8,128)(2,1)S(1)} %pad_maximum_fusion), channel_id=3, replica_groups={{8,16},{24,32},{40,48},{56,64},{72,80},{88,96},{104,112},{120,128},{136..., dimensions={0}, use_global_device_ids=true | all-gather | bytes 294912 | tf_op jit(solution)/shard_map/all_gather | solution.py:104
  80.9 1.8 copy-done.5
  82.6 1.0 copy-done.19
  83.6 2.5 %shard_map.57 = (bf16[64,768]{1,0:T(8,128)(2,1)S(1)}, f32[64,1280]{1,0:T(8,128)S(1)}) custom-call(s32[1]{0:T(128)} %bitcast.par_ref.refs_0_, bf16[2,64,768]{2,1,0:T(8,128)(2,1)S(1)} %bitcast.35, bf16[1,256,768]{2,1,0:T(8,128)(2,1)S(1)} %copy-done.19, bf16[1,256,768]{2,1,0:T(8,128)(2,1)} %collective-permute-done.bp_ref.refs_3_, ...), custom_call_target="tpu_custom_call" | custom-call | flops 100000000 | bytes 4521988 | tf_op jit(solution)/shard_map/pallas_call | solution.py:25
  86.1 4.1 %all-gather.2 = bf16[128,768]{1,0:T(8,128)(2,1)S(1)} all-gather(bf16[64,768]{1,0:T(8,128)(2,1)S(1)} %get-tuple-element.51.refs_1_), channel_id=4, replica_groups={{0,8},{16,24},{32,40},{48,56},{64,72},{80,88},{96,104},{112,120},{128,1..., dimensions={0}, use_global_device_ids=true | all-gather | bytes 294912 | tf_op jit(solution)/shard_map/all_gather | solution.py:104
  90.3 2.2 %shard_map.58 = (bf16[64,768]{1,0:T(8,128)(2,1)S(1)}, f32[64,1024]{1,0:T(8,128)S(1)}) custom-call(s32[1]{0:T(128)} %bitcast.par_ref.refs_0_, bf16[2,64,768]{2,1,0:T(8,128)(2,1)S(1)} %bitcast.36, bf16[1,256,768]{2,1,0:T(8,128)(2,1)S(1)} %get-tuple-element.52.bo_ref.refs_2_, bf16[1,256,768]{2,1,0:T(8,128)(2,1)} %collective-permute-done.1.bp_ref.refs_3_, ...), custom_call_target="tpu_custom_call" | custom-call | flops 100000000 | bytes 4194308 | tf_op jit(solution)/shard_map/pallas_call | solution.py:25
  92.5 7.5 %all-gather.3 = bf16[128,768]{1,0:T(8,128)(2,1)S(1)} all-gather(bf16[64,768]{1,0:T(8,128)(2,1)S(1)} %get-tuple-element.55.refs_1_), channel_id=5, replica_groups={{8,16},{24,32},{40,48},{56,64},{72,80},{88,96},{104,112},{120,128},{136..., dimensions={0}, use_global_device_ids=true | all-gather | bytes 294912 | tf_op jit(solution)/shard_map/all_gather | solution.py:104
  100.0 1.1 shard_map.59
  101.1 4.1 %all-gather.4 = bf16[128,768]{1,0:T(8,128)(2,1)S(1)} all-gather(bf16[64,768]{1,0:T(8,128)(2,1)S(1)} %get-tuple-element.59.refs_1_), channel_id=6, replica_groups={{0,8},{16,24},{32,40},{48,56},{64,72},{80,88},{96,104},{112,120},{128,1..., dimensions={0}, use_global_device_ids=true | all-gather | bytes 294912 | tf_op jit(solution)/shard_map/all_gather | solution.py:104
  105.3 2.1 %shard_map.60 = (bf16[64,768]{1,0:T(8,128)(2,1)S(1)}, f32[64,512]{1,0:T(8,128)S(1)}) custom-call(s32[1]{0:T(128)} %bitcast.par_ref.refs_0_, bf16[2,64,768]{2,1,0:T(8,128)(2,1)S(1)} %bitcast.38, bf16[2,256,768]{2,1,0:T(8,128)(2,1)S(1)} %copy-done.3, bf16[2,256,768]{2,1,0:T(8,128)(2,1)} %collective-permute-done.3.bp_ref.refs_3_, ...), custom_call_target="tpu_custom_call" | custom-call | flops 100000000 | bytes 4063236 | tf_op jit(solution)/shard_map/pallas_call | solution.py:25
  107.4 7.5 %all-gather.5 = bf16[128,768]{1,0:T(8,128)(2,1)S(1)} all-gather(bf16[64,768]{1,0:T(8,128)(2,1)S(1)} %get-tuple-element.63.refs_1_), channel_id=7, replica_groups={{8,16},{24,32},{40,48},{56,64},{72,80},{88,96},{104,112},{120,128},{136..., dimensions={0}, use_global_device_ids=true | all-gather | bytes 294912 | tf_op jit(solution)/shard_map/all_gather | solution.py:104
  114.9 0.9 shard_map.61
  115.7 4.4 %all-gather.6 = bf16[128,768]{1,0:T(8,128)(2,1)S(1)} all-gather(bf16[64,768]{1,0:T(8,128)(2,1)S(1)} %get-tuple-element.66.refs_1_), channel_id=8, replica_groups={{0,8},{16,24},{32,40},{48,56},{64,72},{80,88},{96,104},{112,120},{128,1..., dimensions={0}, use_global_device_ids=true | all-gather | bytes 294912 | tf_op jit(solution)/shard_map/all_gather | solution.py:104
  120.2 1.8 shard_map.62.refs_1_
  121.9 7.5 %all-gather.7 = bf16[128,768]{1,0:T(8,128)(2,1)S(1)} all-gather(bf16[64,768]{1,0:T(8,128)(2,1)S(1)} %shard_map.62.refs_1_), channel_id=9, replica_groups={{8,16},{24,32},{40,48},{56,64},{72,80},{88,96},{104,112},{120,128},{136..., dimensions={0}, use_global_device_ids=true | all-gather | bytes 294912 | tf_op jit(solution)/shard_map/all_gather | solution.py:104
  129.4 0.4 shard_map.63.refs_1_
  129.8 0.3 shard_map.64
  130.1 4.1 %all-gather.8 = bf16[128,768]{1,0:T(8,128)(2,1)S(1)} all-gather(bf16[64,768]{1,0:T(8,128)(2,1)S(1)} %get-tuple-element.69), channel_id=10, replica_groups={{0,8},{16,24},{32,40},{48,56},{64,72},{80,88},{96,104},{112,120},{128,1..., dimensions={0}, use_global_device_ids=true | all-gather | bytes 294912 | tf_op jit(solution)/shard_map/all_gather | solution.py:104
  134.3 1.5 shard_map.65
  135.8 7.5 %all-gather.9 = bf16[128,768]{1,0:T(8,128)(2,1)S(1)} all-gather(bf16[64,768]{1,0:T(8,128)(2,1)S(1)} %get-tuple-element.72), channel_id=11, replica_groups={{8,16},{24,32},{40,48},{56,64},{72,80},{88,96},{104,112},{120,128},{136..., dimensions={0}, use_global_device_ids=true | all-gather | bytes 294912 | tf_op jit(solution)/shard_map/all_gather | solution.py:104
  143.2 0.4 shard_map.66
  143.7 4.1 %all-gather.10 = bf16[128,768]{1,0:T(8,128)(2,1)S(1)} all-gather(bf16[64,768]{1,0:T(8,128)(2,1)S(1)} %get-tuple-element.75), channel_id=12, replica_groups={{0,8},{16,24},{32,40},{48,56},{64,72},{80,88},{96,104},{112,120},{128,1..., dimensions={0}, use_global_device_ids=true | all-gather | bytes 294912 | tf_op jit(solution)/shard_map/all_gather | solution.py:104
  147.8 1.6 shard_map.67
  149.4 7.5 %all-gather.11 = bf16[128,768]{1,0:T(8,128)(2,1)S(1)} all-gather(bf16[64,768]{1,0:T(8,128)(2,1)S(1)} %get-tuple-element.78), channel_id=13, replica_groups={{8,16},{24,32},{40,48},{56,64},{72,80},{88,96},{104,112},{120,128},{136..., dimensions={0}, use_global_device_ids=true | all-gather | bytes 294912 | tf_op jit(solution)/shard_map/all_gather | solution.py:104
  156.9 0.6 shard_map.68
  157.5 4.5 %all-gather.12 = bf16[128,768]{1,0:T(8,128)(2,1)S(1)} all-gather(bf16[64,768]{1,0:T(8,128)(2,1)S(1)} %get-tuple-element.81), channel_id=14, replica_groups={{0,8},{16,24},{32,40},{48,56},{64,72},{80,88},{96,104},{112,120},{128,1..., dimensions={0}, use_global_device_ids=true | all-gather | bytes 294912 | tf_op jit(solution)/shard_map/all_gather | solution.py:104
  161.9 1.7 shard_map.69
  163.6 7.5 %all-gather.13 = bf16[128,768]{1,0:T(8,128)(2,1)S(1)} all-gather(bf16[64,768]{1,0:T(8,128)(2,1)S(1)} %get-tuple-element.84), channel_id=15, replica_groups={{8,16},{24,32},{40,48},{56,64},{72,80},{88,96},{104,112},{120,128},{136..., dimensions={0}, use_global_device_ids=true | all-gather | bytes 294912 | tf_op jit(solution)/shard_map/all_gather | solution.py:104
  171.1 1.2 shard_map.70
  172.3 3.8 %all-gather.14 = bf16[128,512]{1,0:T(8,128)(2,1)S(1)} all-gather(bf16[64,512]{1,0:T(8,128)(2,1)S(1)} %get-tuple-element.86), channel_id=16, replica_groups={{0,8},{16,24},{32,40},{48,56},{64,72},{80,88},{96,104},{112,120},{128,1..., dimensions={0}, use_global_device_ids=true | all-gather | bytes 196608 | tf_op jit(solution)/shard_map/all_gather | solution.py:104
  176.1 0.1 shard_map.71
  176.3 0.1 copy.32
  176.3 0.4 copy.28
  176.7 0.4 reshape.53
  177.1 27.7 %all_to_all.33 = bf16[8,2,8192]{2,1,0:T(2,128)(2,1)S(1)} all-to-all(bf16[8,2,8192]{2,1,0:T(2,128)(2,1)S(1)} %reshape.53), channel_id=1, replica_groups=mesh['sn'=64,'rhs'=8] {'rhs'}, dimensions={0} | all-to-all | bytes 524288 | tf_op jit(solution)/shard_map/all_to_all | solution.py:234
  204.8 0.3 reshape.54
  205.2 0.3 copy.30
  205.5 1.0 all_to_all.30
  (40 shorter events, 0.1 us)
Async XLA Ops:
  0.8 1.0 copy-start
  1.9 2.6 %copy-start.13 = (bf16[7,24,128,128]{3,2,1,0:T(8,128)(2,1)S(1)}, bf16[7,24,128,128]{3,2,1,0:T(8,128)(2,1)}, u32[]{:S(2)}) copy-start(bf16[7,24,128,128]{3,2,1,0:T(8,128)(2,1)} %t_ref.1) | copy-start | bytes 16515076
  4.4 28.1 %copy-start.21 = (f32[512,8,32]{0,2,1:T(8,128)S(1)}, f32[512,8,32]{0,2,1:T(8,128)}, u32[]{:S(2)}) copy-start(f32[512,8,32]{0,2,1:T(8,128)} %param.5) | copy-start | bytes 1572868
  9.3 0.9 copy-start.2
  10.2 1.5 copy-start.4
  11.7 1.5 copy-start.7
  13.2 1.3 copy-start.9
  14.5 1.2 copy-start.11
  15.7 1.0 copy-start.14
  16.7 0.9 copy-start.16
  17.6 0.8 copy-start.18
  18.4 81.6 %collective-permute-start.2 = (bf16[3,256,768]{2,1,0:T(8,128)(2,1)S(1)}, bf16[3,256,768]{2,1,0:T(8,128)(2,1)S(1)}, u32[]{:S(2)}, u32[]{:S(2)}) collective-permute-start(bf16[3,256,768]{2,1,0:T(8,128)(2,1)S(1)} %get-tuple-element.56.bo_ref.refs_2_), channel_id=1, source_target_pairs={{8,16},{24,32},{40,48},{56,64},{72,80},{88,96},{104,112},{120,128}... | collective-permute-start | bytes 3538952 | tf_op jit(solution)/shard_map/ppermute | solution.py:93
  37.3 12.8 %all-to-all-start = ((bf16[8,2,8192]{2,1,0:T(2,128)(2,1)}), bf16[8,2,8192]{2,1,0:T(2,128)(2,1)S(1)}, u32[]{:S(2)}, u32[]{:S(2)}) async-start(bf16[8,2,8192]{2,1,0:T(2,128)(2,1)} %reshape.51), calls=%async_computation | async-start | bytes 524288 | tf_op jit(solution)/shard_map/all_to_all | solution.py:76
  42.8 12.8 %copy-start.1 = (bf16[8,2,128,128]{3,2,1,0:T(8,128)(2,1)S(1)}, bf16[8,2,128,128]{3,2,1,0:T(8,128)(2,1)}, u32[]{:S(2)}) copy-start(bf16[8,2,128,128]{3,2,1,0:T(8,128)(2,1)} %d_ref.5) | copy-start | bytes 1572868
  42.8 62.5 %collective-permute-start.3 = (bf16[2,256,768]{2,1,0:T(8,128)(2,1)}, bf16[2,256,768]{2,1,0:T(8,128)(2,1)}, u32[]{:S(2)}, u32[]{:S(2)}) collective-permute-start(bf16[2,256,768]{2,1,0:T(8,128)(2,1)} %copy-done.2), channel_id=1, source_target_pairs={{0,8},{16,24},{32,40},{48,56},{64,72},{80,88},{96,104},{112,120},{... | collective-permute-start | bytes 2359304 | tf_op jit(solution)/shard_map/ppermute | solution.py:93
  44.8 36.1 %collective-permute-start = (bf16[1,256,768]{2,1,0:T(8,128)(2,1)}, bf16[1,256,768]{2,1,0:T(8,128)(2,1)}, u32[]{:S(2)}, u32[]{:S(2)}) collective-permute-start(bf16[1,256,768]{2,1,0:T(8,128)(2,1)} %copy-done.18), channel_id=1, source_target_pairs={{8,16},{24,32},{40,48},{56,64},{72,80},{88,96},{104,112},{120,128}... | collective-permute-start | bytes 1179656 | tf_op jit(solution)/shard_map/ppermute | solution.py:93
  48.2 42.1 %collective-permute-start.1 = (bf16[1,256,768]{2,1,0:T(8,128)(2,1)S(1)}, bf16[1,256,768]{2,1,0:T(8,128)(2,1)}, u32[]{:S(2)}, u32[]{:S(2)}) collective-permute-start(bf16[1,256,768]{2,1,0:T(8,128)(2,1)S(1)} %get-tuple-element.52.bo_ref.refs_2_), channel_id=1, source_target_pairs={{0,8},{16,24},{32,40},{48,56},{64,72},{80,88},{96,104},{112,120},{... | collective-permute-start | bytes 1179656 | tf_op jit(solution)/shard_map/ppermute | solution.py:93
  80.9 1.8 copy-start.5
  82.6 1.0 copy-start.19
  83.6 6.6 %copy-start.8 = (bf16[1536,768]{1,0:T(8,128)(2,1)S(1)}, bf16[1536,768]{1,0:T(8,128)(2,1)}, u32[]{:S(2)}) copy-start(bf16[1536,768]{1,0:T(8,128)(2,1)} %copy-done.7) | copy-start | bytes 7077892
  90.3 9.7 %copy-start.10 = (bf16[1280,768]{1,0:T(8,128)(2,1)S(1)}, bf16[1280,768]{1,0:T(8,128)(2,1)}, u32[]{:S(2)}) copy-start(bf16[1280,768]{1,0:T(8,128)(2,1)} %copy-done.9) | copy-start | bytes 5898244
  100.0 5.3 %copy-start.3 = (bf16[2,256,768]{2,1,0:T(8,128)(2,1)S(1)}, bf16[2,256,768]{2,1,0:T(8,128)(2,1)}, u32[]{:S(2)}) copy-start(bf16[2,256,768]{2,1,0:T(8,128)(2,1)} %copy-done.2) | copy-start | bytes 2359300
  100.0 5.3 %copy-start.12 = (bf16[1024,768]{1,0:T(8,128)(2,1)S(1)}, bf16[1024,768]{1,0:T(8,128)(2,1)}, u32[]{:S(2)}) copy-start(bf16[1024,768]{1,0:T(8,128)(2,1)} %copy-done.11) | copy-start | bytes 4718596
  105.3 9.6 %copy-start.15 = (bf16[768,768]{1,0:T(8,128)(2,1)S(1)}, bf16[768,768]{1,0:T(8,128)(2,1)}, u32[]{:S(2)}) copy-start(bf16[768,768]{1,0:T(8,128)(2,1)} %copy-done.14) | copy-start | bytes 3538948
  114.9 5.3 %copy-start.17 = (bf16[512,768]{1,0:T(8,128)(2,1)S(1)}, bf16[512,768]{1,0:T(8,128)(2,1)}, u32[]{:S(2)}) copy-start(bf16[512,768]{1,0:T(8,128)(2,1)} %copy-done.16) | copy-start | bytes 2359300
  156.9 5.0 %copy-start.6 = (bf16[1792,768]{1,0:T(8,128)(2,1)S(1)}, bf16[1792,768]{1,0:T(8,128)(2,1)}, u32[]{:S(2)}) copy-start(bf16[1792,768]{1,0:T(8,128)(2,1)} %copy-done.4) | copy-start | bytes 8257540
  161.9 9.1 %copy-start.20 = (bf16[1,256,768]{2,1,0:T(8,128)(2,1)S(1)}, bf16[1,256,768]{2,1,0:T(8,128)(2,1)}, u32[]{:S(2)}) copy-start(bf16[1,256,768]{2,1,0:T(8,128)(2,1)} %copy-done.18) | copy-start | bytes 1179652

commit v3 on v2

v3 whole, which is shorter than its diff:
```python
import jax
import jax.numpy as jnp
from jax import lax
from jax.experimental import pallas as pl
from jax.experimental.pallas import tpu as pltpu
from jax.sharding import PartitionSpec as P

BF = jnp.bfloat16
F32 = jnp.float32
VMEM = pl.BlockSpec(memory_space=pltpu.VMEM)
SMEM = pl.BlockSpec(memory_space=pltpu.SMEM)
HBM = pl.BlockSpec(memory_space=pltpu.HBM)


def dot_t(a, w):
    return lax.dot_general(a, w, (((1,), (1,)), ((), ())), preferred_element_type=F32)


def dot_n(a, w):
    return lax.dot_general(a, w, (((1,), (0,)), ((), ())), preferred_element_type=F32)


def call(body, outs, args, scratch=(), flops=10**7, mib=12, out_specs=None, size=None):
    specs = [SMEM if a.dtype == jnp.int32 else VMEM for a in args]
    if size is None:
        size = sum(a.size * a.dtype.itemsize for a in args)
    return pl.pallas_call(
        body,
        out_shape=[jax.ShapeDtypeStruct(s, d) for s, d in outs],
        in_specs=specs,
        out_specs=out_specs or [VMEM] * len(outs),
        scratch_shapes=list(scratch),
        compiler_params=pltpu.CompilerParams(vmem_limit_bytes=mib * 2**20),
        cost_estimate=pl.CostEstimate(flops=flops, bytes_accessed=size, transcendentals=0),
    )(*args)


def build_operators(tiles, diag, row_slot, col_slot, parity, side_of):
    levels, owned, b, _ = diag.shape
    count = tiles.shape[1]
    tall = owned * b
    wide = 3 * tall

    def body(row_ref, col_ref, par_ref, t_ref, d_ref, *refs):
        outs, (scratch, sems) = refs[: 2 * levels], refs[2 * levels :]
        s_out, b_out, sends = outs[: levels - 1], outs[levels - 1 : 2 * levels - 2], outs[-2:]
        copies = []
        for l in range(levels - 1):
            size = (levels - 1 - l) * tall
            start = sum((levels - 1 - k) * tall for k in range(l))
            buf = scratch.at[pl.ds(start, size), :]
            buf[...] = jnp.zeros((size, wide), BF)

            def add(t, carry):
                r = pl.multiple_of(row_ref[l, t] * b, b)
                c = pl.multiple_of(col_ref[l, t] * b, b)
                at = (pl.ds(r, b), pl.ds(c, b))
                buf[at] = buf[at] + t_ref[l, t]
                return carry

            lax.fori_loop(0, count, add, 0, unroll=8)
            copies.append(pltpu.make_async_copy(buf, s_out[l], sems.at[l]))
            copies[-1].start()
            for q in range(owned):
                rows = slice(q * b, (q + 1) * b)
                b_out[l][rows, :] = dot_n(d_ref[l + 1, q], buf[rows, :]).astype(BF)
            s = side_of(par_ref, l + 1)
            toward = pl.ds(pl.multiple_of((1 - s) * 2 * tall, tall), tall)
            sends[l % 2][l // 2] = b_out[l][:, toward]
        for c in copies:
            c.wait()

    outs = [(((levels - 1 - l) * tall, wide), BF) for l in range(levels - 1)]
    outs += [((tall, wide), BF)] * (levels - 1)
    outs += [((levels // 2, tall, tall), BF), (((levels - 1) // 2, tall, tall), BF)]
    res = call(
        body,
        outs,
        (row_slot, col_slot, parity, tiles, diag),
        [
            pltpu.VMEM((levels * (levels - 1) // 2 * tall, wide), BF),
            pltpu.SemaphoreType.DMA((levels - 1,)),
        ],
        mib=40,
        out_specs=[HBM] * (levels - 1) + [VMEM] * (levels + 1),
        size=2**10,
    )
    return res[: levels - 1], res[levels - 1 : 2 * levels - 2], res[-2:]


def on_device(lanczos_block, diag_inv, factor_tiles, tile_rows, tile_cols):
    levels, owned, b = diag_inv.shape[:3]
    group_tiles = factor_tiles.shape[1]
    n = lax.axis_size("sn")
    peers = lax.axis_size("rhs")
    own = lax.axis_index("sn")
    per_level = owned * n
    w = owned * b
    total, _, piece = lanczos_block.shape
    cols = total // peers
    parity = (own % 2).astype(jnp.int32).reshape(1)

    def side_of(par_ref, l):
        return par_ref[0] if l % 2 == 0 else 1 - par_ref[0]

    def pack(x_ref, o_ref):
        rows = [x_ref[pl.ds(k, total, stride=levels), :] for k in range(levels)]
        v = jnp.concatenate(rows, axis=1).astype(BF)
        for j in range(peers):
            o_ref[j] = v[j * cols : (j + 1) * cols]

    (sent,) = call(pack, [((peers, cols, levels * piece), BF)], (lanczos_block.reshape(total * levels, piece),))
    arrived = lax.all_to_all(sent, "rhs", split_axis=0, concat_axis=0, tiled=True)

    my_rows = lax.dynamic_slice_in_dim(tile_rows, own * group_tiles, group_tiles, 1)
    my_cols = lax.dynamic_slice_in_dim(tile_cols, own * group_tiles, group_tiles, 1)
    above = jnp.arange(1, levels, dtype=jnp.int32)[:, None]
    group = (jnp.arange(group_tiles, dtype=jnp.int32) // (group_tiles // 3))[None, :]
    row_slot = (my_rows // per_level - above) * owned + my_rows % owned
    col_slot = group * owned + my_cols % owned
    sent, factor_tiles = lax.optimization_barrier((sent, factor_tiles))
    S, B, toward = build_operators(factor_tiles, diag_inv, row_slot, col_slot, parity, side_of)

    pairs = [
        [[i, i + 1] for i in range(0, n, 2)],
        [[i, (i + 1) % n] for i in range(1, n, 2)],
    ]
    swaps = [[(p, q) for p, q in g] + [(q, p) for p, q in g] for g in pairs]
    far_odd, far_even = (lax.ppermute(toward[k], "sn", swaps[1 - k]) for k in range(2))
    far = [None] + [(far_odd if l % 2 else far_even)[(l - 1) // 2] for l in range(1, levels)]

    def swap(l, message):
        return lax.all_gather(message, "sn", axis_index_groups=pairs[l % 2])

    def diag_fwd(d_ref, l, f):
        f = f.astype(BF)
        return jnp.concatenate(
            [dot_t(f[:, q * b : (q + 1) * b], d_ref[l, q]) for q in range(owned)], axis=1
        )

    def diag_bwd(d_ref, l, e):
        return jnp.concatenate(
            [dot_n(e[:, q * b : (q + 1) * b], d_ref[l, q]) for q in range(owned)], axis=1
        ).astype(BF)

    def at(start, size):
        return pl.ds(pl.multiple_of(start, w), size)

    def unpack(a_ref, d_ref, x_ref, y_ref):
        for k in range(levels):
            parts = [a_ref[j].astype(F32)[:, k * piece : (k + 1) * piece] for j in range(peers)]
            x_ref[:, k * w : (k + 1) * w] = jnp.concatenate(parts, axis=1)
        y_ref[...] = diag_fwd(d_ref, 0, x_ref[:, :w]).astype(BF)

    x, y0 = call(unpack, [((cols, levels * w), F32), ((cols, w), BF)], (arrived, diag_inv))

    def forward_step(l, got, before, acc):
        more, rest_levels = l + 1 < levels, levels - l - 2
        base = 2 * w if l == 1 else (w if l == 0 else 0)
        args, outs = (parity, got), [((cols, 2 * w), BF)]
        if l:
            args += (B[l - 1], far[l])
        if more:
            args += (B[l], diag_inv, acc)
            outs.append(((cols, 2 * w), BF))
            if l:
                args += (S[l - 1], before)
                if rest_levels:
                    outs.append(((cols, rest_levels * w), F32))
        n_in = len(args)

        def step(*refs):
            par_ref, g_ref = refs[:2]
            p_ref, y3 = refs[n_in], refs[-1]
            s = side_of(par_ref, l)
            if l:
                near_ref, far_ref = refs[2:4]
                y_own, y_par = g_ref[s, :, w:], g_ref[1 - s, :, w:]
                q_own, q_par = g_ref[s, :, :w].astype(F32), g_ref[1 - s, :, :w].astype(F32)
                new = (q_own - dot_t(y_par, near_ref[:, at((1 - s) * 2 * w, w)])).astype(BF)
                p_ref[:, at(s * w, w)] = new
                p_ref[:, at((1 - s) * w, w)] = (q_par - dot_t(y_own, far_ref[...])).astype(BF)
            else:
                p_ref[:, :w] = g_ref[0]
                p_ref[:, w:] = g_ref[1]
                new = g_ref[s]
            if not more:
                return
            m_ref = refs[n_in + 1]
            m_ref[:, w:] = new
            k = 4 if l else 2
            next_ref, d_ref, acc_ref = refs[k : k + 3]
            f = acc_ref[:, base : base + w]
            if l:
                s_ref, before_ref = refs[k + 3 : k + 5]
                y3[:, at(s * w, 2 * w)] = before_ref[...]
                y3[:, at((1 - s) * 2 * w, w)] = y_par
                f = f - dot_t(y3[...], s_ref[w : 2 * w, :])
            h = diag_fwd(d_ref, l + 1, f)
            q = h - dot_t(p_ref[...], next_ref[:, at((1 - s) * w, 2 * w)])
            m_ref[:, :w] = q.astype(BF)
            if l and rest_levels:
                refs[n_in + 2][...] = acc_ref[:, base + w :] - dot_t(y3[...], s_ref[2 * w :, :])

        res = call(step, outs, args, [pltpu.VMEM((cols, 3 * w), BF)])
        return res[0], res[1] if more else None, res[-1] if l else acc

    pair_y = [None] * levels
    acc, message, before = x, y0, None
    for l in range(levels):
        before, message, acc = forward_step(l, swap(l, message), before, acc)
        pair_y[l] = before

    def backward_step(l, got, older, above):
        top, more = l == levels - 1, l >= 2
        args = (parity, pair_y[l], B[l - 1], far[l], diag_inv)
        if not top:
            args += (got, older)
        if more:
            args += (S[l - 2], *above)
        n_in = len(args)
        outs = [((cols, 3 * w if more else 2 * w), BF), ((cols, w), BF)]
        if more:
            outs.append(((cols, 3 * w), F32))

        def step(*refs):
            par_ref, y_ref, near_ref, far_ref, d_ref = refs[:5]
            m_ref, z_ref = refs[n_in : n_in + 2]
            e_ref = refs[-1]
            s = side_of(par_ref, l)
            e = y_ref[...]
            if not top:
                g_ref, old_ref = refs[5:7]
                e = e.astype(F32) - g_ref[0, :, : 2 * w].astype(F32) - g_ref[1, :, : 2 * w].astype(F32)
            e_ref[...] = e.astype(BF)
            e_own, e_par = e_ref[:, at(s * w, w)], e_ref[:, at((1 - s) * w, w)]
            z_own = diag_bwd(d_ref, l, e_own)
            z_ref[...] = z_own
            part = dot_n(e_own, near_ref[:, at(s * w, 2 * w)])
            extra = dot_n(e_par, far_ref[...])
            if not top:
                part = part + old_ref[:, at(s * w, 2 * w)]
                extra = extra + g_ref[1 - s, :, 2 * w :].astype(F32)
            for k in range(2):
                half = part[:, k * w : (k + 1) * w]
                m_ref[:, k * w : (k + 1) * w] = jnp.where(s == 1 - k, half + extra, half).astype(BF)
            if more:
                s_ref, old_out = refs[n_in - 1 - len(above)], refs[n_in + 2]
                sums = dot_n(z_own, s_ref[w : 2 * w, :])
                for k, zr in enumerate(refs[n_in - len(above) : n_in]):
                    sums = sums + dot_n(zr[...], s_ref[(k + 2) * w : (k + 3) * w, :])
                old_out[...] = sums
                m_ref[:, 2 * w :] = old_out[:, at(s * 2 * w, w)].astype(BF)

        res = call(step, outs, args, [pltpu.VMEM((cols, 2 * w), BF)])
        return res[0], res[1], res[2] if more else None

    z = [None] * levels
    got, older = None, None
    for l in range(levels - 1, 0, -1):
        message, z[l], older = backward_step(l, got, older, z[l + 1 :])
        got = swap(l - 1, message)

    def finish(par_ref, g_ref, y_ref, d_ref, *rest):
        o_ref = rest[-1]
        here = at(par_ref[0] * w, w)
        terms = g_ref[0, :, here].astype(F32) + g_ref[1, :, here].astype(F32)
        e = (y_ref[...].astype(F32) - terms).astype(BF)
        values = [diag_bwd(d_ref, 0, e).astype(F32)] + [r[...].astype(F32) for r in rest[:-1]]
        for j in range(peers):
            parts = [v[:, j * piece : (j + 1) * piece] for v in values]
            o_ref[j] = jnp.concatenate(parts, axis=1).astype(BF)

    (result,) = call(finish, [((peers, cols, levels * piece), BF)], (parity, got, y0, diag_inv, *z[1:]))
    result = lax.all_to_all(result, "rhs", split_axis=0, concat_axis=0, tiled=True)
    return result.reshape(total, levels, piece)


def solution(mesh):
    placed = (
        P(None, None, ("sn", "rhs")),
        P(None, "sn", None, None),
        P(None, "sn", None, None),
        P(),
        P(),
    )
    return jax.shard_map(
        on_device,
        mesh=mesh,
        in_specs=placed,
        out_specs=P(None, None, ("sn", "rhs")),
        check_vma=False,
    )
```

time: 208 us -> 162 us (0.78)
  local copies, waits for them, and re-layouts: 28.2 us -> 3.3 us
  starting transfers between devices: 26.9 us -> 16.8 us
  Pallas kernels: 23.5 us -> 17.9 us
  blocking collectives: 127 us -> 122 us
    unnamed x49 -> x5, local copies, waits for them, and re-layouts: 20.8 us -> 1.9 us
    all_gather x15, blocking collectives: 99.2 us -> 84 us  [swap(): return lax.all_gather(message, 'sn', axis_index_groups=pairs[l % 2])]
    all_to_all x1 -> x2, blocking collectives: 27.7 us -> 38.3 us  [the longest x1 26 us: on_device(): lax.all_to_all(result, 'rhs', split_axis=0, concat_axis=0, tiled=True)]
    pallas_call x17 -> x19, Pallas kernels: 23.5 us -> 17.9 us  [call(): pl.pallas_call(body, out_shape=[jax.ShapeDtypeStruct(s, d) for s, d in ou...]
    all_to_all x1 -> x0, starting transfers between devices: 5.42 us -> none  [on_device(): lax.all_to_all(lanczos_block.astype(BF), 'rhs', split_axis=0, concat_axis...]
    ppermute x4 -> x2, starting transfers between devices: 21.4 us -> 16.8 us  [on_device(): lax.ppermute(toward[k], 'sn', swaps[1 - k])]
    all_to_all x3 -> x1, local copies, waits for them, and re-layouts: 4.06 us -> 0.31 us  [on_device(): lax.all_to_all(result, 'rhs', split_axis=0, concat_axis=0, tiled=True)]
  transfers between devices with their start and end apart: 5 -> 2, of which waited for: 0 -> 0; matrix products, arithmetic and copies ran while one was open for 5% -> 0% of each run, Pallas kernels for 3% -> 0%
where the time goes in v3:
time: 162 us; the launch traced here: 161 us
  blocking collectives  122 us (75%)
  Pallas kernels  17.9 us (11%)
  starting transfers between devices  16.8 us (10%)
  local copies, waits for them, and re-layouts  3.3 us (2%)
    all_gather x15, blocking collectives, swap(): return lax.all_gather(message, 'sn', axis_index_groups=pairs[l % 2])  84 us
    all_to_all x1, blocking collectives, on_device(): lax.all_to_all(result, 'rhs', split_axis=0, concat_axis=0, tiled=True)  26 us
    pallas_call x19, Pallas kernels, call(): pl.pallas_call(body, out_shape=[jax.ShapeDtypeStruct(s, d) for s, d in ou...  17.9 us
    ppermute x2, starting transfers between devices, on_device(): lax.ppermute(toward[k], 'sn', swaps[1 - k])  16.8 us
    all_to_all x1, blocking collectives, on_device(): lax.all_to_all(sent, 'rhs', split_axis=0, concat_axis=0, tiled=True)  12.3 us
  transfers between devices with their start and end apart: 2, of which 0 were waited for; matrix products, arithmetic and copies ran while one was open for 0% of the time, Pallas kernels for 0%

profile of v3, /device:TPU:1, one launch (start us, length us, event | category | flops | bytes accessed | tf_op | source)
XLA Modules:
  0.0 161.3 jit_solution(15634374685691418149)
XLA Ops:
  0.0 0.0 copy-start
  0.0 1.9 %copy.8 = f32[512,8,32]{2,1,0:T(8,128)S(1)} copy(f32[512,8,32]{0,2,1:T(8,128)} %param.5) | data formatting | bytes 1048576 | tf_op args[0]
  1.9 0.5 shard_map.55
  2.4 0.8 fusion.3
  3.2 0.0 copy-done
  3.2 7.8 %shard_map.57 = (bf16[1792,768]{1,0:T(8,128)(2,1)}, bf16[1536,768]{1,0:T(8,128)(2,1)S(1)}, bf16[1280,768]{1,0:T(8,128)(2,1)S(1)}, bf16[1024,768]{1,0:T(8,128)(2,...) custom-call(s32[7,24]{1,0:T(8,128)S(1)} %get-tuple-element.126.row_r, ...), custom_call_target="tpu_custom_call" | custom-call | flops 10000000 | bytes 1024 | tf_op jit(solution)/shard_map/pallas_call | solution.py:27
  11.1 4.4 %collective-permute-start.1 = (bf16[3,256,256]{2,1,0:T(8,128)(2,1)S(1)}, bf16[3,256,256]{2,1,0:T(8,128)(2,1)S(1)}, u32[]{:S(2)}, u32[]{:S(2)}) collective-permute-start(bf16[3,256,256]{2,1,0:T(8,128)(2,1)S(1)} %get-tuple-element.73), channel_id=1, source_target_pairs={{0,8},{16,24},{32,40},{48,56},{64,72},{80,88},{96,104},{112,120},{... | collective-permute-start | bytes 1179656 | tf_op jit(solution)/shard_map/ppermute | solution.py:129
  15.4 12.4 %collective-permute-start = (bf16[4,256,256]{2,1,0:T(8,128)(2,1)S(1)}, bf16[4,256,256]{2,1,0:T(8,128)(2,1)S(1)}, u32[]{:S(2)}, u32[]{:S(2)}) collective-permute-start(bf16[4,256,256]{2,1,0:T(8,128)(2,1)S(1)} %get-tuple-element.67), channel_id=1, source_target_pairs={{8,16},{24,32},{40,48},{56,64},{72,80},{88,96},{104,112},{120,128}... | collective-permute-start | bytes 1572872 | tf_op jit(solution)/shard_map/ppermute | solution.py:129
  27.8 12.3 %all_to_all.10.a_ref = bf16[8,64,256]{2,1,0:T(8,128)(2,1)S(1)} all-to-all(bf16[8,64,256]{2,1,0:T(8,128)(2,1)S(1)} %shard_map.55), channel_id=1, replica_groups=mesh['sn'=64,'rhs'=8] {'rhs'}, dimensions={0} | all-to-all | bytes 524288 | tf_op jit(solution)/shard_map/all_to_all | solution.py:113
  40.1 0.0 copy-start.1
  40.1 0.3 shard_map.56
  40.4 3.6 %all-gather = bf16[128,256]{1,0:T(8,128)(2,1)S(1)} all-gather(bf16[64,256]{1,0:T(8,128)(2,1)S(1)} %get-tuple-element.62.y_ref), channel_id=2, replica_groups={{0,8},{16,24},{32,40},{48,56},{64,72},{80,88},{96,104},{112,120},{128,1..., dimensions={0}, use_global_device_ids=true | all-gather | bytes 98304 | tf_op jit(solution)/shard_map/all_gather | solution.py:133
  44.0 0.2 shard_map.58
  44.2 7.1 %all-gather.1 = bf16[128,512]{1,0:T(8,128)(2,1)S(1)} all-gather(bf16[64,512]{1,0:T(8,128)(2,1)S(1)} %get-tuple-element.66), channel_id=3, replica_groups={{8,16},{24,32},{40,48},{56,64},{72,80},{88,96},{104,112},{120,128},{136..., dimensions={0}, use_global_device_ids=true | all-gather | bytes 196608 | tf_op jit(solution)/shard_map/all_gather | solution.py:133
  51.4 0.0 collective-permute-done.1
  51.4 0.0 collective-permute-done
  51.5 0.0 copy-done.1
  51.5 1.1 shard_map.59
  52.6 3.8 %all-gather.2 = bf16[128,512]{1,0:T(8,128)(2,1)S(1)} all-gather(bf16[64,512]{1,0:T(8,128)(2,1)S(1)} %get-tuple-element.72), channel_id=4, replica_groups={{0,8},{16,24},{32,40},{48,56},{64,72},{80,88},{96,104},{112,120},{128,1..., dimensions={0}, use_global_device_ids=true | all-gather | bytes 196608 | tf_op jit(solution)/shard_map/all_gather | solution.py:133
  56.4 1.1 shard_map.60
  57.5 7.1 %all-gather.3 = bf16[128,512]{1,0:T(8,128)(2,1)S(1)} all-gather(bf16[64,512]{1,0:T(8,128)(2,1)S(1)} %get-tuple-element.78), channel_id=5, replica_groups={{8,16},{24,32},{40,48},{56,64},{72,80},{88,96},{104,112},{120,128},{136..., dimensions={0}, use_global_device_ids=true | all-gather | bytes 196608 | tf_op jit(solution)/shard_map/all_gather | solution.py:133
  64.6 0.9 shard_map.61
  65.6 4.0 %all-gather.4 = bf16[128,512]{1,0:T(8,128)(2,1)S(1)} all-gather(bf16[64,512]{1,0:T(8,128)(2,1)S(1)} %get-tuple-element.83), channel_id=6, replica_groups={{0,8},{16,24},{32,40},{48,56},{64,72},{80,88},{96,104},{112,120},{128,1..., dimensions={0}, use_global_device_ids=true | all-gather | bytes 196608 | tf_op jit(solution)/shard_map/all_gather | solution.py:133
  69.6 0.9 shard_map.62
  70.5 7.1 %all-gather.5 = bf16[128,512]{1,0:T(8,128)(2,1)S(1)} all-gather(bf16[64,512]{1,0:T(8,128)(2,1)S(1)} %get-tuple-element.88), channel_id=7, replica_groups={{8,16},{24,32},{40,48},{56,64},{72,80},{88,96},{104,112},{120,128},{136..., dimensions={0}, use_global_device_ids=true | all-gather | bytes 196608 | tf_op jit(solution)/shard_map/all_gather | solution.py:133
  77.6 0.7 shard_map.63
  78.3 4.1 %all-gather.6 = bf16[128,512]{1,0:T(8,128)(2,1)S(1)} all-gather(bf16[64,512]{1,0:T(8,128)(2,1)S(1)} %get-tuple-element.93), channel_id=8, replica_groups={{0,8},{16,24},{32,40},{48,56},{64,72},{80,88},{96,104},{112,120},{128,1..., dimensions={0}, use_global_device_ids=true | all-gather | bytes 196608 | tf_op jit(solution)/shard_map/all_gather | solution.py:133
  82.4 0.7 shard_map.64
  83.1 7.1 %all-gather.7 = bf16[128,512]{1,0:T(8,128)(2,1)S(1)} all-gather(bf16[64,512]{1,0:T(8,128)(2,1)S(1)} %get-tuple-element.98), channel_id=9, replica_groups={{8,16},{24,32},{40,48},{56,64},{72,80},{88,96},{104,112},{120,128},{136..., dimensions={0}, use_global_device_ids=true | all-gather | bytes 196608 | tf_op jit(solution)/shard_map/all_gather | solution.py:133
  90.2 0.2 shard_map.65.refs_1_
  90.5 0.3 shard_map.66
  90.8 4.1 %all-gather.8 = bf16[128,768]{1,0:T(8,128)(2,1)S(1)} all-gather(bf16[64,768]{1,0:T(8,128)(2,1)S(1)} %get-tuple-element.99), channel_id=10, replica_groups={{0,8},{16,24},{32,40},{48,56},{64,72},{80,88},{96,104},{112,120},{128,1..., dimensions={0}, use_global_device_ids=true | all-gather | bytes 294912 | tf_op jit(solution)/shard_map/all_gather | solution.py:133
  94.9 0.4 shard_map.67
  95.3 7.5 %all-gather.9 = bf16[128,768]{1,0:T(8,128)(2,1)S(1)} all-gather(bf16[64,768]{1,0:T(8,128)(2,1)S(1)} %get-tuple-element.102), channel_id=11, replica_groups={{8,16},{24,32},{40,48},{56,64},{72,80},{88,96},{104,112},{120,128},{136..., dimensions={0}, use_global_device_ids=true | all-gather | bytes 294912 | tf_op jit(solution)/shard_map/all_gather | solution.py:133
  102.8 0.4 shard_map.68
  103.2 4.1 %all-gather.10 = bf16[128,768]{1,0:T(8,128)(2,1)S(1)} all-gather(bf16[64,768]{1,0:T(8,128)(2,1)S(1)} %get-tuple-element.105), channel_id=12, replica_groups={{0,8},{16,24},{32,40},{48,56},{64,72},{80,88},{96,104},{112,120},{128,1..., dimensions={0}, use_global_device_ids=true | all-gather | bytes 294912 | tf_op jit(solution)/shard_map/all_gather | solution.py:133
  107.4 0.5 shard_map.69
  107.9 7.5 %all-gather.11 = bf16[128,768]{1,0:T(8,128)(2,1)S(1)} all-gather(bf16[64,768]{1,0:T(8,128)(2,1)S(1)} %get-tuple-element.108), channel_id=13, replica_groups={{8,16},{24,32},{40,48},{56,64},{72,80},{88,96},{104,112},{120,128},{136..., dimensions={0}, use_global_device_ids=true | all-gather | bytes 294912 | tf_op jit(solution)/shard_map/all_gather | solution.py:133
  115.3 0.6 shard_map.70
  115.9 4.7 %all-gather.12 = bf16[128,768]{1,0:T(8,128)(2,1)S(1)} all-gather(bf16[64,768]{1,0:T(8,128)(2,1)S(1)} %get-tuple-element.111), channel_id=14, replica_groups={{0,8},{16,24},{32,40},{48,56},{64,72},{80,88},{96,104},{112,120},{128,1..., dimensions={0}, use_global_device_ids=true | all-gather | bytes 294912 | tf_op jit(solution)/shard_map/all_gather | solution.py:133
  120.6 0.6 shard_map.71
  121.2 8.4 %all-gather.13 = bf16[128,768]{1,0:T(8,128)(2,1)S(1)} all-gather(bf16[64,768]{1,0:T(8,128)(2,1)S(1)} %get-tuple-element.114), channel_id=15, replica_groups={{8,16},{24,32},{40,48},{56,64},{72,80},{88,96},{104,112},{120,128},{136..., dimensions={0}, use_global_device_ids=true | all-gather | bytes 294912 | tf_op jit(solution)/shard_map/all_gather | solution.py:133
  129.6 0.2 shard_map.72
  129.8 3.8 %all-gather.14 = bf16[128,512]{1,0:T(8,128)(2,1)S(1)} all-gather(bf16[64,512]{1,0:T(8,128)(2,1)S(1)} %get-tuple-element.116), channel_id=16, replica_groups={{0,8},{16,24},{32,40},{48,56},{64,72},{80,88},{96,104},{112,120},{128,1..., dimensions={0}, use_global_device_ids=true | all-gather | bytes 196608 | tf_op jit(solution)/shard_map/all_gather | solution.py:133
  133.6 0.3 shard_map.73
  133.9 26.0 %all_to_all.11 = bf16[8,64,256]{2,1,0:T(8,128)(2,1)S(1)} all-to-all(bf16[8,64,256]{2,1,0:T(8,128)(2,1)S(1)} %shard_map.73), channel_id=1, replica_groups=mesh['sn'=64,'rhs'=8] {'rhs'}, dimensions={0} | all-to-all | bytes 524288 | tf_op jit(solution)/shard_map/all_to_all | solution.py:275
  160.0 0.3 copy.9
  160.3 1.0 reshape.30
  (4 shorter events, 0.1 us)
Async XLA Ops:
  0.0 3.2 %copy-start = (bf16[8,2,128,128]{3,2,1,0:T(8,128)(2,1)S(1)}, bf16[8,2,128,128]{3,2,1,0:T(8,128)(2,1)}, u32[]{:S(2)}) copy-start(bf16[8,2,128,128]{3,2,1,0:T(8,128)(2,1)} %d_ref.5) | copy-start | bytes 1572868
  11.1 40.3 %collective-permute-start.1 = (bf16[3,256,256]{2,1,0:T(8,128)(2,1)S(1)}, bf16[3,256,256]{2,1,0:T(8,128)(2,1)S(1)}, u32[]{:S(2)}, u32[]{:S(2)}) collective-permute-start(bf16[3,256,256]{2,1,0:T(8,128)(2,1)S(1)} %get-tuple-element.73), channel_id=1, source_target_pairs={{0,8},{16,24},{32,40},{48,56},{64,72},{80,88},{96,104},{112,120},{... | collective-permute-start | bytes 1179656 | tf_op jit(solution)/shard_map/ppermute | solution.py:129
  15.4 36.0 %collective-permute-start = (bf16[4,256,256]{2,1,0:T(8,128)(2,1)S(1)}, bf16[4,256,256]{2,1,0:T(8,128)(2,1)S(1)}, u32[]{:S(2)}, u32[]{:S(2)}) collective-permute-start(bf16[4,256,256]{2,1,0:T(8,128)(2,1)S(1)} %get-tuple-element.67), channel_id=1, source_target_pairs={{8,16},{24,32},{40,48},{56,64},{72,80},{88,96},{104,112},{120,128}... | collective-permute-start | bytes 1572872 | tf_op jit(solution)/shard_map/ppermute | solution.py:129
  40.1 11.3 %copy-start.1 = (bf16[1792,768]{1,0:T(8,128)(2,1)S(1)}, bf16[1792,768]{1,0:T(8,128)(2,1)}, u32[]{:S(2)}) copy-start(bf16[1792,768]{1,0:T(8,128)(2,1)} %get-tuple-element.69.refs_7_) | copy-start | bytes 8257540

commit v4 on v3

--- a/solution.py
+++ b/solution.py
@@ -20,8 +20,8 @@
     return lax.dot_general(a, w, (((1,), (0,)), ((), ())), preferred_element_type=F32)
 
 
-def call(body, outs, args, scratch=(), flops=10**7, mib=12, out_specs=None, size=None):
-    specs = [SMEM if a.dtype == jnp.int32 else VMEM for a in args]
+def call(body, outs, args, scratch=(), flops=10**7, mib=12, specs=None, out_specs=None, size=None):
+    specs = specs or [SMEM if a.dtype == jnp.int32 else VMEM for a in args]
     if size is None:
         size = sum(a.size * a.dtype.itemsize for a in args)
     return pl.pallas_call(
@@ -42,20 +42,26 @@
     wide = 3 * tall
 
     def body(row_ref, col_ref, par_ref, t_ref, d_ref, *refs):
-        outs, (scratch, sems) = refs[: 2 * levels], refs[2 * levels :]
+        outs, (scratch, held, sems, in_sems) = refs[: 2 * levels], refs[2 * levels :]
         s_out, b_out, sends = outs[: levels - 1], outs[levels - 1 : 2 * levels - 2], outs[-2:]
+        loads = [
+            pltpu.make_async_copy(t_ref.at[l], held.at[l], in_sems.at[l]) for l in range(levels - 1)
+        ]
+        for c in loads:
+            c.start()
         copies = []
         for l in range(levels - 1):
             size = (levels - 1 - l) * tall
             start = sum((levels - 1 - k) * tall for k in range(l))
             buf = scratch.at[pl.ds(start, size), :]
             buf[...] = jnp.zeros((size, wide), BF)
+            loads[l].wait()
 
             def add(t, carry):
                 r = pl.multiple_of(row_ref[l, t] * b, b)
                 c = pl.multiple_of(col_ref[l, t] * b, b)
                 at = (pl.ds(r, b), pl.ds(c, b))
-                buf[at] = buf[at] + t_ref[l, t]
+                buf[at] = buf[at] + held[l, t]
                 return carry
 
             lax.fori_loop(0, count, add, 0, unroll=8)
@@ -79,11 +85,15 @@
         (row_slot, col_slot, parity, tiles, diag),
         [
             pltpu.VMEM((levels * (levels - 1) // 2 * tall, wide), BF),
+            pltpu.VMEM(tiles.shape, BF),
+            pltpu.SemaphoreType.DMA((levels - 1,)),
             pltpu.SemaphoreType.DMA((levels - 1,)),
         ],
-        mib=40,
+        flops=4 * 10**8,
+        mib=60,
+        specs=[SMEM, SMEM, SMEM, HBM, VMEM],
         out_specs=[HBM] * (levels - 1) + [VMEM] * (levels + 1),
-        size=2**10,
+        size=24 * 2**20,
     )
     return res[: levels - 1], res[levels - 1 : 2 * levels - 2], res[-2:]
 
@@ -104,12 +114,12 @@
         return par_ref[0] if l % 2 == 0 else 1 - par_ref[0]
 
     def pack(x_ref, o_ref):
-        rows = [x_ref[pl.ds(k, total, stride=levels), :] for k in range(levels)]
-        v = jnp.concatenate(rows, axis=1).astype(BF)
+        v = x_ref[...].T.astype(BF)
         for j in range(peers):
             o_ref[j] = v[j * cols : (j + 1) * cols]
 
-    (sent,) = call(pack, [((peers, cols, levels * piece), BF)], (lanczos_block.reshape(total * levels, piece),))
+    flat = lanczos_block.transpose(1, 2, 0).reshape(levels * piece, total)
+    (sent,) = call(pack, [((peers, cols, levels * piece), BF)], (flat,))
     arrived = lax.all_to_all(sent, "rhs", split_axis=0, concat_axis=0, tiled=True)
 
     my_rows = lax.dynamic_slice_in_dim(tile_rows, own * group_tiles, group_tiles, 1)
@@ -126,6 +136,7 @@
         [[i, (i + 1) % n] for i in range(1, n, 2)],
     ]
     swaps = [[(p, q) for p, q in g] + [(q, p) for p, q in g] for g in pairs]
+    arrived, toward = lax.optimization_barrier((arrived, list(toward)))
     far_odd, far_even = (lax.ppermute(toward[k], "sn", swaps[1 - k]) for k in range(2))
     far = [None] + [(far_odd if l % 2 else far_even)[(l - 1) // 2] for l in range(1, levels)]
 
@@ -273,7 +284,13 @@
 
     (result,) = call(finish, [((peers, cols, levels * piece), BF)], (parity, got, y0, diag_inv, *z[1:]))
     result = lax.all_to_all(result, "rhs", split_axis=0, concat_axis=0, tiled=True)
-    return result.reshape(total, levels, piece)
+
+    def turn(r_ref, o_ref):
+        for j in range(peers):
+            o_ref[:, j * cols : (j + 1) * cols] = r_ref[j].astype(F32).T.astype(BF)
+
+    (result,) = call(turn, [((levels * piece, total), BF)], (result,))
+    return result.reshape(levels, piece, total).transpose(2, 0, 1)
 
 
 def solution(mesh):

time: 162 us -> 159 us (0.981)
  blocking collectives: 122 us -> 112 us
  starting transfers between devices: 16.8 us -> 22.2 us
  Pallas kernels: 17.9 us -> 20.1 us
    all_to_all x1 -> x0, blocking collectives: 12.3 us -> none  [on_device(): lax.all_to_all(sent, 'rhs', split_axis=0, concat_axis=0, tiled=True)]
    all_to_all x0 -> x1, starting transfers between devices: none -> 10.2 us  [on_device(): lax.all_to_all(sent, 'rhs', split_axis=0, concat_axis=0, tiled=True)]
    ppermute x2, starting transfers between devices: 16.8 us -> 12 us  [on_device(): lax.ppermute(toward[k], 'sn', swaps[1 - k])]
    pallas_call x19 -> x20, Pallas kernels: 17.9 us -> 20.1 us  [call(): pl.pallas_call(body, out_shape=[jax.ShapeDtypeStruct(s, d) for s, d in ou...]
    all_to_all x1, blocking collectives: 26 us -> 27.7 us  [on_device(): lax.all_to_all(result, 'rhs', split_axis=0, concat_axis=0, tiled=True)]
  transfers between devices with their start and end apart: 2 -> 3, of which waited for: 0 -> 0; matrix products, arithmetic and copies ran while one was open for 0% -> 1% of each run, Pallas kernels for 0% -> 6%
where the time goes in v4:
time: 159 us; the launch traced here: 158 us
  blocking collectives  112 us (70%)
  starting transfers between devices  22.2 us (14%)
  Pallas kernels  20.1 us (13%)
  local copies, waits for them, and re-layouts  2.16 us (1%)
    all_gather x15, blocking collectives, swap(): return lax.all_gather(message, 'sn', axis_index_groups=pairs[l % 2])  84.3 us
    all_to_all x1, blocking collectives, on_device(): lax.all_to_all(result, 'rhs', split_axis=0, concat_axis=0, tiled=True)  27.7 us
    pallas_call x20, Pallas kernels, call(): pl.pallas_call(body, out_shape=[jax.ShapeDtypeStruct(s, d) for s, d in ou...  20.1 us
    ppermute x2, starting transfers between devices, on_device(): lax.ppermute(toward[k], 'sn', swaps[1 - k])  12 us
    all_to_all x1, starting transfers between devices, on_device(): lax.all_to_all(sent, 'rhs', split_axis=0, concat_axis=0, tiled=True)  10.2 us
  transfers between devices with their start and end apart: 3, of which 0 were waited for; matrix products, arithmetic and copies ran while one was open for 1% of the time, Pallas kernels for 6%

profile of v4, /device:TPU:1, one launch (start us, length us, event | category | flops | bytes accessed | tf_op | source)
XLA Modules:
  0.0 158.2 jit_solution(9341830968555342650)
XLA Ops:
  0.0 1.0 copy-done.15
  1.0 0.8 shard_map.55
  1.9 10.2 %all-to-all-start = ((bf16[8,64,256]{2,1,0:T(8,128)(2,1)}), bf16[8,64,256]{2,1,0:T(8,128)(2,1)S(1)}, u32[]{:S(2)}, u32[]{:S(2)}) async-start(bf16[8,64,256]{2,1,0:T(8,128)(2,1)} %shard_map.55), calls=%async_computation | async-start | bytes 524288 | tf_op jit(solution)/shard_map/all_to_all | solution.py:123
  12.1 1.4 fusion.3
  13.5 8.6 %shard_map.56 = (bf16[1792,768]{1,0:T(8,128)(2,1)}, bf16[1536,768]{1,0:T(8,128)(2,1)}, bf16[1280,768]{1,0:T(8,128)(2,1)}, bf16[1024,768]{1,0:T(8,128)(2,1)}, bf1...) custom-call(s32[7,24]{1,0:T(8,128)} %get-tuple-element.132.row_ref, ...), custom_call_target="tpu_custom_call" | custom-call | flops 400000000 | bytes 25165824 | tf_op jit(solution)/shard_map/pallas_call | solution.py:27
  22.1 0.0 copy-start.1
  22.1 0.0 all-to-all-done.a_ref
  22.1 0.0 copy-start.6
  22.1 2.2 %collective-permute-start.1 = (bf16[3,256,256]{2,1,0:T(8,128)(2,1)}, bf16[3,256,256]{2,1,0:T(8,128)(2,1)S(1)}, u32[]{:S(2)}, u32[]{:S(2)}) collective-permute-start(bf16[3,256,256]{2,1,0:T(8,128)(2,1)} %get-tuple-element.79), channel_id=1, source_target_pairs={{0,8},{16,24},{32,40},{48,56},{64,72},{80,88},{96,104},{112,120},{... | collective-permute-start | bytes 1179656 | tf_op jit(solution)/shard_map/ppermute | solution.py:140
  24.3 9.8 %collective-permute-start = (bf16[4,256,256]{2,1,0:T(8,128)(2,1)}, bf16[4,256,256]{2,1,0:T(8,128)(2,1)S(1)}, u32[]{:S(2)}, u32[]{:S(2)}) collective-permute-start(bf16[4,256,256]{2,1,0:T(8,128)(2,1)} %get-tuple-element.73), channel_id=1, source_target_pairs={{8,16},{24,32},{40,48},{56,64},{72,80},{88,96},{104,112},{120,128}... | collective-permute-start | bytes 1572872 | tf_op jit(solution)/shard_map/ppermute | solution.py:140
  34.1 0.0 copy-done
  34.1 0.3 shard_map.57
  34.4 3.7 %all-gather = bf16[128,256]{1,0:T(8,128)(2,1)S(1)} all-gather(bf16[64,256]{1,0:T(8,128)(2,1)S(1)} %get-tuple-element.69.y_ref), channel_id=2, replica_groups={{0,8},{16,24},{32,40},{48,56},{64,72},{80,88},{96,104},{112,120},{128,1..., dimensions={0}, use_global_device_ids=true | all-gather | bytes 98304 | tf_op jit(solution)/shard_map/all_gather | solution.py:144
  38.2 1.0 copy-done.8
  39.2 0.3 shard_map.58
  39.4 7.8 %all-gather.1 = bf16[128,512]{1,0:T(8,128)(2,1)S(1)} all-gather(bf16[64,512]{1,0:T(8,128)(2,1)S(1)} %get-tuple-element.72), channel_id=3, replica_groups={{8,16},{24,32},{40,48},{56,64},{72,80},{88,96},{104,112},{120,128},{136..., dimensions={0}, use_global_device_ids=true | all-gather | bytes 196608 | tf_op jit(solution)/shard_map/all_gather | solution.py:144
  47.2 0.0 collective-permute-done.1
  47.3 0.0 collective-permute-done
  47.3 0.0 copy-done.1
  47.3 0.0 copy-done.6
  47.3 0.0 copy-start.2
  47.3 0.0 copy-start.7
  47.3 1.1 shard_map.59
  48.5 0.0 copy-start.3
  48.5 0.0 copy-start.11
  48.5 3.9 %all-gather.2 = bf16[128,512]{1,0:T(8,128)(2,1)S(1)} all-gather(bf16[64,512]{1,0:T(8,128)(2,1)S(1)} %get-tuple-element.78), channel_id=4, replica_groups={{0,8},{16,24},{32,40},{48,56},{64,72},{80,88},{96,104},{112,120},{128,1..., dimensions={0}, use_global_device_ids=true | all-gather | bytes 196608 | tf_op jit(solution)/shard_map/all_gather | solution.py:144
  52.4 0.0 copy-done.2
  52.4 0.0 copy-done.7
  52.4 1.1 shard_map.60
  53.6 0.0 copy-start.4
  53.6 0.0 copy-start.12
  53.6 7.3 %all-gather.3 = bf16[128,512]{1,0:T(8,128)(2,1)S(1)} all-gather(bf16[64,512]{1,0:T(8,128)(2,1)S(1)} %get-tuple-element.84), channel_id=5, replica_groups={{8,16},{24,32},{40,48},{56,64},{72,80},{88,96},{104,112},{120,128},{136..., dimensions={0}, use_global_device_ids=true | all-gather | bytes 196608 | tf_op jit(solution)/shard_map/all_gather | solution.py:144
  60.9 0.0 copy-done.3
  60.9 0.0 copy-done.11
  60.9 0.9 shard_map.61
  61.8 0.0 copy-start.5
  61.8 3.9 %all-gather.4 = bf16[128,512]{1,0:T(8,128)(2,1)S(1)} all-gather(bf16[64,512]{1,0:T(8,128)(2,1)S(1)} %get-tuple-element.89), channel_id=6, replica_groups={{0,8},{16,24},{32,40},{48,56},{64,72},{80,88},{96,104},{112,120},{128,1..., dimensions={0}, use_global_device_ids=true | all-gather | bytes 196608 | tf_op jit(solution)/shard_map/all_gather | solution.py:144
  65.7 0.0 copy-done.12
  65.7 0.9 shard_map.62
  66.7 7.2 %all-gather.5 = bf16[128,512]{1,0:T(8,128)(2,1)S(1)} all-gather(bf16[64,512]{1,0:T(8,128)(2,1)S(1)} %get-tuple-element.94), channel_id=7, replica_groups={{8,16},{24,32},{40,48},{56,64},{72,80},{88,96},{104,112},{120,128},{136..., dimensions={0}, use_global_device_ids=true | all-gather | bytes 196608 | tf_op jit(solution)/shard_map/all_gather | solution.py:144
  73.9 0.0 copy-done.5
  73.9 0.7 shard_map.63
  74.6 4.1 %all-gather.6 = bf16[128,512]{1,0:T(8,128)(2,1)S(1)} all-gather(bf16[64,512]{1,0:T(8,128)(2,1)S(1)} %get-tuple-element.99), channel_id=8, replica_groups={{0,8},{16,24},{32,40},{48,56},{64,72},{80,88},{96,104},{112,120},{128,1..., dimensions={0}, use_global_device_ids=true | all-gather | bytes 196608 | tf_op jit(solution)/shard_map/all_gather | solution.py:144
  78.7 0.0 copy-done.14
  78.7 0.7 shard_map.64
  79.4 7.1 %all-gather.7 = bf16[128,512]{1,0:T(8,128)(2,1)S(1)} all-gather(bf16[64,512]{1,0:T(8,128)(2,1)S(1)} %get-tuple-element.104), channel_id=9, replica_groups={{8,16},{24,32},{40,48},{56,64},{72,80},{88,96},{104,112},{120,128},{136..., dimensions={0}, use_global_device_ids=true | all-gather | bytes 196608 | tf_op jit(solution)/shard_map/all_gather | solution.py:144
  86.6 0.2 shard_map.65.refs_1_
  86.8 0.3 shard_map.66
  87.1 4.1 %all-gather.8 = bf16[128,768]{1,0:T(8,128)(2,1)S(1)} all-gather(bf16[64,768]{1,0:T(8,128)(2,1)S(1)} %get-tuple-element.105), channel_id=10, replica_groups={{0,8},{16,24},{32,40},{48,56},{64,72},{80,88},{96,104},{112,120},{128,1..., dimensions={0}, use_global_device_ids=true | all-gather | bytes 294912 | tf_op jit(solution)/shard_map/all_gather | solution.py:144
  91.2 0.4 shard_map.67
  91.6 7.5 %all-gather.9 = bf16[128,768]{1,0:T(8,128)(2,1)S(1)} all-gather(bf16[64,768]{1,0:T(8,128)(2,1)S(1)} %get-tuple-element.108), channel_id=11, replica_groups={{8,16},{24,32},{40,48},{56,64},{72,80},{88,96},{104,112},{120,128},{136..., dimensions={0}, use_global_device_ids=true | all-gather | bytes 294912 | tf_op jit(solution)/shard_map/all_gather | solution.py:144
  99.1 0.4 shard_map.68
  99.5 4.1 %all-gather.10 = bf16[128,768]{1,0:T(8,128)(2,1)S(1)} all-gather(bf16[64,768]{1,0:T(8,128)(2,1)S(1)} %get-tuple-element.111), channel_id=12, replica_groups={{0,8},{16,24},{32,40},{48,56},{64,72},{80,88},{96,104},{112,120},{128,1..., dimensions={0}, use_global_device_ids=true | all-gather | bytes 294912 | tf_op jit(solution)/shard_map/all_gather | solution.py:144
  103.7 0.5 shard_map.69
  104.2 7.5 %all-gather.11 = bf16[128,768]{1,0:T(8,128)(2,1)S(1)} all-gather(bf16[64,768]{1,0:T(8,128)(2,1)S(1)} %get-tuple-element.114), channel_id=13, replica_groups={{8,16},{24,32},{40,48},{56,64},{72,80},{88,96},{104,112},{120,128},{136..., dimensions={0}, use_global_device_ids=true | all-gather | bytes 294912 | tf_op jit(solution)/shard_map/all_gather | solution.py:144
  111.6 0.6 shard_map.70
  112.2 4.1 %all-gather.12 = bf16[128,768]{1,0:T(8,128)(2,1)S(1)} all-gather(bf16[64,768]{1,0:T(8,128)(2,1)S(1)} %get-tuple-element.117), channel_id=14, replica_groups={{0,8},{16,24},{32,40},{48,56},{64,72},{80,88},{96,104},{112,120},{128,1..., dimensions={0}, use_global_device_ids=true | all-gather | bytes 294912 | tf_op jit(solution)/shard_map/all_gather | solution.py:144
  116.3 0.6 shard_map.71
  117.0 8.1 %all-gather.13 = bf16[128,768]{1,0:T(8,128)(2,1)S(1)} all-gather(bf16[64,768]{1,0:T(8,128)(2,1)S(1)} %get-tuple-element.120), channel_id=15, replica_groups={{8,16},{24,32},{40,48},{56,64},{72,80},{88,96},{104,112},{120,128},{136..., dimensions={0}, use_global_device_ids=true | all-gather | bytes 294912 | tf_op jit(solution)/shard_map/all_gather | solution.py:144
  125.1 0.2 shard_map.72
  125.3 3.8 %all-gather.14 = bf16[128,512]{1,0:T(8,128)(2,1)S(1)} all-gather(bf16[64,512]{1,0:T(8,128)(2,1)S(1)} %get-tuple-element.122), channel_id=16, replica_groups={{0,8},{16,24},{32,40},{48,56},{64,72},{80,88},{96,104},{112,120},{128,1..., dimensions={0}, use_global_device_ids=true | all-gather | bytes 196608 | tf_op jit(solution)/shard_map/all_gather | solution.py:144
  129.1 0.3 shard_map.73
  129.4 27.7 %all_to_all.10.r_ref = bf16[8,64,256]{2,1,0:T(8,128)(2,1)S(1)} all-to-all(bf16[8,64,256]{2,1,0:T(8,128)(2,1)S(1)} %shard_map.73), channel_id=1, replica_groups=mesh['sn'=64,'rhs'=8] {'rhs'}, dimensions={0} | all-to-all | bytes 524288 | tf_op jit(solution)/shard_map/all_to_all | solution.py:286
  157.1 1.1 shard_map.74
  (15 shorter events, 0.1 us)
Async XLA Ops:
  0.0 1.0 copy-start.15
  1.9 20.2 %all-to-all-start = ((bf16[8,64,256]{2,1,0:T(8,128)(2,1)}), bf16[8,64,256]{2,1,0:T(8,128)(2,1)S(1)}, u32[]{:S(2)}, u32[]{:S(2)}) async-start(bf16[8,64,256]{2,1,0:T(8,128)(2,1)} %shard_map.55), calls=%async_computation | async-start | bytes 524288 | tf_op jit(solution)/shard_map/all_to_all | solution.py:123
  13.5 20.6 %copy-start = (bf16[8,2,128,128]{3,2,1,0:T(8,128)(2,1)S(1)}, bf16[8,2,128,128]{3,2,1,0:T(8,128)(2,1)}, u32[]{:S(2)}) copy-start(bf16[8,2,128,128]{3,2,1,0:T(8,128)(2,1)} %d_ref.5) | copy-start | bytes 1572868
  22.1 25.2 %copy-start.1 = (bf16[1792,768]{1,0:T(8,128)(2,1)S(1)}, bf16[1792,768]{1,0:T(8,128)(2,1)}, u32[]{:S(2)}) copy-start(bf16[1792,768]{1,0:T(8,128)(2,1)} %get-tuple-element.75.refs_7_) | copy-start | bytes 8257540
  22.1 25.2 %copy-start.6 = (bf16[256,768]{1,0:T(8,128)(2,1)S(1)}, bf16[256,768]{1,0:T(8,128)(2,1)}, u32[]{:S(2)}) copy-start(bf16[256,768]{1,0:T(8,128)(2,1)} %get-tuple-element.74.refs_4_.refs_2_) | copy-start | bytes 1179652
  22.1 25.1 %collective-permute-start.1 = (bf16[3,256,256]{2,1,0:T(8,128)(2,1)}, bf16[3,256,256]{2,1,0:T(8,128)(2,1)S(1)}, u32[]{:S(2)}, u32[]{:S(2)}) collective-permute-start(bf16[3,256,256]{2,1,0:T(8,128)(2,1)} %get-tuple-element.79), channel_id=1, source_target_pairs={{0,8},{16,24},{32,40},{48,56},{64,72},{80,88},{96,104},{112,120},{... | collective-permute-start | bytes 1179656 | tf_op jit(solution)/shard_map/ppermute | solution.py:140
  24.3 22.9 %collective-permute-start = (bf16[4,256,256]{2,1,0:T(8,128)(2,1)}, bf16[4,256,256]{2,1,0:T(8,128)(2,1)S(1)}, u32[]{:S(2)}, u32[]{:S(2)}) collective-permute-start(bf16[4,256,256]{2,1,0:T(8,128)(2,1)} %get-tuple-element.73), channel_id=1, source_target_pairs={{8,16},{24,32},{40,48},{56,64},{72,80},{88,96},{104,112},{120,128}... | collective-permute-start | bytes 1572872 | tf_op jit(solution)/shard_map/ppermute | solution.py:140
  38.2 1.0 copy-start.8
  47.3 5.1 %copy-start.2 = (bf16[1536,768]{1,0:T(8,128)(2,1)S(1)}, bf16[1536,768]{1,0:T(8,128)(2,1)}, u32[]{:S(2)}) copy-start(bf16[1536,768]{1,0:T(8,128)(2,1)} %get-tuple-element.82.refs_7_) | copy-start | bytes 7077892
  47.3 5.1 %copy-start.7 = (bf16[256,768]{1,0:T(8,128)(2,1)S(1)}, bf16[256,768]{1,0:T(8,128)(2,1)}, u32[]{:S(2)}) copy-start(bf16[256,768]{1,0:T(8,128)(2,1)} %get-tuple-element.80.refs_4_.refs_2_) | copy-start | bytes 1179652
  48.5 12.4 %copy-start.3 = (bf16[1280,768]{1,0:T(8,128)(2,1)S(1)}, bf16[1280,768]{1,0:T(8,128)(2,1)}, u32[]{:S(2)}) copy-start(bf16[1280,768]{1,0:T(8,128)(2,1)} %get-tuple-element.87.refs_7_) | copy-start | bytes 5898244
  48.5 12.4 %copy-start.11 = (bf16[256,768]{1,0:T(8,128)(2,1)S(1)}, bf16[256,768]{1,0:T(8,128)(2,1)}, u32[]{:S(2)}) copy-start(bf16[256,768]{1,0:T(8,128)(2,1)} %get-tuple-element.85.refs_4_.refs_2_) | copy-start | bytes 1179652
  53.6 12.1 %copy-start.4 = (bf16[1024,768]{1,0:T(8,128)(2,1)S(1)}, bf16[1024,768]{1,0:T(8,128)(2,1)}, u32[]{:S(2)}) copy-start(bf16[1024,768]{1,0:T(8,128)(2,1)} %get-tuple-element.92.refs_7_) | copy-start | bytes 4718596
  53.6 12.1 %copy-start.12 = (bf16[256,768]{1,0:T(8,128)(2,1)S(1)}, bf16[256,768]{1,0:T(8,128)(2,1)}, u32[]{:S(2)}) copy-start(bf16[256,768]{1,0:T(8,128)(2,1)} %get-tuple-element.90.refs_4_.refs_2_) | copy-start | bytes 1179652
  61.8 12.1 %copy-start.5 = (bf16[768,768]{1,0:T(8,128)(2,1)S(1)}, bf16[768,768]{1,0:T(8,128)(2,1)}, u32[]{:S(2)}) copy-start(bf16[768,768]{1,0:T(8,128)(2,1)} %get-tuple-element.97.refs_7_) | copy-start | bytes 3538948
  61.8 12.1 %copy-start.13 = (bf16[256,768]{1,0:T(8,128)(2,1)S(1)}, bf16[256,768]{1,0:T(8,128)(2,1)}, u32[]{:S(2)}) copy-start(bf16[256,768]{1,0:T(8,128)(2,1)} %get-tuple-element.95.refs_4_.refs_2_) | copy-start | bytes 1179652
  66.7 12.1 %copy-start.10 = (bf16[256,768]{1,0:T(8,128)(2,1)S(1)}, bf16[256,768]{1,0:T(8,128)(2,1)}, u32[]{:S(2)}) copy-start(bf16[256,768]{1,0:T(8,128)(2,1)} %get-tuple-element.100.refs_4_.refs_2_) | copy-start | bytes 1179652
  66.7 12.1 %copy-start.14 = (bf16[512,768]{1,0:T(8,128)(2,1)S(1)}, bf16[512,768]{1,0:T(8,128)(2,1)}, u32[]{:S(2)}) copy-start(bf16[512,768]{1,0:T(8,128)(2,1)} %get-tuple-element.102.refs_7_.refs_5_) | copy-start | bytes 2359300
  116.3 8.7 %copy-start.9 = (bf16[256,768]{1,0:T(8,128)(2,1)S(1)}, bf16[256,768]{1,0:T(8,128)(2,1)}, u32[]{:S(2)}) copy-start(bf16[256,768]{1,0:T(8,128)(2,1)} %get-tuple-element.70.refs_2_) | copy-start | bytes 1179652

commit v5 on v4

--- a/solution.py
+++ b/solution.py
@@ -20,7 +20,7 @@
     return lax.dot_general(a, w, (((1,), (0,)), ((), ())), preferred_element_type=F32)
 
 
-def call(body, outs, args, scratch=(), flops=10**7, mib=12, specs=None, out_specs=None, size=None):
+def call(body, outs, args, scratch=(), flops=10**7, mib=12, specs=None, out_specs=None, size=None, aliases=None):
     specs = specs or [SMEM if a.dtype == jnp.int32 else VMEM for a in args]
     if size is None:
         size = sum(a.size * a.dtype.itemsize for a in args)
@@ -30,20 +30,21 @@
         in_specs=specs,
         out_specs=out_specs or [VMEM] * len(outs),
         scratch_shapes=list(scratch),
+        input_output_aliases=aliases or {},
         compiler_params=pltpu.CompilerParams(vmem_limit_bytes=mib * 2**20),
         cost_estimate=pl.CostEstimate(flops=flops, bytes_accessed=size, transcendentals=0),
     )(*args)
 
 
-def build_operators(tiles, diag, row_slot, col_slot, parity, side_of):
+def build_operators(tiles, diag, row_slot, col_slot, place, side_of):
     levels, owned, b, _ = diag.shape
     count = tiles.shape[1]
     tall = owned * b
     wide = 3 * tall
 
     def body(row_ref, col_ref, par_ref, t_ref, d_ref, *refs):
-        outs, (scratch, held, sems, in_sems) = refs[: 2 * levels], refs[2 * levels :]
-        s_out, b_out, sends = outs[: levels - 1], outs[levels - 1 : 2 * levels - 2], outs[-2:]
+        outs, (scratch, held, sems, in_sems) = refs[: 2 * levels - 1], refs[2 * levels - 1 :]
+        s_out, b_out, send = outs[: levels - 1], outs[levels - 1 : 2 * levels - 2], outs[-1]
         loads = [
             pltpu.make_async_copy(t_ref.at[l], held.at[l], in_sems.at[l]) for l in range(levels - 1)
         ]
@@ -72,17 +73,25 @@
                 b_out[l][rows, :] = dot_n(d_ref[l + 1, q], buf[rows, :]).astype(BF)
             s = side_of(par_ref, l + 1)
             toward = pl.ds(pl.multiple_of((1 - s) * 2 * tall, tall), tall)
-            sends[l % 2][l // 2] = b_out[l][:, toward]
+
+            @pl.when(par_ref[1] == (l + 1) % 2)
+            def _():
+                send[l // 2] = b_out[l][:, toward]
+
+        @pl.when(par_ref[1] == 0)
+        def _():
+            send[levels // 2 - 1] = jnp.zeros((tall, tall), BF)
+
         for c in copies:
             c.wait()
 
     outs = [(((levels - 1 - l) * tall, wide), BF) for l in range(levels - 1)]
     outs += [((tall, wide), BF)] * (levels - 1)
-    outs += [((levels // 2, tall, tall), BF), (((levels - 1) // 2, tall, tall), BF)]
+    outs += [((levels // 2, tall, tall), BF)]
     res = call(
         body,
         outs,
-        (row_slot, col_slot, parity, tiles, diag),
+        (row_slot, col_slot, place, tiles, diag),
         [
             pltpu.VMEM((levels * (levels - 1) // 2 * tall, wide), BF),
             pltpu.VMEM(tiles.shape, BF),
@@ -92,10 +101,10 @@
         flops=4 * 10**8,
         mib=60,
         specs=[SMEM, SMEM, SMEM, HBM, VMEM],
-        out_specs=[HBM] * (levels - 1) + [VMEM] * (levels + 1),
+        out_specs=[HBM] * (levels - 1) + [VMEM] * levels,
         size=24 * 2**20,
     )
-    return res[: levels - 1], res[levels - 1 : 2 * levels - 2], res[-2:]
+    return res[: levels - 1], res[levels - 1 : 2 * levels - 2], res[-1]
 
 
 def on_device(lanczos_block, diag_inv, factor_tiles, tile_rows, tile_cols):
@@ -108,19 +117,12 @@
     w = owned * b
     total, _, piece = lanczos_block.shape
     cols = total // peers
+    core = lax.axis_index("rhs") % 2
     parity = (own % 2).astype(jnp.int32).reshape(1)
+    place = jnp.stack([own % 2, core]).astype(jnp.int32)
 
     def side_of(par_ref, l):
         return par_ref[0] if l % 2 == 0 else 1 - par_ref[0]
-
-    def pack(x_ref, o_ref):
-        v = x_ref[...].T.astype(BF)
-        for j in range(peers):
-            o_ref[j] = v[j * cols : (j + 1) * cols]
-
-    flat = lanczos_block.transpose(1, 2, 0).reshape(levels * piece, total)
-    (sent,) = call(pack, [((peers, cols, levels * piece), BF)], (flat,))
-    arrived = lax.all_to_all(sent, "rhs", split_axis=0, concat_axis=0, tiled=True)
 
     my_rows = lax.dynamic_slice_in_dim(tile_rows, own * group_tiles, group_tiles, 1)
     my_cols = lax.dynamic_slice_in_dim(tile_cols, own * group_tiles, group_tiles, 1)
@@ -128,17 +130,26 @@
     group = (jnp.arange(group_tiles, dtype=jnp.int32) // (group_tiles // 3))[None, :]
     row_slot = (my_rows // per_level - above) * owned + my_rows % owned
     col_slot = group * owned + my_cols % owned
+    def pack(x_ref, o_ref):
+        v = x_ref[...].T.astype(BF)
+        for j in range(peers):
+            o_ref[j] = v[j * cols : (j + 1) * cols]
+
+    flat = lanczos_block.transpose(1, 2, 0).reshape(levels * piece, total)
+    (sent,) = call(pack, [((peers, cols, levels * piece), BF)], (flat,))
+    arrived = lax.all_to_all(sent, "rhs", split_axis=0, concat_axis=0, tiled=True)
+
     sent, factor_tiles = lax.optimization_barrier((sent, factor_tiles))
-    S, B, toward = build_operators(factor_tiles, diag_inv, row_slot, col_slot, parity, side_of)
+    S, B, toward = build_operators(factor_tiles, diag_inv, row_slot, col_slot, place, side_of)
 
     pairs = [
         [[i, i + 1] for i in range(0, n, 2)],
         [[i, (i + 1) % n] for i in range(1, n, 2)],
     ]
-    swaps = [[(p, q) for p, q in g] + [(q, p) for p, q in g] for g in pairs]
-    arrived, toward = lax.optimization_barrier((arrived, list(toward)))
-    far_odd, far_even = (lax.ppermute(toward[k], "sn", swaps[1 - k]) for k in range(2))
-    far = [None] + [(far_odd if l % 2 else far_even)[(l - 1) // 2] for l in range(1, levels)]
+    arrived, toward = lax.optimization_barrier((arrived, toward))
+    partner = [{p: q for g in pairs[k] for p, q in (g, g[::-1])} for k in range(2)]
+    fetch = [(i * peers + r, partner[r % 2][i] * peers + r) for i in range(n) for r in range(peers)]
+    fetched = lax.ppermute(toward, ("sn", "rhs"), fetch)
 
     def swap(l, message):
         return lax.all_gather(message, "sn", axis_index_groups=pairs[l % 2])
@@ -178,6 +189,11 @@
                 args += (S[l - 1], before)
                 if rest_levels:
                     outs.append(((cols, rest_levels * w), F32))
+        aliases, extra = {}, {}
+        if l == 0:
+            aliases, extra = {len(args): len(outs)}, {len(args): pl.BlockSpec(memory_space=pl.ANY)}
+            args += (fetched,)
+            outs.append((fetched.shape, BF))
         n_in = len(args)
 
         def step(*refs):
@@ -213,12 +229,19 @@
             if l and rest_levels:
                 refs[n_in + 2][...] = acc_ref[:, base + w :] - dot_t(y3[...], s_ref[2 * w :, :])
 
-        res = call(step, outs, args, [pltpu.VMEM((cols, 3 * w), BF)])
-        return res[0], res[1] if more else None, res[-1] if l else acc
+        specs = [extra.get(k, SMEM if a.dtype == jnp.int32 else VMEM) for k, a in enumerate(args)]
+        out_specs = [pl.BlockSpec(memory_space=pl.ANY) if k in aliases.values() else VMEM for k in range(len(outs))]
+        res = call(step, outs, args, [pltpu.VMEM((cols, 3 * w), BF)], specs=specs, out_specs=out_specs, aliases=aliases)
+        return res[0], res[1] if more else None, res[-1]
 
     pair_y = [None] * levels
     acc, message, before = x, y0, None
-    for l in range(levels):
+    before, message, fetched = forward_step(0, swap(0, message), before, acc)
+    other = lax.ppermute(fetched, "rhs", [(r, r ^ 1) for r in range(peers)])
+    far = [None] + [
+        jnp.where(core == l % 2, fetched[(l - 1) // 2], other[(l - 1) // 2]) for l in range(1, levels)
+    ]
+    for l in range(1, levels):
         before, message, acc = forward_step(l, swap(l, message), before, acc)
         pair_y[l] = before
 

time: 159 us -> 162 us (1.019)
  waiting for transfers between devices: 0.01 us -> 3.12 us
  blocking collectives: 112 us -> 110 us
  other arithmetic: 1.41 us -> 3.4 us
    ppermute x2, waiting for transfers between devices: 0.01 us -> 3.12 us  [the longest x1 3.11 us: on_device(): fetched = lax.ppermute(toward, ('sn', 'rhs'), fetch)]
  transfers between devices with their start and end apart: 3 -> 3, of which waited for: 0 -> 1; matrix products, arithmetic and copies ran while one was open for 1% -> 1% of each run, Pallas kernels for 6% -> 6%
where the time goes in v5:
time: 162 us; the launch traced here: 161 us
  blocking collectives  110 us (68%)
  starting transfers between devices  21.5 us (13%)
  Pallas kernels  20.1 us (12%)
  other arithmetic  3.4 us (2%)
  waiting for transfers between devices  3.12 us (2%)
  local copies, waits for them, and re-layouts  2.11 us (1%)
    all_gather x15, blocking collectives, swap(): return lax.all_gather(message, 'sn', axis_index_groups=pairs[l % 2])  83.3 us
    all_to_all x1, blocking collectives, on_device(): lax.all_to_all(result, 'rhs', split_axis=0, concat_axis=0, tiled=True)  27.1 us
    pallas_call x20, Pallas kernels, call(): pl.pallas_call(body, out_shape=[jax.ShapeDtypeStruct(s, d) for s, d in ou...  20.1 us
    all_to_all x1, starting transfers between devices, on_device(): lax.all_to_all(sent, 'rhs', split_axis=0, concat_axis=0, tiled=True)  10.2 us
    ppermute x1, starting transfers between devices, on_device(): fetched = lax.ppermute(toward, ('sn', 'rhs'), fetch)  9.35 us
  transfers between devices with their start and end apart: 3, of which 1 were waited for; matrix products, arithmetic and copies ran while one was open for 1% of the time, Pallas kernels for 6%

profile of v5, /device:TPU:1, one launch (start us, length us, event | category | flops | bytes accessed | tf_op | source)
XLA Modules:
  0.0 160.9 jit_solution(16389031324652755912)
XLA Ops:
  0.0 1.0 copy-done.17
  1.0 0.8 shard_map.55
  1.9 10.2 %all-to-all-start = ((bf16[8,64,256]{2,1,0:T(8,128)(2,1)}), bf16[8,64,256]{2,1,0:T(8,128)(2,1)S(1)}, u32[]{:S(2)}, u32[]{:S(2)}) async-start(bf16[8,64,256]{2,1,0:T(8,128)(2,1)} %shard_map.55), calls=%async_computation | async-start | bytes 524288 | tf_op jit(solution)/shard_map/all_to_all | solution.py:140
  12.1 0.7 pad_add_fusion.par_ref
  12.8 1.4 fusion.4
  14.2 8.6 %shard_map.56 = (bf16[1792,768]{1,0:T(8,128)(2,1)}, bf16[1536,768]{1,0:T(8,128)(2,1)}, bf16[1280,768]{1,0:T(8,128)(2,1)}, bf16[1024,768]{1,0:T(8,128)(2,1)}, bf1...) custom-call(s32[7,24]{1,0:T(8,128)} %get-tuple-element.130.row_ref, ...), custom_call_target="tpu_custom_call" | custom-call | flops 400000000 | bytes 25165824 | tf_op jit(solution)/shard_map/pallas_call | solution.py:27
  22.8 0.0 all-to-all-done.a_ref
  22.8 9.3 %collective-permute-start = (bf16[4,256,256]{2,1,0:T(8,128)(2,1)}, bf16[4,256,256]{2,1,0:T(8,128)(2,1)}, u32[]{:S(2)}, u32[]{:S(2)}) collective-permute-start(bf16[4,256,256]{2,1,0:T(8,128)(2,1)} %get-tuple-element.70), channel_id=1, source_target_pairs={{0,8},{1,505},{2,10},{3,507},{4,12},{5,509},{6,14},{7,511},{8,0},{... | collective-permute-start | bytes 1572872 | tf_op jit(solution)/shard_map/ppermute | solution.py:152
  32.2 0.3 shard_map.57
  32.5 0.0 copy-start.18
  32.5 3.4 %all-gather = bf16[128,256]{1,0:T(8,128)(2,1)S(1)} all-gather(bf16[64,256]{1,0:T(8,128)(2,1)S(1)} %get-tuple-element.67.y_ref), channel_id=2, replica_groups={{0,8},{16,24},{32,40},{48,56},{64,72},{80,88},{96,104},{112,120},{128,1..., dimensions={0}, use_global_device_ids=true | all-gather | bytes 98304 | tf_op jit(solution)/shard_map/all_gather | solution.py:155
  35.9 3.1 %collective-permute-done.refs_5_ = bf16[4,256,256]{2,1,0:T(8,128)(2,1)} collective-permute-done((bf16[4,256,256]{2,1,0:T(8,128)(2,1)}, bf16[4,256,256]{2,1,0:T(8,128)(2,1)}, u32[]{:S(2)}, u32[]{:S(2)}) %collective-permute-start) | collective-permute-done | bytes 524320 | tf_op jit(solution)/shard_map/ppermute | solution.py:152
  39.0 1.0 copy-done.8
  40.0 0.2 shard_map.58
  40.3 0.0 copy-done.15
  40.3 0.0 copy-done.18
  40.3 1.9 %collective-permute-start.1 = (bf16[4,256,256]{2,1,0:T(8,128)(2,1)}, bf16[4,256,256]{2,1,0:T(8,128)(2,1)}, u32[]{:S(2)}, u32[]{:S(2)}) collective-permute-start(bf16[4,256,256]{2,1,0:T(8,128)(2,1)} %get-tuple-element.72), channel_id=1, source_target_pairs={{0,1},{1,0},{2,3},{3,2},{4,5},{5,4},{6,7},{7,6},{8,9},{9,8},{10,11... | collective-permute-start | bytes 1572872 | tf_op jit(solution)/shard_map/ppermute | solution.py:240
  42.2 0.0 copy-start.6
  42.2 0.0 copy-start.9
  42.3 0.0 copy-start.16
  42.3 7.2 %all-gather.1 = bf16[128,512]{1,0:T(8,128)(2,1)S(1)} all-gather(bf16[64,512]{1,0:T(8,128)(2,1)S(1)} %get-tuple-element.71), channel_id=3, replica_groups={{8,16},{24,32},{40,48},{56,64},{72,80},{88,96},{104,112},{120,128},{136..., dimensions={0}, use_global_device_ids=true | all-gather | bytes 196608 | tf_op jit(solution)/shard_map/all_gather | solution.py:155
  49.5 0.0 collective-permute-done.1
  49.5 1.4 fusion
  50.9 0.0 copy-done.1
  50.9 0.0 copy-done.6
  50.9 0.0 copy-done.9
  50.9 0.0 copy-done.16
  50.9 0.0 copy-start.2
  50.9 0.0 copy-start.7
  50.9 1.1 shard_map.59
  52.1 0.0 copy-start.3
  52.1 0.0 copy-start.11
  52.1 3.9 %all-gather.2 = bf16[128,512]{1,0:T(8,128)(2,1)S(1)} all-gather(bf16[64,512]{1,0:T(8,128)(2,1)S(1)} %get-tuple-element.77), channel_id=4, replica_groups={{0,8},{16,24},{32,40},{48,56},{64,72},{80,88},{96,104},{112,120},{128,1..., dimensions={0}, use_global_device_ids=true | all-gather | bytes 196608 | tf_op jit(solution)/shard_map/all_gather | solution.py:155
  56.0 0.0 copy-done.2
  56.0 1.1 shard_map.60
  57.2 7.2 %all-gather.3 = bf16[128,512]{1,0:T(8,128)(2,1)S(1)} all-gather(bf16[64,512]{1,0:T(8,128)(2,1)S(1)} %get-tuple-element.82), channel_id=5, replica_groups={{8,16},{24,32},{40,48},{56,64},{72,80},{88,96},{104,112},{120,128},{136..., dimensions={0}, use_global_device_ids=true | all-gather | bytes 196608 | tf_op jit(solution)/shard_map/all_gather | solution.py:155
  64.4 0.0 copy-done.3
  64.4 0.9 shard_map.61
  65.3 0.0 copy-start.5
  65.3 3.9 %all-gather.4 = bf16[128,512]{1,0:T(8,128)(2,1)S(1)} all-gather(bf16[64,512]{1,0:T(8,128)(2,1)S(1)} %get-tuple-element.87), channel_id=6, replica_groups={{0,8},{16,24},{32,40},{48,56},{64,72},{80,88},{96,104},{112,120},{128,1..., dimensions={0}, use_global_device_ids=true | all-gather | bytes 196608 | tf_op jit(solution)/shard_map/all_gather | solution.py:155
  69.3 0.9 shard_map.62
  70.2 7.2 %all-gather.5 = bf16[128,512]{1,0:T(8,128)(2,1)S(1)} all-gather(bf16[64,512]{1,0:T(8,128)(2,1)S(1)} %get-tuple-element.92), channel_id=7, replica_groups={{8,16},{24,32},{40,48},{56,64},{72,80},{88,96},{104,112},{120,128},{136..., dimensions={0}, use_global_device_ids=true | all-gather | bytes 196608 | tf_op jit(solution)/shard_map/all_gather | solution.py:155
  77.5 0.7 shard_map.63
  78.2 4.1 %all-gather.6 = bf16[128,512]{1,0:T(8,128)(2,1)S(1)} all-gather(bf16[64,512]{1,0:T(8,128)(2,1)S(1)} %get-tuple-element.97), channel_id=8, replica_groups={{0,8},{16,24},{32,40},{48,56},{64,72},{80,88},{96,104},{112,120},{128,1..., dimensions={0}, use_global_device_ids=true | all-gather | bytes 196608 | tf_op jit(solution)/shard_map/all_gather | solution.py:155
  82.3 0.7 shard_map.64
  83.0 7.1 %all-gather.7 = bf16[128,512]{1,0:T(8,128)(2,1)S(1)} all-gather(bf16[64,512]{1,0:T(8,128)(2,1)S(1)} %get-tuple-element.102), channel_id=9, replica_groups={{8,16},{24,32},{40,48},{56,64},{72,80},{88,96},{104,112},{120,128},{136..., dimensions={0}, use_global_device_ids=true | all-gather | bytes 196608 | tf_op jit(solution)/shard_map/all_gather | solution.py:155
  90.1 0.2 shard_map.65.refs_1_
  90.3 0.3 shard_map.66
  90.6 4.1 %all-gather.8 = bf16[128,768]{1,0:T(8,128)(2,1)S(1)} all-gather(bf16[64,768]{1,0:T(8,128)(2,1)S(1)} %get-tuple-element.103), channel_id=10, replica_groups={{0,8},{16,24},{32,40},{48,56},{64,72},{80,88},{96,104},{112,120},{128,1..., dimensions={0}, use_global_device_ids=true | all-gather | bytes 294912 | tf_op jit(solution)/shard_map/all_gather | solution.py:155
  94.8 0.4 shard_map.67
  95.1 7.5 %all-gather.9 = bf16[128,768]{1,0:T(8,128)(2,1)S(1)} all-gather(bf16[64,768]{1,0:T(8,128)(2,1)S(1)} %get-tuple-element.106), channel_id=11, replica_groups={{8,16},{24,32},{40,48},{56,64},{72,80},{88,96},{104,112},{120,128},{136..., dimensions={0}, use_global_device_ids=true | all-gather | bytes 294912 | tf_op jit(solution)/shard_map/all_gather | solution.py:155
  102.6 0.4 shard_map.68
  103.0 4.1 %all-gather.10 = bf16[128,768]{1,0:T(8,128)(2,1)S(1)} all-gather(bf16[64,768]{1,0:T(8,128)(2,1)S(1)} %get-tuple-element.109), channel_id=12, replica_groups={{0,8},{16,24},{32,40},{48,56},{64,72},{80,88},{96,104},{112,120},{128,1..., dimensions={0}, use_global_device_ids=true | all-gather | bytes 294912 | tf_op jit(solution)/shard_map/all_gather | solution.py:155
  107.2 0.5 shard_map.69
  107.7 7.5 %all-gather.11 = bf16[128,768]{1,0:T(8,128)(2,1)S(1)} all-gather(bf16[64,768]{1,0:T(8,128)(2,1)S(1)} %get-tuple-element.112), channel_id=13, replica_groups={{8,16},{24,32},{40,48},{56,64},{72,80},{88,96},{104,112},{120,128},{136..., dimensions={0}, use_global_device_ids=true | all-gather | bytes 294912 | tf_op jit(solution)/shard_map/all_gather | solution.py:155
  115.1 0.6 shard_map.70
  115.7 4.1 %all-gather.12 = bf16[128,768]{1,0:T(8,128)(2,1)S(1)} all-gather(bf16[64,768]{1,0:T(8,128)(2,1)S(1)} %get-tuple-element.115), channel_id=14, replica_groups={{0,8},{16,24},{32,40},{48,56},{64,72},{80,88},{96,104},{112,120},{128,1..., dimensions={0}, use_global_device_ids=true | all-gather | bytes 294912 | tf_op jit(solution)/shard_map/all_gather | solution.py:155
  119.9 0.6 shard_map.71
  120.5 7.9 %all-gather.13 = bf16[128,768]{1,0:T(8,128)(2,1)S(1)} all-gather(bf16[64,768]{1,0:T(8,128)(2,1)S(1)} %get-tuple-element.118), channel_id=15, replica_groups={{8,16},{24,32},{40,48},{56,64},{72,80},{88,96},{104,112},{120,128},{136..., dimensions={0}, use_global_device_ids=true | all-gather | bytes 294912 | tf_op jit(solution)/shard_map/all_gather | solution.py:155
  128.4 0.2 shard_map.72
  128.6 3.8 %all-gather.14 = bf16[128,512]{1,0:T(8,128)(2,1)S(1)} all-gather(bf16[64,512]{1,0:T(8,128)(2,1)S(1)} %get-tuple-element.120), channel_id=16, replica_groups={{0,8},{16,24},{32,40},{48,56},{64,72},{80,88},{96,104},{112,120},{128,1..., dimensions={0}, use_global_device_ids=true | all-gather | bytes 196608 | tf_op jit(solution)/shard_map/all_gather | solution.py:155
  132.4 0.3 shard_map.73
  132.7 27.1 %all_to_all.10.r_ref = bf16[8,64,256]{2,1,0:T(8,128)(2,1)S(1)} all-to-all(bf16[8,64,256]{2,1,0:T(8,128)(2,1)S(1)} %shard_map.73), channel_id=1, replica_groups=mesh['sn'=64,'rhs'=8] {'rhs'}, dimensions={0} | all-to-all | bytes 524288 | tf_op jit(solution)/shard_map/all_to_all | solution.py:309
  159.8 1.1 shard_map.74
  (23 shorter events, 0.0 us)
Async XLA Ops:
  0.0 1.0 copy-start.17
  1.9 20.9 %all-to-all-start = ((bf16[8,64,256]{2,1,0:T(8,128)(2,1)}), bf16[8,64,256]{2,1,0:T(8,128)(2,1)S(1)}, u32[]{:S(2)}, u32[]{:S(2)}) async-start(bf16[8,64,256]{2,1,0:T(8,128)(2,1)} %shard_map.55), calls=%async_computation | async-start | bytes 524288 | tf_op jit(solution)/shard_map/all_to_all | solution.py:140
  14.1 18.0 %copy-start = (bf16[8,2,128,128]{3,2,1,0:T(8,128)(2,1)S(1)}, bf16[8,2,128,128]{3,2,1,0:T(8,128)(2,1)}, u32[]{:S(2)}) copy-start(bf16[8,2,128,128]{3,2,1,0:T(8,128)(2,1)} %d_ref.5) | copy-start | bytes 1572868
  22.8 28.1 %copy-start.1 = (bf16[1792,768]{1,0:T(8,128)(2,1)S(1)}, bf16[1792,768]{1,0:T(8,128)(2,1)}, u32[]{:S(2)}) copy-start(bf16[1792,768]{1,0:T(8,128)(2,1)} %get-tuple-element.74.refs_7_) | copy-start | bytes 8257540
  22.8 16.2 %collective-permute-start = (bf16[4,256,256]{2,1,0:T(8,128)(2,1)}, bf16[4,256,256]{2,1,0:T(8,128)(2,1)}, u32[]{:S(2)}, u32[]{:S(2)}) collective-permute-start(bf16[4,256,256]{2,1,0:T(8,128)(2,1)} %get-tuple-element.70), channel_id=1, source_target_pairs={{0,8},{1,505},{2,10},{3,507},{4,12},{5,509},{6,14},{7,511},{8,0},{... | collective-permute-start | bytes 1572872 | tf_op jit(solution)/shard_map/ppermute | solution.py:152
  32.5 7.8 %copy-start.15 = (f32[64,2048]{1,0:T(8,128)}, f32[64,2048]{1,0:T(8,128)S(1)}, u32[]{:S(2)}) copy-start(f32[64,2048]{1,0:T(8,128)S(1)} %get-tuple-element.69.refs_4_.refs_6_) | copy-start | bytes 1572868
  32.5 7.8 %copy-start.18 = (bf16[64,256]{1,0:T(8,128)(2,1)}, bf16[64,256]{1,0:T(8,128)(2,1)S(1)}, u32[]{:S(2)}) copy-start(bf16[64,256]{1,0:T(8,128)(2,1)S(1)} %get-tuple-element.67.y_ref) | copy-start | bytes 98308
  39.0 1.0 copy-start.8
  40.3 9.2 %collective-permute-start.1 = (bf16[4,256,256]{2,1,0:T(8,128)(2,1)}, bf16[4,256,256]{2,1,0:T(8,128)(2,1)}, u32[]{:S(2)}, u32[]{:S(2)}) collective-permute-start(bf16[4,256,256]{2,1,0:T(8,128)(2,1)} %get-tuple-element.72), channel_id=1, source_target_pairs={{0,1},{1,0},{2,3},{3,2},{4,5},{5,4},{6,7},{7,6},{8,9},{9,8},{10,11... | collective-permute-start | bytes 1572872 | tf_op jit(solution)/shard_map/ppermute | solution.py:240
  42.2 8.6 %copy-start.6 = (bf16[256,768]{1,0:T(8,128)(2,1)S(1)}, bf16[256,768]{1,0:T(8,128)(2,1)}, u32[]{:S(2)}) copy-start(bf16[256,768]{1,0:T(8,128)(2,1)} %get-tuple-element.73.refs_4_.refs_2_) | copy-start | bytes 1179652
  42.2 8.6 %copy-start.9 = (bf16[256,768]{1,0:T(8,128)(2,1)S(1)}, bf16[256,768]{1,0:T(8,128)(2,1)}, u32[]{:S(2)}) copy-start(bf16[256,768]{1,0:T(8,128)(2,1)} %get-tuple-element.68.refs_2_) | copy-start | bytes 1179652
  42.3 8.6 %copy-start.16 = (f32[64,2048]{1,0:T(8,128)S(1)}, f32[64,2048]{1,0:T(8,128)}, u32[]{:S(2)}) copy-start(f32[64,2048]{1,0:T(8,128)} %copy-done.15) | copy-start | bytes 1572868
  50.9 5.1 %copy-start.2 = (bf16[1536,768]{1,0:T(8,128)(2,1)S(1)}, bf16[1536,768]{1,0:T(8,128)(2,1)}, u32[]{:S(2)}) copy-start(bf16[1536,768]{1,0:T(8,128)(2,1)} %get-tuple-element.80.refs_7_) | copy-start | bytes 7077892
  50.9 5.1 %copy-start.7 = (bf16[256,768]{1,0:T(8,128)(2,1)S(1)}, bf16[256,768]{1,0:T(8,128)(2,1)}, u32[]{:S(2)}) copy-start(bf16[256,768]{1,0:T(8,128)(2,1)} %get-tuple-element.78.refs_4_.refs_2_) | copy-start | bytes 1179652
  52.1 12.4 %copy-start.3 = (bf16[1280,768]{1,0:T(8,128)(2,1)S(1)}, bf16[1280,768]{1,0:T(8,128)(2,1)}, u32[]{:S(2)}) copy-start(bf16[1280,768]{1,0:T(8,128)(2,1)} %get-tuple-element.85.refs_7_) | copy-start | bytes 5898244
  52.1 12.4 %copy-start.11 = (bf16[256,768]{1,0:T(8,128)(2,1)S(1)}, bf16[256,768]{1,0:T(8,128)(2,1)}, u32[]{:S(2)}) copy-start(bf16[256,768]{1,0:T(8,128)(2,1)} %get-tuple-element.83.refs_4_.refs_2_) | copy-start | bytes 1179652
  57.1 12.1 %copy-start.4 = (bf16[1024,768]{1,0:T(8,128)(2,1)S(1)}, bf16[1024,768]{1,0:T(8,128)(2,1)}, u32[]{:S(2)}) copy-start(bf16[1024,768]{1,0:T(8,128)(2,1)} %get-tuple-element.90.refs_7_) | copy-start | bytes 4718596
  57.2 12.1 %copy-start.12 = (bf16[256,768]{1,0:T(8,128)(2,1)S(1)}, bf16[256,768]{1,0:T(8,128)(2,1)}, u32[]{:S(2)}) copy-start(bf16[256,768]{1,0:T(8,128)(2,1)} %get-tuple-element.88.refs_4_.refs_2_) | copy-start | bytes 1179652
  65.3 12.1 %copy-start.5 = (bf16[768,768]{1,0:T(8,128)(2,1)S(1)}, bf16[768,768]{1,0:T(8,128)(2,1)}, u32[]{:S(2)}) copy-start(bf16[768,768]{1,0:T(8,128)(2,1)} %get-tuple-element.95.refs_7_) | copy-start | bytes 3538948
  65.3 12.1 %copy-start.13 = (bf16[256,768]{1,0:T(8,128)(2,1)S(1)}, bf16[256,768]{1,0:T(8,128)(2,1)}, u32[]{:S(2)}) copy-start(bf16[256,768]{1,0:T(8,128)(2,1)} %get-tuple-element.93.refs_4_.refs_2_) | copy-start | bytes 1179652
  70.2 12.1 %copy-start.10 = (bf16[256,768]{1,0:T(8,128)(2,1)S(1)}, bf16[256,768]{1,0:T(8,128)(2,1)}, u32[]{:S(2)}) copy-start(bf16[256,768]{1,0:T(8,128)(2,1)} %get-tuple-element.98.refs_4_.refs_2_) | copy-start | bytes 1179652
  70.2 12.1 %copy-start.14 = (bf16[512,768]{1,0:T(8,128)(2,1)S(1)}, bf16[512,768]{1,0:T(8,128)(2,1)}, u32[]{:S(2)}) copy-start(bf16[512,768]{1,0:T(8,128)(2,1)} %get-tuple-element.100.refs_7_.refs_5_) | copy-start | bytes 2359300
  119.9 12.5 %copy-start.19 = (bf16[64,256]{1,0:T(8,128)(2,1)S(1)}, bf16[64,256]{1,0:T(8,128)(2,1)}, u32[]{:S(2)}) copy-start(bf16[64,256]{1,0:T(8,128)(2,1)} %copy-done.18) | copy-start | bytes 98308

commit v6 on v4

--- a/solution.py
+++ b/solution.py
@@ -222,67 +222,65 @@
         before, message, acc = forward_step(l, swap(l, message), before, acc)
         pair_y[l] = before
 
-    def backward_step(l, got, older, above):
+    def backward_step(l, got, cot, older, above):
         top, more = l == levels - 1, l >= 2
-        args = (parity, pair_y[l], B[l - 1], far[l], diag_inv)
-        if not top:
-            args += (got, older)
+        args = (parity, pair_y[l - 1], B[l - 1], far[l], diag_inv)
+        args += (pair_y[l],) if top else (got, cot, older)
         if more:
-            args += (S[l - 2], *above)
+            args += (B[l - 2], S[l - 2], *above)
         n_in = len(args)
-        outs = [((cols, 3 * w if more else 2 * w), BF), ((cols, w), BF)]
+        outs = [((cols, 2 * w if more else w), BF), ((cols, w), BF), ((cols, w), F32)]
         if more:
             outs.append(((cols, 3 * w), F32))
 
         def step(*refs):
             par_ref, y_ref, near_ref, far_ref, d_ref = refs[:5]
-            m_ref, z_ref = refs[n_in : n_in + 2]
-            e_ref = refs[-1]
+            m_ref, z_ref, cot_ref = refs[n_in : n_in + 3]
             s = side_of(par_ref, l)
-            e = y_ref[...]
+            if top:
+                q = refs[5][:, at(s * w, w)]
+                down = -dot_n(refs[5][:, at((1 - s) * w, w)], far_ref[...])
+            else:
+                g_ref, own_ref, old_ref = refs[5:8]
+                q = (own_ref[...] + g_ref[1 - s, :, :w].astype(F32)).astype(BF)
+                down = g_ref[1 - s, :, w:].astype(F32) - dot_n(g_ref[s, :, :w], far_ref[...])
+            z_own = diag_bwd(d_ref, l, q)
+            z_ref[...] = z_own
+            pair = -dot_n(q, near_ref[:, at(s * w, 2 * w)])
             if not top:
-                g_ref, old_ref = refs[5:7]
-                e = e.astype(F32) - g_ref[0, :, : 2 * w].astype(F32) - g_ref[1, :, : 2 * w].astype(F32)
-            e_ref[...] = e.astype(BF)
-            e_own, e_par = e_ref[:, at(s * w, w)], e_ref[:, at((1 - s) * w, w)]
-            z_own = diag_bwd(d_ref, l, e_own)
-            z_ref[...] = z_own
-            part = dot_n(e_own, near_ref[:, at(s * w, 2 * w)])
-            extra = dot_n(e_par, far_ref[...])
-            if not top:
-                part = part + old_ref[:, at(s * w, 2 * w)]
-                extra = extra + g_ref[1 - s, :, 2 * w :].astype(F32)
-            for k in range(2):
-                half = part[:, k * w : (k + 1) * w]
-                m_ref[:, k * w : (k + 1) * w] = jnp.where(s == 1 - k, half + extra, half).astype(BF)
+                pair = pair - old_ref[:, at(s * w, 2 * w)]
+            left, right = pair[:, :w], pair[:, w:]
+            mine = jnp.where(s == 1, left, right) + down + y_ref[:, at((1 - s) * w, w)].astype(F32)
+            cot_ref[...] = mine
+            m_ref[:, :w] = jnp.where(s == 1, right, left).astype(BF)
             if more:
-                s_ref, old_out = refs[n_in - 1 - len(above)], refs[n_in + 2]
+                k = 6 if top else 8
+                next_ref, s_ref, zs, old_out = refs[k], refs[k + 1], refs[k + 2 : n_in], refs[n_in + 3]
                 sums = dot_n(z_own, s_ref[w : 2 * w, :])
-                for k, zr in enumerate(refs[n_in - len(above) : n_in]):
-                    sums = sums + dot_n(zr[...], s_ref[(k + 2) * w : (k + 3) * w, :])
+                for i, zr in enumerate(zs):
+                    sums = sums + dot_n(zr[...], s_ref[(i + 2) * w : (i + 3) * w, :])
                 old_out[...] = sums
-                m_ref[:, 2 * w :] = old_out[:, at(s * 2 * w, w)].astype(BF)
-
-        res = call(step, outs, args, [pltpu.VMEM((cols, 2 * w), BF)])
-        return res[0], res[1], res[2] if more else None
+                toward = at(s * 2 * w, w)
+                m_ref[:, w:] = (-dot_n(mine.astype(BF), next_ref[:, toward]) - old_out[:, toward]).astype(BF)
+
+        res = call(step, outs, args)
+        return res[0], res[1], res[2], res[3] if more else None
 
     z = [None] * levels
-    got, older = None, None
+    got, cot, older = None, None, None
     for l in range(levels - 1, 0, -1):
-        message, z[l], older = backward_step(l, got, older, z[l + 1 :])
+        message, z[l], cot, older = backward_step(l, got, cot, older, z[l + 1 :])
         got = swap(l - 1, message)
 
     def finish(par_ref, g_ref, y_ref, d_ref, *rest):
         o_ref = rest[-1]
-        here = at(par_ref[0] * w, w)
-        terms = g_ref[0, :, here].astype(F32) + g_ref[1, :, here].astype(F32)
-        e = (y_ref[...].astype(F32) - terms).astype(BF)
+        e = (y_ref[...] + g_ref[1 - par_ref[0]].astype(F32)).astype(BF)
         values = [diag_bwd(d_ref, 0, e).astype(F32)] + [r[...].astype(F32) for r in rest[:-1]]
         for j in range(peers):
             parts = [v[:, j * piece : (j + 1) * piece] for v in values]
             o_ref[j] = jnp.concatenate(parts, axis=1).astype(BF)
 
-    (result,) = call(finish, [((peers, cols, levels * piece), BF)], (parity, got, y0, diag_inv, *z[1:]))
+    (result,) = call(finish, [((peers, cols, levels * piece), BF)], (parity, got, cot, diag_inv, *z[1:]))
     result = lax.all_to_all(result, "rhs", split_axis=0, concat_axis=0, tiled=True)
 
     def turn(r_ref, o_ref):

time: 159 us -> 156 us (0.981)
  blocking collectives: 112 us -> 109 us
    all_gather x15, blocking collectives: 84.3 us -> 82.2 us  [swap(): return lax.all_gather(message, 'sn', axis_index_groups=pairs[l % 2])]
where the time goes in v6:
time: 156 us
  blocking collectives  109 us (70%)
  starting transfers between devices  22.2 us (14%)
  Pallas kernels  20.2 us (13%)
  local copies, waits for them, and re-layouts  2.16 us (1%)
    all_gather x15, blocking collectives, swap(): return lax.all_gather(message, 'sn', axis_index_groups=pairs[l % 2])  82.2 us
    all_to_all x1, blocking collectives, on_device(): lax.all_to_all(result, 'rhs', split_axis=0, concat_axis=0, tiled=True)  27.1 us
    pallas_call x20, Pallas kernels, call(): pl.pallas_call(body, out_shape=[jax.ShapeDtypeStruct(s, d) for s, d in ou...  20.2 us
    ppermute x2, starting transfers between devices, on_device(): lax.ppermute(toward[k], 'sn', swaps[1 - k])  12 us
    all_to_all x1, starting transfers between devices, on_device(): lax.all_to_all(sent, 'rhs', split_axis=0, concat_axis=0, tiled=True)  10.2 us
  transfers between devices with their start and end apart: 3, of which 0 were waited for; matrix products, arithmetic and copies ran while one was open for 1% of the time, Pallas kernels for 6%

profile of v6, /device:TPU:1, one launch (start us, length us, event | category | flops | bytes accessed | tf_op | source)
XLA Modules:
  0.0 155.6 jit_solution(12864532947987815086)
XLA Ops:
  0.0 1.0 copy-done.15
  1.0 0.8 shard_map.55
  1.9 10.2 %all-to-all-start = ((bf16[8,64,256]{2,1,0:T(8,128)(2,1)}), bf16[8,64,256]{2,1,0:T(8,128)(2,1)S(1)}, u32[]{:S(2)}, u32[]{:S(2)}) async-start(bf16[8,64,256]{2,1,0:T(8,128)(2,1)} %shard_map.55), calls=%async_computation | async-start | bytes 524288 | tf_op jit(solution)/shard_map/all_to_all | solution.py:123
  12.1 1.4 fusion.3
  13.5 8.6 %shard_map.56 = (bf16[1792,768]{1,0:T(8,128)(2,1)}, bf16[1536,768]{1,0:T(8,128)(2,1)}, bf16[1280,768]{1,0:T(8,128)(2,1)}, bf16[1024,768]{1,0:T(8,128)(2,1)}, bf1...) custom-call(s32[7,24]{1,0:T(8,128)} %get-tuple-element.146.row_ref, ...), custom_call_target="tpu_custom_call" | custom-call | flops 400000000 | bytes 25165824 | tf_op jit(solution)/shard_map/pallas_call | solution.py:27
  22.1 0.0 copy-start.1
  22.1 0.0 all-to-all-done.a_ref
  22.1 0.0 copy-start.4
  22.1 2.2 %collective-permute-start.1 = (bf16[3,256,256]{2,1,0:T(8,128)(2,1)}, bf16[3,256,256]{2,1,0:T(8,128)(2,1)S(1)}, u32[]{:S(2)}, u32[]{:S(2)}) collective-permute-start(bf16[3,256,256]{2,1,0:T(8,128)(2,1)} %get-tuple-element.85), channel_id=1, source_target_pairs={{0,8},{16,24},{32,40},{48,56},{64,72},{80,88},{96,104},{112,120},{... | collective-permute-start | bytes 1179656 | tf_op jit(solution)/shard_map/ppermute | solution.py:140
  24.3 9.8 %collective-permute-start = (bf16[4,256,256]{2,1,0:T(8,128)(2,1)}, bf16[4,256,256]{2,1,0:T(8,128)(2,1)S(1)}, u32[]{:S(2)}, u32[]{:S(2)}) collective-permute-start(bf16[4,256,256]{2,1,0:T(8,128)(2,1)} %get-tuple-element.80), channel_id=1, source_target_pairs={{8,16},{24,32},{40,48},{56,64},{72,80},{88,96},{104,112},{120,128}... | collective-permute-start | bytes 1572872 | tf_op jit(solution)/shard_map/ppermute | solution.py:140
  34.1 0.0 copy-done
  34.1 0.3 shard_map.57
  34.4 3.7 %all-gather = bf16[128,256]{1,0:T(8,128)(2,1)S(1)} all-gather(bf16[64,256]{1,0:T(8,128)(2,1)S(1)} %get-tuple-element.76), channel_id=2, replica_groups={{0,8},{16,24},{32,40},{48,56},{64,72},{80,88},{96,104},{112,120},{128,1..., dimensions={0}, use_global_device_ids=true | all-gather | bytes 98304 | tf_op jit(solution)/shard_map/all_gather | solution.py:144
  38.2 1.0 copy-done.6
  39.2 0.3 shard_map.58
  39.4 7.8 %all-gather.1 = bf16[128,512]{1,0:T(8,128)(2,1)S(1)} all-gather(bf16[64,512]{1,0:T(8,128)(2,1)S(1)} %get-tuple-element.81), channel_id=3, replica_groups={{8,16},{24,32},{40,48},{56,64},{72,80},{88,96},{104,112},{120,128},{136..., dimensions={0}, use_global_device_ids=true | all-gather | bytes 196608 | tf_op jit(solution)/shard_map/all_gather | solution.py:144
  47.2 0.0 collective-permute-done.1
  47.3 0.0 collective-permute-done
  47.3 0.0 copy-done.1
  47.3 0.0 copy-done.4
  47.3 0.0 copy-start.2
  47.3 0.0 copy-start.5
  47.3 1.1 shard_map.59
  48.5 0.0 copy-start.3
  48.5 0.0 copy-start.10
  48.5 3.9 %all-gather.2 = bf16[128,512]{1,0:T(8,128)(2,1)S(1)} all-gather(bf16[64,512]{1,0:T(8,128)(2,1)S(1)} %get-tuple-element.86), channel_id=4, replica_groups={{0,8},{16,24},{32,40},{48,56},{64,72},{80,88},{96,104},{112,120},{128,1..., dimensions={0}, use_global_device_ids=true | all-gather | bytes 196608 | tf_op jit(solution)/shard_map/all_gather | solution.py:144
  52.4 0.0 copy-done.2
  52.4 0.0 copy-done.5
  52.4 1.1 shard_map.60
  53.6 0.0 copy-start.9
  53.6 0.0 copy-start.11
  53.6 7.3 %all-gather.3 = bf16[128,512]{1,0:T(8,128)(2,1)S(1)} all-gather(bf16[64,512]{1,0:T(8,128)(2,1)S(1)} %get-tuple-element.91), channel_id=5, replica_groups={{8,16},{24,32},{40,48},{56,64},{72,80},{88,96},{104,112},{120,128},{136..., dimensions={0}, use_global_device_ids=true | all-gather | bytes 196608 | tf_op jit(solution)/shard_map/all_gather | solution.py:144
  60.9 0.0 copy-done.3
  60.9 0.9 shard_map.61
  61.8 0.0 copy-start.8
  61.8 3.9 %all-gather.4 = bf16[128,512]{1,0:T(8,128)(2,1)S(1)} all-gather(bf16[64,512]{1,0:T(8,128)(2,1)S(1)} %get-tuple-element.96), channel_id=6, replica_groups={{0,8},{16,24},{32,40},{48,56},{64,72},{80,88},{96,104},{112,120},{128,1..., dimensions={0}, use_global_device_ids=true | all-gather | bytes 196608 | tf_op jit(solution)/shard_map/all_gather | solution.py:144
  65.7 0.0 copy-done.11
  65.7 0.9 shard_map.62
  66.7 7.2 %all-gather.5 = bf16[128,512]{1,0:T(8,128)(2,1)S(1)} all-gather(bf16[64,512]{1,0:T(8,128)(2,1)S(1)} %get-tuple-element.101), channel_id=7, replica_groups={{8,16},{24,32},{40,48},{56,64},{72,80},{88,96},{104,112},{120,128},{136..., dimensions={0}, use_global_device_ids=true | all-gather | bytes 196608 | tf_op jit(solution)/shard_map/all_gather | solution.py:144
  73.9 0.0 copy-done.8
  73.9 0.7 shard_map.63
  74.6 4.1 %all-gather.6 = bf16[128,512]{1,0:T(8,128)(2,1)S(1)} all-gather(bf16[64,512]{1,0:T(8,128)(2,1)S(1)} %get-tuple-element.106), channel_id=8, replica_groups={{0,8},{16,24},{32,40},{48,56},{64,72},{80,88},{96,104},{112,120},{128,1..., dimensions={0}, use_global_device_ids=true | all-gather | bytes 196608 | tf_op jit(solution)/shard_map/all_gather | solution.py:144
  78.7 0.7 shard_map.64
  79.4 7.1 %all-gather.7 = bf16[128,512]{1,0:T(8,128)(2,1)S(1)} all-gather(bf16[64,512]{1,0:T(8,128)(2,1)S(1)} %get-tuple-element.111), channel_id=9, replica_groups={{8,16},{24,32},{40,48},{56,64},{72,80},{88,96},{104,112},{120,128},{136..., dimensions={0}, use_global_device_ids=true | all-gather | bytes 196608 | tf_op jit(solution)/shard_map/all_gather | solution.py:144
  86.6 0.2 shard_map.65.refs_5_
  86.8 0.3 shard_map.66
  87.1 3.8 %all-gather.8 = bf16[128,512]{1,0:T(8,128)(2,1)S(1)} all-gather(bf16[64,512]{1,0:T(8,128)(2,1)S(1)} %get-tuple-element.112), channel_id=10, replica_groups={{0,8},{16,24},{32,40},{48,56},{64,72},{80,88},{96,104},{112,120},{128,1..., dimensions={0}, use_global_device_ids=true | all-gather | bytes 196608 | tf_op jit(solution)/shard_map/all_gather | solution.py:144
  90.9 0.4 shard_map.67
  91.3 7.1 %all-gather.9 = bf16[128,512]{1,0:T(8,128)(2,1)S(1)} all-gather(bf16[64,512]{1,0:T(8,128)(2,1)S(1)} %get-tuple-element.116), channel_id=11, replica_groups={{8,16},{24,32},{40,48},{56,64},{72,80},{88,96},{104,112},{120,128},{136..., dimensions={0}, use_global_device_ids=true | all-gather | bytes 196608 | tf_op jit(solution)/shard_map/all_gather | solution.py:144
  98.4 0.5 shard_map.68
  98.9 3.8 %all-gather.10 = bf16[128,512]{1,0:T(8,128)(2,1)S(1)} all-gather(bf16[64,512]{1,0:T(8,128)(2,1)S(1)} %get-tuple-element.120), channel_id=12, replica_groups={{0,8},{16,24},{32,40},{48,56},{64,72},{80,88},{96,104},{112,120},{128,1..., dimensions={0}, use_global_device_ids=true | all-gather | bytes 196608 | tf_op jit(solution)/shard_map/all_gather | solution.py:144
  102.7 0.5 shard_map.69
  103.2 0.0 copy-start.7
  103.2 7.3 %all-gather.11 = bf16[128,512]{1,0:T(8,128)(2,1)S(1)} all-gather(bf16[64,512]{1,0:T(8,128)(2,1)S(1)} %get-tuple-element.124), channel_id=13, replica_groups={{8,16},{24,32},{40,48},{56,64},{72,80},{88,96},{104,112},{120,128},{136..., dimensions={0}, use_global_device_ids=true | all-gather | bytes 196608 | tf_op jit(solution)/shard_map/all_gather | solution.py:144
  110.5 0.6 shard_map.70
  111.1 3.8 %all-gather.12 = bf16[128,512]{1,0:T(8,128)(2,1)S(1)} all-gather(bf16[64,512]{1,0:T(8,128)(2,1)S(1)} %get-tuple-element.128), channel_id=14, replica_groups={{0,8},{16,24},{32,40},{48,56},{64,72},{80,88},{96,104},{112,120},{128,1..., dimensions={0}, use_global_device_ids=true | all-gather | bytes 196608 | tf_op jit(solution)/shard_map/all_gather | solution.py:144
  114.9 0.0 copy-done.7
  114.9 0.7 shard_map.71
  115.5 7.9 %all-gather.13 = bf16[128,512]{1,0:T(8,128)(2,1)S(1)} all-gather(bf16[64,512]{1,0:T(8,128)(2,1)S(1)} %get-tuple-element.132), channel_id=15, replica_groups={{8,16},{24,32},{40,48},{56,64},{72,80},{88,96},{104,112},{120,128},{136..., dimensions={0}, use_global_device_ids=true | all-gather | bytes 196608 | tf_op jit(solution)/shard_map/all_gather | solution.py:144
  123.4 0.2 shard_map.72
  123.7 3.4 %all-gather.14 = bf16[128,256]{1,0:T(8,128)(2,1)S(1)} all-gather(bf16[64,256]{1,0:T(8,128)(2,1)S(1)} %get-tuple-element.135), channel_id=16, replica_groups={{0,8},{16,24},{32,40},{48,56},{64,72},{80,88},{96,104},{112,120},{128,1..., dimensions={0}, use_global_device_ids=true | all-gather | bytes 98304 | tf_op jit(solution)/shard_map/all_gather | solution.py:144
  127.1 0.3 shard_map.73
  127.4 27.1 %all_to_all.10.r_ref = bf16[8,64,256]{2,1,0:T(8,128)(2,1)S(1)} all-to-all(bf16[8,64,256]{2,1,0:T(8,128)(2,1)S(1)} %shard_map.73), channel_id=1, replica_groups=mesh['sn'=64,'rhs'=8] {'rhs'}, dimensions={0} | all-to-all | bytes 524288 | tf_op jit(solution)/shard_map/all_to_all | solution.py:284
  154.6 1.1 shard_map.74
  (15 shorter events, 0.1 us)
Async XLA Ops:
  0.0 1.0 copy-start.15
  1.9 20.2 %all-to-all-start = ((bf16[8,64,256]{2,1,0:T(8,128)(2,1)}), bf16[8,64,256]{2,1,0:T(8,128)(2,1)S(1)}, u32[]{:S(2)}, u32[]{:S(2)}) async-start(bf16[8,64,256]{2,1,0:T(8,128)(2,1)} %shard_map.55), calls=%async_computation | async-start | bytes 524288 | tf_op jit(solution)/shard_map/all_to_all | solution.py:123
  13.5 20.6 %copy-start = (bf16[8,2,128,128]{3,2,1,0:T(8,128)(2,1)S(1)}, bf16[8,2,128,128]{3,2,1,0:T(8,128)(2,1)}, u32[]{:S(2)}) copy-start(bf16[8,2,128,128]{3,2,1,0:T(8,128)(2,1)} %d_ref.5) | copy-start | bytes 1572868
  22.1 25.2 %copy-start.1 = (bf16[1792,768]{1,0:T(8,128)(2,1)S(1)}, bf16[1792,768]{1,0:T(8,128)(2,1)}, u32[]{:S(2)}) copy-start(bf16[1792,768]{1,0:T(8,128)(2,1)} %get-tuple-element.83.refs_7_.refs_9_) | copy-start | bytes 8257540
  22.1 25.2 %copy-start.4 = (bf16[256,768]{1,0:T(8,128)(2,1)S(1)}, bf16[256,768]{1,0:T(8,128)(2,1)}, u32[]{:S(2)}) copy-start(bf16[256,768]{1,0:T(8,128)(2,1)} %get-tuple-element.82.refs_4_.refs_2_.refs_8_) | copy-start | bytes 1179652
  22.1 25.1 %collective-permute-start.1 = (bf16[3,256,256]{2,1,0:T(8,128)(2,1)}, bf16[3,256,256]{2,1,0:T(8,128)(2,1)S(1)}, u32[]{:S(2)}, u32[]{:S(2)}) collective-permute-start(bf16[3,256,256]{2,1,0:T(8,128)(2,1)} %get-tuple-element.85), channel_id=1, source_target_pairs={{0,8},{16,24},{32,40},{48,56},{64,72},{80,88},{96,104},{112,120},{... | collective-permute-start | bytes 1179656 | tf_op jit(solution)/shard_map/ppermute | solution.py:140
  24.3 22.9 %collective-permute-start = (bf16[4,256,256]{2,1,0:T(8,128)(2,1)}, bf16[4,256,256]{2,1,0:T(8,128)(2,1)S(1)}, u32[]{:S(2)}, u32[]{:S(2)}) collective-permute-start(bf16[4,256,256]{2,1,0:T(8,128)(2,1)} %get-tuple-element.80), channel_id=1, source_target_pairs={{8,16},{24,32},{40,48},{56,64},{72,80},{88,96},{104,112},{120,128}... | collective-permute-start | bytes 1572872 | tf_op jit(solution)/shard_map/ppermute | solution.py:140
  38.2 1.0 copy-start.6
  47.3 5.1 %copy-start.2 = (bf16[1536,768]{1,0:T(8,128)(2,1)S(1)}, bf16[1536,768]{1,0:T(8,128)(2,1)}, u32[]{:S(2)}) copy-start(bf16[1536,768]{1,0:T(8,128)(2,1)} %get-tuple-element.89.refs_7_.refs_9_) | copy-start | bytes 7077892
  47.3 5.1 %copy-start.5 = (bf16[256,768]{1,0:T(8,128)(2,1)S(1)}, bf16[256,768]{1,0:T(8,128)(2,1)}, u32[]{:S(2)}) copy-start(bf16[256,768]{1,0:T(8,128)(2,1)} %get-tuple-element.87.refs_4_.refs_2_.refs_8_) | copy-start | bytes 1179652
  48.5 12.4 %copy-start.3 = (bf16[1280,768]{1,0:T(8,128)(2,1)S(1)}, bf16[1280,768]{1,0:T(8,128)(2,1)}, u32[]{:S(2)}) copy-start(bf16[1280,768]{1,0:T(8,128)(2,1)} %get-tuple-element.94.refs_7_.refs_9_) | copy-start | bytes 5898244
  48.5 12.4 %copy-start.10 = (bf16[256,768]{1,0:T(8,128)(2,1)S(1)}, bf16[256,768]{1,0:T(8,128)(2,1)}, u32[]{:S(2)}) copy-start(bf16[256,768]{1,0:T(8,128)(2,1)} %get-tuple-element.92.refs_4_.refs_2_.refs_8_) | copy-start | bytes 1179652
  53.6 12.1 %copy-start.9 = (bf16[1024,768]{1,0:T(8,128)(2,1)S(1)}, bf16[1024,768]{1,0:T(8,128)(2,1)}, u32[]{:S(2)}) copy-start(bf16[1024,768]{1,0:T(8,128)(2,1)} %get-tuple-element.99.refs_7_.refs_9_) | copy-start | bytes 4718596
  53.6 12.1 %copy-start.11 = (bf16[256,768]{1,0:T(8,128)(2,1)S(1)}, bf16[256,768]{1,0:T(8,128)(2,1)}, u32[]{:S(2)}) copy-start(bf16[256,768]{1,0:T(8,128)(2,1)} %get-tuple-element.97.refs_4_.refs_2_.refs_8_) | copy-start | bytes 1179652
  61.8 12.1 %copy-start.8 = (bf16[256,768]{1,0:T(8,128)(2,1)S(1)}, bf16[256,768]{1,0:T(8,128)(2,1)}, u32[]{:S(2)}) copy-start(bf16[256,768]{1,0:T(8,128)(2,1)} %get-tuple-element.102.refs_4_.refs_2_.refs_6_) | copy-start | bytes 1179652
  61.8 12.1 %copy-start.12 = (bf16[768,768]{1,0:T(8,128)(2,1)S(1)}, bf16[768,768]{1,0:T(8,128)(2,1)}, u32[]{:S(2)}) copy-start(bf16[768,768]{1,0:T(8,128)(2,1)} %get-tuple-element.104.refs_7_.refs_9_) | copy-start | bytes 3538948
  66.7 12.1 %copy-start.13 = (bf16[256,768]{1,0:T(8,128)(2,1)S(1)}, bf16[256,768]{1,0:T(8,128)(2,1)}, u32[]{:S(2)}) copy-start(bf16[256,768]{1,0:T(8,128)(2,1)} %get-tuple-element.107.refs_4_.refs_2_) | copy-start | bytes 1179652
  66.7 12.1 %copy-start.14 = (bf16[512,768]{1,0:T(8,128)(2,1)S(1)}, bf16[512,768]{1,0:T(8,128)(2,1)}, u32[]{:S(2)}) copy-start(bf16[512,768]{1,0:T(8,128)(2,1)} %get-tuple-element.109.refs_7_) | copy-start | bytes 2359300
  103.2 11.7 %copy-start.7 = (bf16[256,768]{1,0:T(8,128)(2,1)S(1)}, bf16[256,768]{1,0:T(8,128)(2,1)}, u32[]{:S(2)}) copy-start(bf16[256,768]{1,0:T(8,128)(2,1)} %get-tuple-element.77.refs_2_.refs_8_) | copy-start | bytes 1179652

commit v7 on v6

--- a/solution.py
+++ b/solution.py
@@ -20,7 +20,7 @@
     return lax.dot_general(a, w, (((1,), (0,)), ((), ())), preferred_element_type=F32)
 
 
-def call(body, outs, args, scratch=(), flops=10**7, mib=12, specs=None, out_specs=None, size=None):
+def call(body, outs, args, scratch=(), flops=10**7, mib=12, specs=None, out_specs=None, size=None, aliases=None):
     specs = specs or [SMEM if a.dtype == jnp.int32 else VMEM for a in args]
     if size is None:
         size = sum(a.size * a.dtype.itemsize for a in args)
@@ -30,6 +30,7 @@
         in_specs=specs,
         out_specs=out_specs or [VMEM] * len(outs),
         scratch_shapes=list(scratch),
+        input_output_aliases=aliases or {},
         compiler_params=pltpu.CompilerParams(vmem_limit_bytes=mib * 2**20),
         cost_estimate=pl.CostEstimate(flops=flops, bytes_accessed=size, transcendentals=0),
     )(*args)
@@ -42,8 +43,8 @@
     wide = 3 * tall
 
     def body(row_ref, col_ref, par_ref, t_ref, d_ref, *refs):
-        outs, (scratch, held, sems, in_sems) = refs[: 2 * levels], refs[2 * levels :]
-        s_out, b_out, sends = outs[: levels - 1], outs[levels - 1 : 2 * levels - 2], outs[-2:]
+        outs, (scratch, held, sems, in_sems) = refs[: 2 * levels + 1], refs[2 * levels + 1 :]
+        s_out, b_out, sends = outs[: levels - 1], outs[levels - 1 : 2 * levels - 2], outs[-3:]
         loads = [
             pltpu.make_async_copy(t_ref.at[l], held.at[l], in_sems.at[l]) for l in range(levels - 1)
         ]
@@ -72,13 +73,13 @@
                 b_out[l][rows, :] = dot_n(d_ref[l + 1, q], buf[rows, :]).astype(BF)
             s = side_of(par_ref, l + 1)
             toward = pl.ds(pl.multiple_of((1 - s) * 2 * tall, tall), tall)
-            sends[l % 2][l // 2] = b_out[l][:, toward]
+            sends[0 if l == 0 else 1 + l % 2][(l - 1) // 2 if l else 0] = b_out[l][:, toward]
         for c in copies:
             c.wait()
 
     outs = [(((levels - 1 - l) * tall, wide), BF) for l in range(levels - 1)]
     outs += [((tall, wide), BF)] * (levels - 1)
-    outs += [((levels // 2, tall, tall), BF), (((levels - 1) // 2, tall, tall), BF)]
+    outs += [((k, tall, tall), BF) for k in (1, levels // 2 - 1, (levels - 1) // 2)]
     res = call(
         body,
         outs,
@@ -92,10 +93,10 @@
         flops=4 * 10**8,
         mib=60,
         specs=[SMEM, SMEM, SMEM, HBM, VMEM],
-        out_specs=[HBM] * (levels - 1) + [VMEM] * (levels + 1),
+        out_specs=[HBM] * (levels - 1) + [VMEM] * (levels + 2),
         size=24 * 2**20,
     )
-    return res[: levels - 1], res[levels - 1 : 2 * levels - 2], res[-2:]
+    return res[: levels - 1], res[levels - 1 : 2 * levels - 2], res[-3:]
 
 
 def on_device(lanczos_block, diag_inv, factor_tiles, tile_rows, tile_cols):
@@ -137,8 +138,9 @@
     ]
     swaps = [[(p, q) for p, q in g] + [(q, p) for p, q in g] for g in pairs]
     arrived, toward = lax.optimization_barrier((arrived, list(toward)))
-    far_odd, far_even = (lax.ppermute(toward[k], "sn", swaps[1 - k]) for k in range(2))
-    far = [None] + [(far_odd if l % 2 else far_even)[(l - 1) // 2] for l in range(1, levels)]
+    far = [None] * levels
+    first_far = lax.ppermute(toward[0], "sn", swaps[1])
+    far[1] = first_far[0]
 
     def swap(l, message):
         return lax.all_gather(message, "sn", axis_index_groups=pairs[l % 2])
@@ -178,6 +180,15 @@
                 args += (S[l - 1], before)
                 if rest_levels:
                     outs.append(((cols, rest_levels * w), F32))
+        aliases, extra = {}, {}
+        if l < 2:
+            carried = toward[2 - l]
+            aliases, extra = {len(args): len(outs)}, {len(args): pl.BlockSpec(memory_space=pl.ANY)}
+            args += (carried,)
+            outs.append((carried.shape, BF))
+        if l == 0:
+            extra[len(args)] = pl.BlockSpec(memory_space=pl.ANY)
+            args += (first_far,)
         n_in = len(args)
 
         def step(*refs):
@@ -213,14 +224,22 @@
             if l and rest_levels:
                 refs[n_in + 2][...] = acc_ref[:, base + w :] - dot_t(y3[...], s_ref[2 * w :, :])
 
-        res = call(step, outs, args, [pltpu.VMEM((cols, 3 * w), BF)])
-        return res[0], res[1] if more else None, res[-1] if l else acc
+        specs = [extra.get(k, SMEM if a.dtype == jnp.int32 else VMEM) for k, a in enumerate(args)]
+        out_specs = [pl.BlockSpec(memory_space=pl.ANY) if k in aliases.values() else VMEM for k in range(len(outs))]
+        res = list(call(step, outs, args, [pltpu.VMEM((cols, 3 * w), BF)], specs=specs, out_specs=out_specs, aliases=aliases))
+        passed = res.pop() if l < 2 else None
+        return res[0], res[1] if more else None, res[-1], passed
 
     pair_y = [None] * levels
-    acc, message, before = x, y0, None
-    for l in range(levels):
-        before, message, acc = forward_step(l, swap(l, message), before, acc)
-        pair_y[l] = before
+    pair_y[0], message, _, carried = forward_step(0, swap(0, y0), None, x)
+    acc = x
+    for l in range(1, levels):
+        if l < 3:
+            fetched = lax.ppermute(carried, "sn", swaps[l - 1])
+            for k in range(l + 1, levels, 2):
+                far[k] = fetched[(k - l - 1) // 2]
+        got = swap(l, message)
+        pair_y[l], message, acc, carried = forward_step(l, got, pair_y[l - 1], acc)
 
     def backward_step(l, got, cot, older, above):
         top, more = l == levels - 1, l >= 2

time: 156 us -> 163 us (1.045)
  starting transfers between devices: 22.2 us -> 27.9 us
  local copies, waits for them, and re-layouts: 2.16 us -> 4.14 us
    ppermute x2 -> x3, starting transfers between devices: 12 us -> 17.7 us  [the longest x1 9.35 us: on_device(): first_far = lax.ppermute(toward[0], 'sn', swaps[1])]
    unnamed x32 -> x36, local copies, waits for them, and re-layouts: 2.1 us -> 4.08 us
  transfers between devices with their start and end apart: 3 -> 4, of which waited for: 0 -> 0; matrix products, arithmetic and copies ran while one was open for 1% -> 1% of each run, Pallas kernels for 6% -> 7%
where the time goes in v7:
time: 163 us
  blocking collectives  109 us (67%)
  starting transfers between devices  27.9 us (17%)
  Pallas kernels  20.3 us (12%)
  local copies, waits for them, and re-layouts  4.14 us (3%)
    all_gather x15, blocking collectives, swap(): return lax.all_gather(message, 'sn', axis_index_groups=pairs[l % 2])  80.9 us
    all_to_all x1, blocking collectives, on_device(): lax.all_to_all(result, 'rhs', split_axis=0, concat_axis=0, tiled=True)  27.6 us
    pallas_call x20, Pallas kernels, call(): pl.pallas_call(body, out_shape=[jax.ShapeDtypeStruct(s, d) for s, d in ou...  20.3 us
    all_to_all x1, starting transfers between devices, on_device(): lax.all_to_all(sent, 'rhs', split_axis=0, concat_axis=0, tiled=True)  10.2 us
    ppermute x1, starting transfers between devices, on_device(): first_far = lax.ppermute(toward[0], 'sn', swaps[1])  9.35 us
    ppermute x2, starting transfers between devices, on_device(): fetched = lax.ppermute(carried, 'sn', swaps[l - 1])  8.39 us
    unnamed x36, local copies, waits for them, and re-layouts  4.08 us
  transfers between devices with their start and end apart: 4, of which 0 were waited for; matrix products, arithmetic and copies ran while one was open for 1% of the time, Pallas kernels for 7%

profile of v7, /device:TPU:1, one launch (start us, length us, event | category | flops | bytes accessed | tf_op | source)
XLA Modules:
  0.0 162.6 jit_solution(14062353011735786307)
XLA Ops:
  0.0 1.0 copy-done.16
  1.0 0.8 shard_map.55
  1.9 10.2 %all-to-all-start = ((bf16[8,64,256]{2,1,0:T(8,128)(2,1)}), bf16[8,64,256]{2,1,0:T(8,128)(2,1)S(1)}, u32[]{:S(2)}, u32[]{:S(2)}) async-start(bf16[8,64,256]{2,1,0:T(8,128)(2,1)} %shard_map.55), calls=%async_computation | async-start | bytes 524288 | tf_op jit(solution)/shard_map/all_to_all | solution.py:124
  12.1 1.4 fusion.3
  13.5 8.7 %shard_map.56 = (bf16[1792,768]{1,0:T(8,128)(2,1)}, bf16[1536,768]{1,0:T(8,128)(2,1)}, bf16[1280,768]{1,0:T(8,128)(2,1)}, bf16[1024,768]{1,0:T(8,128)(2,1)}, bf1...) custom-call(s32[7,24]{1,0:T(8,128)} %get-tuple-element.153.row_ref, ...), custom_call_target="tpu_custom_call" | custom-call | flops 400000000 | bytes 25165824 | tf_op jit(solution)/shard_map/pallas_call | solution.py:27
  22.2 0.0 copy-start.1
  22.2 0.0 all-to-all-done.a_ref
  22.2 9.3 %collective-permute-start = (bf16[1,256,256]{2,1,0:T(8,128)(2,1)}, bf16[1,256,256]{2,1,0:T(8,128)(2,1)S(1)}, u32[]{:S(2)}, u32[]{:S(2)}) collective-permute-start(bf16[1,256,256]{2,1,0:T(8,128)(2,1)} %get-tuple-element.85), channel_id=1, source_target_pairs={{8,16},{24,32},{40,48},{56,64},{72,80},{88,96},{104,112},{120,128}... | collective-permute-start | bytes 393224 | tf_op jit(solution)/shard_map/ppermute | solution.py:142
  31.6 0.0 copy-done
  31.6 0.3 shard_map.57
  31.8 3.7 %all-gather = bf16[128,256]{1,0:T(8,128)(2,1)S(1)} all-gather(bf16[64,256]{1,0:T(8,128)(2,1)S(1)} %get-tuple-element.81), channel_id=2, replica_groups={{0,8},{16,24},{32,40},{48,56},{64,72},{80,88},{96,104},{112,120},{128,1..., dimensions={0}, use_global_device_ids=true | all-gather | bytes 98304 | tf_op jit(solution)/shard_map/all_gather | solution.py:146
  35.6 0.0 collective-permute-done.refs_6_
  35.6 1.0 copy-done.11
  36.6 1.0 copy-done.17
  37.6 0.3 shard_map.58
  37.9 1.9 %collective-permute-start.1 = (bf16[3,256,256]{2,1,0:T(8,128)(2,1)S(1)}, bf16[3,256,256]{2,1,0:T(8,128)(2,1)S(1)}, u32[]{:S(2)}, u32[]{:S(2)}) collective-permute-start(bf16[3,256,256]{2,1,0:T(8,128)(2,1)S(1)} %get-tuple-element.92), channel_id=1, source_target_pairs={{0,8},{16,24},{32,40},{48,56},{64,72},{80,88},{96,104},{112,120},{... | collective-permute-start | bytes 1179656 | tf_op jit(solution)/shard_map/ppermute | solution.py:238
  39.8 7.1 %all-gather.1 = bf16[128,512]{1,0:T(8,128)(2,1)S(1)} all-gather(bf16[64,512]{1,0:T(8,128)(2,1)S(1)} %get-tuple-element.87), channel_id=3, replica_groups={{8,16},{24,32},{40,48},{56,64},{72,80},{88,96},{104,112},{120,128},{136..., dimensions={0}, use_global_device_ids=true | all-gather | bytes 196608 | tf_op jit(solution)/shard_map/all_gather | solution.py:146
  46.9 0.0 copy-done.1
  46.9 1.0 copy-done.7
  47.9 1.1 shard_map.59
  49.0 6.5 %collective-permute-start.2 = (bf16[3,256,256]{2,1,0:T(8,128)(2,1)}, bf16[3,256,256]{2,1,0:T(8,128)(2,1)S(1)}, u32[]{:S(2)}, u32[]{:S(2)}) collective-permute-start(bf16[3,256,256]{2,1,0:T(8,128)(2,1)} %get-tuple-element.98), channel_id=1, source_target_pairs={{8,16},{24,32},{40,48},{56,64},{72,80},{88,96},{104,112},{120,128}... | collective-permute-start | bytes 1179656 | tf_op jit(solution)/shard_map/ppermute | solution.py:238
  55.5 3.8 %all-gather.2 = bf16[128,512]{1,0:T(8,128)(2,1)S(1)} all-gather(bf16[64,512]{1,0:T(8,128)(2,1)S(1)} %get-tuple-element.93), channel_id=4, replica_groups={{0,8},{16,24},{32,40},{48,56},{64,72},{80,88},{96,104},{112,120},{128,1..., dimensions={0}, use_global_device_ids=true | all-gather | bytes 196608 | tf_op jit(solution)/shard_map/all_gather | solution.py:146
  59.3 0.0 collective-permute-done.1
  59.3 0.0 copy-done.2
  59.3 0.0 copy-done.4
  59.4 0.0 copy-done.8
  59.4 0.0 copy-start.3
  59.4 0.0 copy-start.9
  59.4 1.1 shard_map.60
  60.5 7.1 %all-gather.3 = bf16[128,512]{1,0:T(8,128)(2,1)S(1)} all-gather(bf16[64,512]{1,0:T(8,128)(2,1)S(1)} %get-tuple-element.99), channel_id=5, replica_groups={{8,16},{24,32},{40,48},{56,64},{72,80},{88,96},{104,112},{120,128},{136..., dimensions={0}, use_global_device_ids=true | all-gather | bytes 196608 | tf_op jit(solution)/shard_map/all_gather | solution.py:146
  67.7 0.0 collective-permute-done.2
  67.7 0.0 copy-done.3
  67.7 0.0 copy-done.9
  67.7 0.9 shard_map.61
  68.6 0.0 copy-start.5
  68.6 0.0 copy-start.13
  68.6 3.9 %all-gather.4 = bf16[128,512]{1,0:T(8,128)(2,1)S(1)} all-gather(bf16[64,512]{1,0:T(8,128)(2,1)S(1)} %get-tuple-element.104), channel_id=6, replica_groups={{0,8},{16,24},{32,40},{48,56},{64,72},{80,88},{96,104},{112,120},{128,1..., dimensions={0}, use_global_device_ids=true | all-gather | bytes 196608 | tf_op jit(solution)/shard_map/all_gather | solution.py:146
  72.6 0.9 shard_map.62
  73.5 0.0 copy-start.14
  73.5 0.0 copy-start.15
  73.5 7.2 %all-gather.5 = bf16[128,512]{1,0:T(8,128)(2,1)S(1)} all-gather(bf16[64,512]{1,0:T(8,128)(2,1)S(1)} %get-tuple-element.109), channel_id=7, replica_groups={{8,16},{24,32},{40,48},{56,64},{72,80},{88,96},{104,112},{120,128},{136..., dimensions={0}, use_global_device_ids=true | all-gather | bytes 196608 | tf_op jit(solution)/shard_map/all_gather | solution.py:146
  80.8 0.7 shard_map.63
  81.5 4.1 %all-gather.6 = bf16[128,512]{1,0:T(8,128)(2,1)S(1)} all-gather(bf16[64,512]{1,0:T(8,128)(2,1)S(1)} %get-tuple-element.114), channel_id=8, replica_groups={{0,8},{16,24},{32,40},{48,56},{64,72},{80,88},{96,104},{112,120},{128,1..., dimensions={0}, use_global_device_ids=true | all-gather | bytes 196608 | tf_op jit(solution)/shard_map/all_gather | solution.py:146
  85.6 0.0 copy-done.14
  85.6 0.7 shard_map.64
  86.3 7.1 %all-gather.7 = bf16[128,512]{1,0:T(8,128)(2,1)S(1)} all-gather(bf16[64,512]{1,0:T(8,128)(2,1)S(1)} %get-tuple-element.119), channel_id=9, replica_groups={{8,16},{24,32},{40,48},{56,64},{72,80},{88,96},{104,112},{120,128},{136..., dimensions={0}, use_global_device_ids=true | all-gather | bytes 196608 | tf_op jit(solution)/shard_map/all_gather | solution.py:146
  93.4 0.2 shard_map.65.refs_5_
  93.6 0.3 shard_map.66
  93.9 3.8 %all-gather.8 = bf16[128,512]{1,0:T(8,128)(2,1)S(1)} all-gather(bf16[64,512]{1,0:T(8,128)(2,1)S(1)} %get-tuple-element.120), channel_id=10, replica_groups={{0,8},{16,24},{32,40},{48,56},{64,72},{80,88},{96,104},{112,120},{128,1..., dimensions={0}, use_global_device_ids=true | all-gather | bytes 196608 | tf_op jit(solution)/shard_map/all_gather | solution.py:146
  97.7 0.4 shard_map.67
  98.1 7.1 %all-gather.9 = bf16[128,512]{1,0:T(8,128)(2,1)S(1)} all-gather(bf16[64,512]{1,0:T(8,128)(2,1)S(1)} %get-tuple-element.124), channel_id=11, replica_groups={{8,16},{24,32},{40,48},{56,64},{72,80},{88,96},{104,112},{120,128},{136..., dimensions={0}, use_global_device_ids=true | all-gather | bytes 196608 | tf_op jit(solution)/shard_map/all_gather | solution.py:146
  105.2 0.5 shard_map.68
  105.7 3.8 %all-gather.10 = bf16[128,512]{1,0:T(8,128)(2,1)S(1)} all-gather(bf16[64,512]{1,0:T(8,128)(2,1)S(1)} %get-tuple-element.128), channel_id=12, replica_groups={{0,8},{16,24},{32,40},{48,56},{64,72},{80,88},{96,104},{112,120},{128,1..., dimensions={0}, use_global_device_ids=true | all-gather | bytes 196608 | tf_op jit(solution)/shard_map/all_gather | solution.py:146
  109.5 0.5 shard_map.69
  110.1 7.2 %all-gather.11 = bf16[128,512]{1,0:T(8,128)(2,1)S(1)} all-gather(bf16[64,512]{1,0:T(8,128)(2,1)S(1)} %get-tuple-element.132), channel_id=13, replica_groups={{8,16},{24,32},{40,48},{56,64},{72,80},{88,96},{104,112},{120,128},{136..., dimensions={0}, use_global_device_ids=true | all-gather | bytes 196608 | tf_op jit(solution)/shard_map/all_gather | solution.py:146
  117.3 0.6 shard_map.70
  117.9 3.9 %all-gather.12 = bf16[128,512]{1,0:T(8,128)(2,1)S(1)} all-gather(bf16[64,512]{1,0:T(8,128)(2,1)S(1)} %get-tuple-element.136), channel_id=14, replica_groups={{0,8},{16,24},{32,40},{48,56},{64,72},{80,88},{96,104},{112,120},{128,1..., dimensions={0}, use_global_device_ids=true | all-gather | bytes 196608 | tf_op jit(solution)/shard_map/all_gather | solution.py:146
  121.8 0.7 shard_map.71
  122.5 7.5 %all-gather.13 = bf16[128,512]{1,0:T(8,128)(2,1)S(1)} all-gather(bf16[64,512]{1,0:T(8,128)(2,1)S(1)} %get-tuple-element.140), channel_id=15, replica_groups={{8,16},{24,32},{40,48},{56,64},{72,80},{88,96},{104,112},{120,128},{136..., dimensions={0}, use_global_device_ids=true | all-gather | bytes 196608 | tf_op jit(solution)/shard_map/all_gather | solution.py:146
  130.0 0.2 shard_map.72
  130.2 3.4 %all-gather.14 = bf16[128,256]{1,0:T(8,128)(2,1)S(1)} all-gather(bf16[64,256]{1,0:T(8,128)(2,1)S(1)} %get-tuple-element.143), channel_id=16, replica_groups={{0,8},{16,24},{32,40},{48,56},{64,72},{80,88},{96,104},{112,120},{128,1..., dimensions={0}, use_global_device_ids=true | all-gather | bytes 98304 | tf_op jit(solution)/shard_map/all_gather | solution.py:146
  133.7 0.3 shard_map.73
  134.0 27.6 %all_to_all.10.r_ref = bf16[8,64,256]{2,1,0:T(8,128)(2,1)S(1)} all-to-all(bf16[8,64,256]{2,1,0:T(8,128)(2,1)S(1)} %shard_map.73), channel_id=1, replica_groups=mesh['sn'=64,'rhs'=8] {'rhs'}, dimensions={0} | all-to-all | bytes 524288 | tf_op jit(solution)/shard_map/all_to_all | solution.py:303
  161.6 1.1 shard_map.74
  (21 shorter events, 0.1 us)
Async XLA Ops:
  0.0 1.0 copy-start.16
  1.9 20.3 %all-to-all-start = ((bf16[8,64,256]{2,1,0:T(8,128)(2,1)}), bf16[8,64,256]{2,1,0:T(8,128)(2,1)S(1)}, u32[]{:S(2)}, u32[]{:S(2)}) async-start(bf16[8,64,256]{2,1,0:T(8,128)(2,1)} %shard_map.55), calls=%async_computation | async-start | bytes 524288 | tf_op jit(solution)/shard_map/all_to_all | solution.py:124
  13.5 18.1 %copy-start = (bf16[8,2,128,128]{3,2,1,0:T(8,128)(2,1)S(1)}, bf16[8,2,128,128]{3,2,1,0:T(8,128)(2,1)}, u32[]{:S(2)}) copy-start(bf16[8,2,128,128]{3,2,1,0:T(8,128)(2,1)} %d_ref.5) | copy-start | bytes 1572868
  22.2 24.7 %copy-start.1 = (bf16[1792,768]{1,0:T(8,128)(2,1)S(1)}, bf16[1792,768]{1,0:T(8,128)(2,1)}, u32[]{:S(2)}) copy-start(bf16[1792,768]{1,0:T(8,128)(2,1)} %get-tuple-element.89.refs_7_.refs_9_) | copy-start | bytes 8257540
  22.2 13.4 %collective-permute-start = (bf16[1,256,256]{2,1,0:T(8,128)(2,1)}, bf16[1,256,256]{2,1,0:T(8,128)(2,1)S(1)}, u32[]{:S(2)}, u32[]{:S(2)}) collective-permute-start(bf16[1,256,256]{2,1,0:T(8,128)(2,1)} %get-tuple-element.85), channel_id=1, source_target_pairs={{8,16},{24,32},{40,48},{56,64},{72,80},{88,96},{104,112},{120,128}... | collective-permute-start | bytes 393224 | tf_op jit(solution)/shard_map/ppermute | solution.py:142
  35.6 1.0 copy-start.11
  36.6 1.0 copy-start.17
  37.9 21.4 %collective-permute-start.1 = (bf16[3,256,256]{2,1,0:T(8,128)(2,1)S(1)}, bf16[3,256,256]{2,1,0:T(8,128)(2,1)S(1)}, u32[]{:S(2)}, u32[]{:S(2)}) collective-permute-start(bf16[3,256,256]{2,1,0:T(8,128)(2,1)S(1)} %get-tuple-element.92), channel_id=1, source_target_pairs={{0,8},{16,24},{32,40},{48,56},{64,72},{80,88},{96,104},{112,120},{... | collective-permute-start | bytes 1179656 | tf_op jit(solution)/shard_map/ppermute | solution.py:238
  46.9 1.0 copy-start.7
  47.9 11.4 %copy-start.2 = (bf16[1536,768]{1,0:T(8,128)(2,1)S(1)}, bf16[1536,768]{1,0:T(8,128)(2,1)}, u32[]{:S(2)}) copy-start(bf16[1536,768]{1,0:T(8,128)(2,1)} %get-tuple-element.96.refs_7_.refs_9_) | copy-start | bytes 7077892
  47.9 11.4 %copy-start.4 = (bf16[256,768]{1,0:T(8,128)(2,1)S(1)}, bf16[256,768]{1,0:T(8,128)(2,1)}, u32[]{:S(2)}) copy-start(bf16[256,768]{1,0:T(8,128)(2,1)} %get-tuple-element.94.refs_4_.refs_2_.refs_8_) | copy-start | bytes 1179652
  47.9 11.5 %copy-start.8 = (bf16[256,768]{1,0:T(8,128)(2,1)S(1)}, bf16[256,768]{1,0:T(8,128)(2,1)}, u32[]{:S(2)}) copy-start(bf16[256,768]{1,0:T(8,128)(2,1)} %get-tuple-element.88.refs_4_.refs_2_.refs_8_) | copy-start | bytes 1179652
  49.0 18.6 %collective-permute-start.2 = (bf16[3,256,256]{2,1,0:T(8,128)(2,1)}, bf16[3,256,256]{2,1,0:T(8,128)(2,1)S(1)}, u32[]{:S(2)}, u32[]{:S(2)}) collective-permute-start(bf16[3,256,256]{2,1,0:T(8,128)(2,1)} %get-tuple-element.98), channel_id=1, source_target_pairs={{8,16},{24,32},{40,48},{56,64},{72,80},{88,96},{104,112},{120,128}... | collective-permute-start | bytes 1179656 | tf_op jit(solution)/shard_map/ppermute | solution.py:238
  59.4 8.3 %copy-start.3 = (bf16[1280,768]{1,0:T(8,128)(2,1)S(1)}, bf16[1280,768]{1,0:T(8,128)(2,1)}, u32[]{:S(2)}) copy-start(bf16[1280,768]{1,0:T(8,128)(2,1)} %get-tuple-element.102.refs_7_.refs_9_) | copy-start | bytes 5898244
  59.4 8.3 %copy-start.9 = (bf16[256,768]{1,0:T(8,128)(2,1)S(1)}, bf16[256,768]{1,0:T(8,128)(2,1)}, u32[]{:S(2)}) copy-start(bf16[256,768]{1,0:T(8,128)(2,1)} %get-tuple-element.100.refs_4_.refs_2_.refs_8_) | copy-start | bytes 1179652
  67.7 4.9 %copy-start.6 = (bf16[1024,768]{1,0:T(8,128)(2,1)S(1)}, bf16[1024,768]{1,0:T(8,128)(2,1)}, u32[]{:S(2)}) copy-start(bf16[1024,768]{1,0:T(8,128)(2,1)} %get-tuple-element.107.refs_7_.refs_9_) | copy-start | bytes 4718596
  67.7 4.9 %copy-start.10 = (bf16[256,768]{1,0:T(8,128)(2,1)S(1)}, bf16[256,768]{1,0:T(8,128)(2,1)}, u32[]{:S(2)}) copy-start(bf16[256,768]{1,0:T(8,128)(2,1)} %get-tuple-element.105.refs_4_.refs_2_.refs_8_) | copy-start | bytes 1179652
  68.6 12.1 %copy-start.5 = (bf16[256,768]{1,0:T(8,128)(2,1)S(1)}, bf16[256,768]{1,0:T(8,128)(2,1)}, u32[]{:S(2)}) copy-start(bf16[256,768]{1,0:T(8,128)(2,1)} %get-tuple-element.110.refs_4_.refs_2_.refs_6_) | copy-start | bytes 1179652
  68.6 12.1 %copy-start.13 = (bf16[768,768]{1,0:T(8,128)(2,1)S(1)}, bf16[768,768]{1,0:T(8,128)(2,1)}, u32[]{:S(2)}) copy-start(bf16[768,768]{1,0:T(8,128)(2,1)} %get-tuple-element.112.refs_7_.refs_9_) | copy-start | bytes 3538948
  73.5 12.1 %copy-start.14 = (bf16[256,768]{1,0:T(8,128)(2,1)S(1)}, bf16[256,768]{1,0:T(8,128)(2,1)}, u32[]{:S(2)}) copy-start(bf16[256,768]{1,0:T(8,128)(2,1)} %get-tuple-element.115.refs_4_.refs_2_) | copy-start | bytes 1179652
  73.5 12.1 %copy-start.15 = (bf16[512,768]{1,0:T(8,128)(2,1)S(1)}, bf16[512,768]{1,0:T(8,128)(2,1)}, u32[]{:S(2)}) copy-start(bf16[512,768]{1,0:T(8,128)(2,1)} %get-tuple-element.117.refs_7_) | copy-start | bytes 2359300
  110.1 11.7 %copy-start.12 = (bf16[256,768]{1,0:T(8,128)(2,1)S(1)}, bf16[256,768]{1,0:T(8,128)(2,1)}, u32[]{:S(2)}) copy-start(bf16[256,768]{1,0:T(8,128)(2,1)} %get-tuple-element.82.refs_2_.refs_8_) | copy-start | bytes 1179652

commit v8 on v6

--- a/solution.py
+++ b/solution.py
@@ -64,7 +64,7 @@
                 buf[at] = buf[at] + held[l, t]
                 return carry
 
-            lax.fori_loop(0, count, add, 0, unroll=8)
+            lax.fori_loop(0, count, add, 0, unroll=24)
             copies.append(pltpu.make_async_copy(buf, s_out[l], sems.at[l]))
             copies[-1].start()
             for q in range(owned):

time: 156 us -> 156 us (level)
  no operation moved by 1% of the time
where the time goes in v8:
time: 156 us
  blocking collectives  109 us (70%)
  starting transfers between devices  22.2 us (14%)
  Pallas kernels  20.2 us (13%)
  local copies, waits for them, and re-layouts  2.16 us (1%)
    all_gather x15, blocking collectives, swap(): return lax.all_gather(message, 'sn', axis_index_groups=pairs[l % 2])  82.2 us
    all_to_all x1, blocking collectives, on_device(): lax.all_to_all(result, 'rhs', split_axis=0, concat_axis=0, tiled=True)  27.1 us
    pallas_call x20, Pallas kernels, call(): pl.pallas_call(body, out_shape=[jax.ShapeDtypeStruct(s, d) for s, d in ou...  20.2 us
    ppermute x2, starting transfers between devices, on_device(): lax.ppermute(toward[k], 'sn', swaps[1 - k])  12 us
    all_to_all x1, starting transfers between devices, on_device(): lax.all_to_all(sent, 'rhs', split_axis=0, concat_axis=0, tiled=True)  10.2 us
  transfers between devices with their start and end apart: 3, of which 0 were waited for; matrix products, arithmetic and copies ran while one was open for 1% of the time, Pallas kernels for 6%

profile of v8, /device:TPU:1, one launch (start us, length us, event | category | flops | bytes accessed | tf_op | source)
XLA Modules:
  0.0 155.6 jit_solution(424831774414457281)
XLA Ops:
  0.0 1.0 copy-done.15
  1.0 0.8 shard_map.55
  1.9 10.2 %all-to-all-start = ((bf16[8,64,256]{2,1,0:T(8,128)(2,1)}), bf16[8,64,256]{2,1,0:T(8,128)(2,1)S(1)}, u32[]{:S(2)}, u32[]{:S(2)}) async-start(bf16[8,64,256]{2,1,0:T(8,128)(2,1)} %shard_map.55), calls=%async_computation | async-start | bytes 524288 | tf_op jit(solution)/shard_map/all_to_all | solution.py:123
  12.1 1.4 fusion.3
  13.5 8.6 %shard_map.56 = (bf16[1792,768]{1,0:T(8,128)(2,1)}, bf16[1536,768]{1,0:T(8,128)(2,1)}, bf16[1280,768]{1,0:T(8,128)(2,1)}, bf16[1024,768]{1,0:T(8,128)(2,1)}, bf1...) custom-call(s32[7,24]{1,0:T(8,128)} %get-tuple-element.146.row_ref, ...), custom_call_target="tpu_custom_call" | custom-call | flops 400000000 | bytes 25165824 | tf_op jit(solution)/shard_map/pallas_call | solution.py:27
  22.1 0.0 copy-start.1
  22.1 0.0 all-to-all-done.a_ref
  22.1 0.0 copy-start.4
  22.1 2.2 %collective-permute-start.1 = (bf16[3,256,256]{2,1,0:T(8,128)(2,1)}, bf16[3,256,256]{2,1,0:T(8,128)(2,1)S(1)}, u32[]{:S(2)}, u32[]{:S(2)}) collective-permute-start(bf16[3,256,256]{2,1,0:T(8,128)(2,1)} %get-tuple-element.85), channel_id=1, source_target_pairs={{0,8},{16,24},{32,40},{48,56},{64,72},{80,88},{96,104},{112,120},{... | collective-permute-start | bytes 1179656 | tf_op jit(solution)/shard_map/ppermute | solution.py:140
  24.3 9.8 %collective-permute-start = (bf16[4,256,256]{2,1,0:T(8,128)(2,1)}, bf16[4,256,256]{2,1,0:T(8,128)(2,1)S(1)}, u32[]{:S(2)}, u32[]{:S(2)}) collective-permute-start(bf16[4,256,256]{2,1,0:T(8,128)(2,1)} %get-tuple-element.80), channel_id=1, source_target_pairs={{8,16},{24,32},{40,48},{56,64},{72,80},{88,96},{104,112},{120,128}... | collective-permute-start | bytes 1572872 | tf_op jit(solution)/shard_map/ppermute | solution.py:140
  34.1 0.0 copy-done
  34.1 0.3 shard_map.57
  34.4 3.7 %all-gather = bf16[128,256]{1,0:T(8,128)(2,1)S(1)} all-gather(bf16[64,256]{1,0:T(8,128)(2,1)S(1)} %get-tuple-element.76), channel_id=2, replica_groups={{0,8},{16,24},{32,40},{48,56},{64,72},{80,88},{96,104},{112,120},{128,1..., dimensions={0}, use_global_device_ids=true | all-gather | bytes 98304 | tf_op jit(solution)/shard_map/all_gather | solution.py:144
  38.2 1.0 copy-done.6
  39.2 0.3 shard_map.58
  39.4 7.8 %all-gather.1 = bf16[128,512]{1,0:T(8,128)(2,1)S(1)} all-gather(bf16[64,512]{1,0:T(8,128)(2,1)S(1)} %get-tuple-element.81), channel_id=3, replica_groups={{8,16},{24,32},{40,48},{56,64},{72,80},{88,96},{104,112},{120,128},{136..., dimensions={0}, use_global_device_ids=true | all-gather | bytes 196608 | tf_op jit(solution)/shard_map/all_gather | solution.py:144
  47.2 0.0 collective-permute-done.1
  47.3 0.0 collective-permute-done
  47.3 0.0 copy-done.1
  47.3 0.0 copy-done.4
  47.3 0.0 copy-start.2
  47.3 0.0 copy-start.5
  47.3 1.1 shard_map.59
  48.5 0.0 copy-start.3
  48.5 0.0 copy-start.10
  48.5 3.9 %all-gather.2 = bf16[128,512]{1,0:T(8,128)(2,1)S(1)} all-gather(bf16[64,512]{1,0:T(8,128)(2,1)S(1)} %get-tuple-element.86), channel_id=4, replica_groups={{0,8},{16,24},{32,40},{48,56},{64,72},{80,88},{96,104},{112,120},{128,1..., dimensions={0}, use_global_device_ids=true | all-gather | bytes 196608 | tf_op jit(solution)/shard_map/all_gather | solution.py:144
  52.4 0.0 copy-done.2
  52.4 0.0 copy-done.5
  52.4 1.1 shard_map.60
  53.6 0.0 copy-start.9
  53.6 0.0 copy-start.11
  53.6 7.3 %all-gather.3 = bf16[128,512]{1,0:T(8,128)(2,1)S(1)} all-gather(bf16[64,512]{1,0:T(8,128)(2,1)S(1)} %get-tuple-element.91), channel_id=5, replica_groups={{8,16},{24,32},{40,48},{56,64},{72,80},{88,96},{104,112},{120,128},{136..., dimensions={0}, use_global_device_ids=true | all-gather | bytes 196608 | tf_op jit(solution)/shard_map/all_gather | solution.py:144
  60.9 0.0 copy-done.3
  60.9 0.9 shard_map.61
  61.8 0.0 copy-start.8
  61.8 3.9 %all-gather.4 = bf16[128,512]{1,0:T(8,128)(2,1)S(1)} all-gather(bf16[64,512]{1,0:T(8,128)(2,1)S(1)} %get-tuple-element.96), channel_id=6, replica_groups={{0,8},{16,24},{32,40},{48,56},{64,72},{80,88},{96,104},{112,120},{128,1..., dimensions={0}, use_global_device_ids=true | all-gather | bytes 196608 | tf_op jit(solution)/shard_map/all_gather | solution.py:144
  65.7 0.0 copy-done.11
  65.7 0.9 shard_map.62
  66.7 7.2 %all-gather.5 = bf16[128,512]{1,0:T(8,128)(2,1)S(1)} all-gather(bf16[64,512]{1,0:T(8,128)(2,1)S(1)} %get-tuple-element.101), channel_id=7, replica_groups={{8,16},{24,32},{40,48},{56,64},{72,80},{88,96},{104,112},{120,128},{136..., dimensions={0}, use_global_device_ids=true | all-gather | bytes 196608 | tf_op jit(solution)/shard_map/all_gather | solution.py:144
  73.9 0.0 copy-done.8
  73.9 0.7 shard_map.63
  74.6 4.1 %all-gather.6 = bf16[128,512]{1,0:T(8,128)(2,1)S(1)} all-gather(bf16[64,512]{1,0:T(8,128)(2,1)S(1)} %get-tuple-element.106), channel_id=8, replica_groups={{0,8},{16,24},{32,40},{48,56},{64,72},{80,88},{96,104},{112,120},{128,1..., dimensions={0}, use_global_device_ids=true | all-gather | bytes 196608 | tf_op jit(solution)/shard_map/all_gather | solution.py:144
  78.7 0.7 shard_map.64
  79.4 7.1 %all-gather.7 = bf16[128,512]{1,0:T(8,128)(2,1)S(1)} all-gather(bf16[64,512]{1,0:T(8,128)(2,1)S(1)} %get-tuple-element.111), channel_id=9, replica_groups={{8,16},{24,32},{40,48},{56,64},{72,80},{88,96},{104,112},{120,128},{136..., dimensions={0}, use_global_device_ids=true | all-gather | bytes 196608 | tf_op jit(solution)/shard_map/all_gather | solution.py:144
  86.6 0.2 shard_map.65.refs_5_
  86.8 0.3 shard_map.66
  87.1 3.8 %all-gather.8 = bf16[128,512]{1,0:T(8,128)(2,1)S(1)} all-gather(bf16[64,512]{1,0:T(8,128)(2,1)S(1)} %get-tuple-element.112), channel_id=10, replica_groups={{0,8},{16,24},{32,40},{48,56},{64,72},{80,88},{96,104},{112,120},{128,1..., dimensions={0}, use_global_device_ids=true | all-gather | bytes 196608 | tf_op jit(solution)/shard_map/all_gather | solution.py:144
  90.9 0.4 shard_map.67
  91.3 7.1 %all-gather.9 = bf16[128,512]{1,0:T(8,128)(2,1)S(1)} all-gather(bf16[64,512]{1,0:T(8,128)(2,1)S(1)} %get-tuple-element.116), channel_id=11, replica_groups={{8,16},{24,32},{40,48},{56,64},{72,80},{88,96},{104,112},{120,128},{136..., dimensions={0}, use_global_device_ids=true | all-gather | bytes 196608 | tf_op jit(solution)/shard_map/all_gather | solution.py:144
  98.4 0.5 shard_map.68
  98.9 3.8 %all-gather.10 = bf16[128,512]{1,0:T(8,128)(2,1)S(1)} all-gather(bf16[64,512]{1,0:T(8,128)(2,1)S(1)} %get-tuple-element.120), channel_id=12, replica_groups={{0,8},{16,24},{32,40},{48,56},{64,72},{80,88},{96,104},{112,120},{128,1..., dimensions={0}, use_global_device_ids=true | all-gather | bytes 196608 | tf_op jit(solution)/shard_map/all_gather | solution.py:144
  102.7 0.5 shard_map.69
  103.2 0.0 copy-start.7
  103.2 7.3 %all-gather.11 = bf16[128,512]{1,0:T(8,128)(2,1)S(1)} all-gather(bf16[64,512]{1,0:T(8,128)(2,1)S(1)} %get-tuple-element.124), channel_id=13, replica_groups={{8,16},{24,32},{40,48},{56,64},{72,80},{88,96},{104,112},{120,128},{136..., dimensions={0}, use_global_device_ids=true | all-gather | bytes 196608 | tf_op jit(solution)/shard_map/all_gather | solution.py:144
  110.5 0.6 shard_map.70
  111.1 3.8 %all-gather.12 = bf16[128,512]{1,0:T(8,128)(2,1)S(1)} all-gather(bf16[64,512]{1,0:T(8,128)(2,1)S(1)} %get-tuple-element.128), channel_id=14, replica_groups={{0,8},{16,24},{32,40},{48,56},{64,72},{80,88},{96,104},{112,120},{128,1..., dimensions={0}, use_global_device_ids=true | all-gather | bytes 196608 | tf_op jit(solution)/shard_map/all_gather | solution.py:144
  114.9 0.0 copy-done.7
  114.9 0.7 shard_map.71
  115.5 7.9 %all-gather.13 = bf16[128,512]{1,0:T(8,128)(2,1)S(1)} all-gather(bf16[64,512]{1,0:T(8,128)(2,1)S(1)} %get-tuple-element.132), channel_id=15, replica_groups={{8,16},{24,32},{40,48},{56,64},{72,80},{88,96},{104,112},{120,128},{136..., dimensions={0}, use_global_device_ids=true | all-gather | bytes 196608 | tf_op jit(solution)/shard_map/all_gather | solution.py:144
  123.4 0.2 shard_map.72
  123.7 3.4 %all-gather.14 = bf16[128,256]{1,0:T(8,128)(2,1)S(1)} all-gather(bf16[64,256]{1,0:T(8,128)(2,1)S(1)} %get-tuple-element.135), channel_id=16, replica_groups={{0,8},{16,24},{32,40},{48,56},{64,72},{80,88},{96,104},{112,120},{128,1..., dimensions={0}, use_global_device_ids=true | all-gather | bytes 98304 | tf_op jit(solution)/shard_map/all_gather | solution.py:144
  127.1 0.3 shard_map.73
  127.4 27.1 %all_to_all.10.r_ref = bf16[8,64,256]{2,1,0:T(8,128)(2,1)S(1)} all-to-all(bf16[8,64,256]{2,1,0:T(8,128)(2,1)S(1)} %shard_map.73), channel_id=1, replica_groups=mesh['sn'=64,'rhs'=8] {'rhs'}, dimensions={0} | all-to-all | bytes 524288 | tf_op jit(solution)/shard_map/all_to_all | solution.py:284
  154.6 1.1 shard_map.74
  (15 shorter events, 0.1 us)
Async XLA Ops:
  0.0 1.0 copy-start.15
  1.9 20.2 %all-to-all-start = ((bf16[8,64,256]{2,1,0:T(8,128)(2,1)}), bf16[8,64,256]{2,1,0:T(8,128)(2,1)S(1)}, u32[]{:S(2)}, u32[]{:S(2)}) async-start(bf16[8,64,256]{2,1,0:T(8,128)(2,1)} %shard_map.55), calls=%async_computation | async-start | bytes 524288 | tf_op jit(solution)/shard_map/all_to_all | solution.py:123
  13.5 20.6 %copy-start = (bf16[8,2,128,128]{3,2,1,0:T(8,128)(2,1)S(1)}, bf16[8,2,128,128]{3,2,1,0:T(8,128)(2,1)}, u32[]{:S(2)}) copy-start(bf16[8,2,128,128]{3,2,1,0:T(8,128)(2,1)} %d_ref.5) | copy-start | bytes 1572868
  22.1 25.2 %copy-start.1 = (bf16[1792,768]{1,0:T(8,128)(2,1)S(1)}, bf16[1792,768]{1,0:T(8,128)(2,1)}, u32[]{:S(2)}) copy-start(bf16[1792,768]{1,0:T(8,128)(2,1)} %get-tuple-element.83.refs_7_.refs_9_) | copy-start | bytes 8257540
  22.1 25.2 %copy-start.4 = (bf16[256,768]{1,0:T(8,128)(2,1)S(1)}, bf16[256,768]{1,0:T(8,128)(2,1)}, u32[]{:S(2)}) copy-start(bf16[256,768]{1,0:T(8,128)(2,1)} %get-tuple-element.82.refs_4_.refs_2_.refs_8_) | copy-start | bytes 1179652
  22.1 25.1 %collective-permute-start.1 = (bf16[3,256,256]{2,1,0:T(8,128)(2,1)}, bf16[3,256,256]{2,1,0:T(8,128)(2,1)S(1)}, u32[]{:S(2)}, u32[]{:S(2)}) collective-permute-start(bf16[3,256,256]{2,1,0:T(8,128)(2,1)} %get-tuple-element.85), channel_id=1, source_target_pairs={{0,8},{16,24},{32,40},{48,56},{64,72},{80,88},{96,104},{112,120},{... | collective-permute-start | bytes 1179656 | tf_op jit(solution)/shard_map/ppermute | solution.py:140
  24.3 22.9 %collective-permute-start = (bf16[4,256,256]{2,1,0:T(8,128)(2,1)}, bf16[4,256,256]{2,1,0:T(8,128)(2,1)S(1)}, u32[]{:S(2)}, u32[]{:S(2)}) collective-permute-start(bf16[4,256,256]{2,1,0:T(8,128)(2,1)} %get-tuple-element.80), channel_id=1, source_target_pairs={{8,16},{24,32},{40,48},{56,64},{72,80},{88,96},{104,112},{120,128}... | collective-permute-start | bytes 1572872 | tf_op jit(solution)/shard_map/ppermute | solution.py:140
  38.2 1.0 copy-start.6
  47.3 5.1 %copy-start.2 = (bf16[1536,768]{1,0:T(8,128)(2,1)S(1)}, bf16[1536,768]{1,0:T(8,128)(2,1)}, u32[]{:S(2)}) copy-start(bf16[1536,768]{1,0:T(8,128)(2,1)} %get-tuple-element.89.refs_7_.refs_9_) | copy-start | bytes 7077892
  47.3 5.1 %copy-start.5 = (bf16[256,768]{1,0:T(8,128)(2,1)S(1)}, bf16[256,768]{1,0:T(8,128)(2,1)}, u32[]{:S(2)}) copy-start(bf16[256,768]{1,0:T(8,128)(2,1)} %get-tuple-element.87.refs_4_.refs_2_.refs_8_) | copy-start | bytes 1179652
  48.5 12.4 %copy-start.3 = (bf16[1280,768]{1,0:T(8,128)(2,1)S(1)}, bf16[1280,768]{1,0:T(8,128)(2,1)}, u32[]{:S(2)}) copy-start(bf16[1280,768]{1,0:T(8,128)(2,1)} %get-tuple-element.94.refs_7_.refs_9_) | copy-start | bytes 5898244
  48.5 12.4 %copy-start.10 = (bf16[256,768]{1,0:T(8,128)(2,1)S(1)}, bf16[256,768]{1,0:T(8,128)(2,1)}, u32[]{:S(2)}) copy-start(bf16[256,768]{1,0:T(8,128)(2,1)} %get-tuple-element.92.refs_4_.refs_2_.refs_8_) | copy-start | bytes 1179652
  53.6 12.1 %copy-start.9 = (bf16[1024,768]{1,0:T(8,128)(2,1)S(1)}, bf16[1024,768]{1,0:T(8,128)(2,1)}, u32[]{:S(2)}) copy-start(bf16[1024,768]{1,0:T(8,128)(2,1)} %get-tuple-element.99.refs_7_.refs_9_) | copy-start | bytes 4718596
  53.6 12.1 %copy-start.11 = (bf16[256,768]{1,0:T(8,128)(2,1)S(1)}, bf16[256,768]{1,0:T(8,128)(2,1)}, u32[]{:S(2)}) copy-start(bf16[256,768]{1,0:T(8,128)(2,1)} %get-tuple-element.97.refs_4_.refs_2_.refs_8_) | copy-start | bytes 1179652
  61.8 12.1 %copy-start.8 = (bf16[256,768]{1,0:T(8,128)(2,1)S(1)}, bf16[256,768]{1,0:T(8,128)(2,1)}, u32[]{:S(2)}) copy-start(bf16[256,768]{1,0:T(8,128)(2,1)} %get-tuple-element.102.refs_4_.refs_2_.refs_6_) | copy-start | bytes 1179652
  61.8 12.1 %copy-start.12 = (bf16[768,768]{1,0:T(8,128)(2,1)S(1)}, bf16[768,768]{1,0:T(8,128)(2,1)}, u32[]{:S(2)}) copy-start(bf16[768,768]{1,0:T(8,128)(2,1)} %get-tuple-element.104.refs_7_.refs_9_) | copy-start | bytes 3538948
  66.7 12.1 %copy-start.13 = (bf16[256,768]{1,0:T(8,128)(2,1)S(1)}, bf16[256,768]{1,0:T(8,128)(2,1)}, u32[]{:S(2)}) copy-start(bf16[256,768]{1,0:T(8,128)(2,1)} %get-tuple-element.107.refs_4_.refs_2_) | copy-start | bytes 1179652
  66.7 12.1 %copy-start.14 = (bf16[512,768]{1,0:T(8,128)(2,1)S(1)}, bf16[512,768]{1,0:T(8,128)(2,1)}, u32[]{:S(2)}) copy-start(bf16[512,768]{1,0:T(8,128)(2,1)} %get-tuple-element.109.refs_7_) | copy-start | bytes 2359300
  103.2 11.7 %copy-start.7 = (bf16[256,768]{1,0:T(8,128)(2,1)S(1)}, bf16[256,768]{1,0:T(8,128)(2,1)}, u32[]{:S(2)}) copy-start(bf16[256,768]{1,0:T(8,128)(2,1)} %get-tuple-element.77.refs_2_.refs_8_) | copy-start | bytes 1179652
